TPU v7x, 32 devices: a whole 2x2x4 slice. The times are simulated.
32 devices in a mesh: row: 8 (over y, x, core), col: 4 (over z).
Axes of the slice: x: 2, y: 2, z: 4, core: 2. Of those that a mesh axis runs over, the one named last changes fastest.
Arguments:
- node_features: bfloat16 [8192, 256], P(('row', 'col')), may hold values from -6 to 6
- tile_values: bfloat16 [8, 4, 128, 128, 128], P('row', 'col'), may hold values from -0.09375 to 0.09375
- tile_coords: int32 [8, 4, 128, 2], P('row', 'col'), may hold values from 0 to 15, as said below
- tile_counts: int32 [8, 4], P('row', 'col'), may hold values from 32 to 128, as said below
- first_weight: bfloat16 [256, 256], replicated, may hold values from -0.375 to 0.375
- second_weight: bfloat16 [256, 128], replicated, may hold values from -0.375 to 0.375
- out_grad: bfloat16 [8192, 128], P(('row', 'col')), may hold values from -6 to 6
Outputs:
- output: bfloat16 [8192, 128], P(('row', 'col'))
- first_grad: float32 [256, 256], replicated
- second_grad: float32 [256, 128], replicated
Inputs may be any that keep to these rules, and one draw needn't show every extreme that they name: `tile_counts`: each grid cell uses at least 32 slots; at least one grid cell uses all 128 in every draw. `tile_coords`: the first entry is a tile row below 16, the second a tile column below 8; within one grid cell no two slots share a position.
All inputs are finite; a program needn't handle non-finite values.
Results may differ from a plain program's by a relative error of at most 0.005.
Values may be sent and summed in bfloat16 or wider, within the bound.
No kernel may reach another device: no remote copies, remote signals or barrier semaphores. Data moves between devices by JAX's collectives and lax.ppermute only.
A program may use at most 64 MiB of HBM per device.

v0:
```python
import math

import jax
import jax.numpy as jnp
from jax import lax
from jax.sharding import PartitionSpec as P

HIGHEST = lax.Precision.HIGHEST


def tile_sum(tile_block, dest_index, source_index, live_slots, source, dest_tiles, flipped):
    slot_count = tile_block.shape[0]
    group_size = math.gcd(slot_count, 32)
    round_count = slot_count // group_size
    edge_size = tile_block.shape[1]
    width_size = source.shape[-1]
    grouped_tiles = tile_block.reshape(round_count, group_size, edge_size, edge_size)
    grouped_dest = dest_index.reshape(round_count, group_size)
    grouped_source = source_index.reshape(round_count, group_size)
    grouped_live = live_slots.reshape(round_count, group_size)
    target_ids = jnp.arange(dest_tiles, dtype=jnp.int32)
    einsum_form = "tba,tbw->taw" if flipped else "tab,tbw->taw"

    def add_group(running, pieces):
        group_tiles, group_dest, group_source, group_live = pieces
        picked = jnp.take(source, group_source, axis=0)
        products = jnp.einsum(einsum_form, group_tiles, picked, preferred_element_type=jnp.float32)
        select = ((group_dest[:, None] == target_ids[None, :]) & group_live[:, None]).astype(
            jnp.float32
        )
        running = running + jnp.einsum("tr,taw->raw", select, products, precision=HIGHEST)
        return (running, None)

    start_sum = jnp.zeros((dest_tiles, edge_size, width_size), jnp.float32)
    running, unused = lax.scan(
        add_group, start_sum, (grouped_tiles, grouped_dest, grouped_source, grouped_live)
    )
    return running.reshape(dest_tiles * edge_size, width_size)


def on_device(
    node_features, tile_values, tile_coords, tile_counts, first_weight, second_weight, out_grad
):
    node_rows = node_features.shape[0]
    edge_size = tile_values.shape[-1]
    slot_count = tile_values.shape[2]
    grid_rows = lax.axis_size("row")
    grid_cols = lax.axis_size("col")
    row_tiles = grid_rows * node_rows // edge_size
    col_tiles = grid_cols * node_rows // edge_size
    tile_block = tile_values.reshape(slot_count, edge_size, edge_size)
    flat_coords = tile_coords.reshape(slot_count, 2)
    tile_row = flat_coords[:, 0]
    tile_col = flat_coords[:, 1]
    live_slots = jnp.arange(slot_count, dtype=jnp.int32) < tile_counts.reshape(())
    gathered_x = lax.all_gather(node_features, "col", axis=0, tiled=True)
    feature_part = tile_sum(
        tile_block,
        tile_row,
        tile_col,
        live_slots,
        gathered_x.reshape(col_tiles, edge_size, -1),
        row_tiles,
        False,
    )
    first_mean = lax.psum_scatter(feature_part, "row", scatter_dimension=0, tiled=True)
    first_pre = jnp.dot(first_mean, first_weight.astype(jnp.float32), precision=HIGHEST)
    hidden_act = jax.nn.silu(first_pre).astype(jnp.bfloat16)
    second_wide = second_weight.astype(jnp.float32)
    gathered_h = lax.all_gather(hidden_act, "col", axis=0, tiled=True)
    hidden_part = tile_sum(
        tile_block,
        tile_row,
        tile_col,
        live_slots,
        gathered_h.reshape(col_tiles, edge_size, -1),
        row_tiles,
        False,
    )
    second_mean = lax.psum_scatter(hidden_part, "row", scatter_dimension=0, tiled=True)
    logit_rows = jnp.dot(second_mean, second_wide, precision=HIGHEST)
    output = logit_rows.astype(jnp.bfloat16)
    gathered_g = lax.all_gather(out_grad, "row", axis=0, tiled=True)
    grad_part = tile_sum(
        tile_block,
        tile_col,
        tile_row,
        live_slots,
        gathered_g.reshape(row_tiles, edge_size, -1),
        col_tiles,
        True,
    )
    back_sum = lax.psum_scatter(grad_part, "col", scatter_dimension=0, tiled=True)
    scale = 1.0 / math.sqrt(node_rows * grid_rows * grid_cols)
    second_local = jnp.dot(hidden_act.astype(jnp.float32).T, back_sum, precision=HIGHEST) * scale
    hidden_grad = jnp.dot(back_sum, second_wide.T, precision=HIGHEST)
    sigma = jax.nn.sigmoid(first_pre)
    pre_grad = hidden_grad * (sigma * (1.0 + first_pre * (1.0 - sigma)))
    second_grad = lax.psum(second_local, ("row", "col"))
    first_local = jnp.dot(first_mean.T, pre_grad, precision=HIGHEST) * scale
    first_grad = lax.psum(first_local, ("row", "col"))
    return (output, first_grad, second_grad)


def solution(mesh):
    return jax.shard_map(
        on_device,
        mesh=mesh,
        in_specs=(
            P(("row", "col"), None),
            P("row", "col", None, None, None),
            P("row", "col", None, None),
            P("row", "col"),
            P(),
            P(),
            P(("row", "col"), None),
        ),
        out_specs=(P(("row", "col"), None), P(), P()),
        check_vma=False,
    )
```

profile of v0, /device:TPU:0, one launch (start us, length us, event | category | flops | bytes accessed | tf_op | source)
XLA Modules:
  0.0 385.1 jit_solution(15042599917803408679)
XLA Ops:
  8.8 17.6 %all_gather.9 = bf16[1024,256]{1,0:T(8,128)(2,1)S(1)} all-gather(bf16[256,256]{1,0:T(8,128)(2,1)} %param.15), channel_id=1, replica_groups=mesh['row'=8,'col'=4] {'col'}, dimensions={0}, use_global_device_ids=true | all-gather | bytes 655360 | tf_op jit(solution)/shard_map/all_gather | solution.py:56
  26.4 50.0 %while.33 = (s32[]{:T(128)}, f32[16,128,256]{2,0,1:T(8,128)}, s32[4,32]{1,0:T(4,128)S(1)}, pred[4,32]{1,0:T(4,128)(4,1)S(1)}, bf16[4,32,128,128]{3,2,1,0:T(8,128...) while((s32[]{:T(128)}, f32[16,128,256]{2,0,1:T(8,128)}, ...), condition=%wide.region_1.3_spmd.clone, body=%wide.region_0.2_spmd.clone.sunk | while | flops 471861440 | bytes 19928724 | solution.py:35
  31.1 7.3 %select_add_fusion.4 = f32[16,128,256]{2,0,1:T(8,128)} fusion(f32[16,128,256]{2,0,1:T(8,128)} %get-tuple-element.410, f32[32,128,256]{2,1,0:T(8,128)} %fusion.98, pred[]{:T(512)S(6)} %compare.9, s32[32]{0:T(128)S(1)} %fusion.99, pred[32]{0:T(512)(128)(4,1)S(1)} %dynamic-slice_bitcast_fusion.6), kind=kOutput, calls=%fused_computation.35.clone.1 | convolution fusion | flops 202376192 | bytes 8388769 | tf_op jit(solution)/shard_map/while/body/eval_jaxpr/tr,taw->raw/dot_general | solution.py:31
  39.1 4.0 %fusion.98 = f32[32,128,256]{2,1,0:T(8,128)} fusion(bf16[32,128,256]{2,1,0:T(8,128)(2,1)S(1)} %gather_fusion, pred[32]{0:T(512)(128)(4,1)S(1)} %get-tuple-element.383, bf16[4,32,128,128]{3,2,1,0:T(8,128)(2,1)} %get-tuple-element.422, s32[]{:T(128)} %get-tuple-element.409), kind=kOutput, calls=%fused_computation.33.clone.1 | convolution fusion | flops 269484032 | bytes 7340576 | tf_op jit(solution)/shard_map/while/body/eval_jaxpr/tab,tbw->taw/dot_general | solution.py:27
  43.1 8.0 %select_add_fusion.4 = f32[16,128,256]{2,0,1:T(8,128)} fusion(f32[16,128,256]{2,0,1:T(8,128)} %get-tuple-element.410, f32[32,128,256]{2,1,0:T(8,128)} %fusion.98, pred[]{:T(512)S(6)} %compare.9, s32[32]{0:T(128)S(1)} %fusion.99, pred[32]{0:T(512)(128)(4,1)S(1)} %dynamic-slice_bitcast_fusion.6), kind=kOutput, calls=%fused_computation.35.clone.1 | convolution fusion | flops 202376192 | bytes 8388769 | tf_op jit(solution)/shard_map/while/body/eval_jaxpr/tr,taw->raw/dot_general | solution.py:31
  51.8 4.0 %fusion.98 = f32[32,128,256]{2,1,0:T(8,128)} fusion(bf16[32,128,256]{2,1,0:T(8,128)(2,1)S(1)} %gather_fusion, pred[32]{0:T(512)(128)(4,1)S(1)} %get-tuple-element.383, bf16[4,32,128,128]{3,2,1,0:T(8,128)(2,1)} %get-tuple-element.422, s32[]{:T(128)} %get-tuple-element.409), kind=kOutput, calls=%fused_computation.33.clone.1 | convolution fusion | flops 269484032 | bytes 7340576 | tf_op jit(solution)/shard_map/while/body/eval_jaxpr/tab,tbw->taw/dot_general | solution.py:27
  55.7 8.0 %select_add_fusion.4 = f32[16,128,256]{2,0,1:T(8,128)} fusion(f32[16,128,256]{2,0,1:T(8,128)} %get-tuple-element.410, f32[32,128,256]{2,1,0:T(8,128)} %fusion.98, pred[]{:T(512)S(6)} %compare.9, s32[32]{0:T(128)S(1)} %fusion.99, pred[32]{0:T(512)(128)(4,1)S(1)} %dynamic-slice_bitcast_fusion.6), kind=kOutput, calls=%fused_computation.35.clone.1 | convolution fusion | flops 202376192 | bytes 8388769 | tf_op jit(solution)/shard_map/while/body/eval_jaxpr/tr,taw->raw/dot_general | solution.py:31
  64.4 4.0 %fusion.98 = f32[32,128,256]{2,1,0:T(8,128)} fusion(bf16[32,128,256]{2,1,0:T(8,128)(2,1)S(1)} %gather_fusion, pred[32]{0:T(512)(128)(4,1)S(1)} %get-tuple-element.383, bf16[4,32,128,128]{3,2,1,0:T(8,128)(2,1)} %get-tuple-element.422, s32[]{:T(128)} %get-tuple-element.409), kind=kOutput, calls=%fused_computation.33.clone.1 | convolution fusion | flops 269484032 | bytes 7340576 | tf_op jit(solution)/shard_map/while/body/eval_jaxpr/tab,tbw->taw/dot_general | solution.py:27
  68.4 8.0 %select_add_fusion.4 = f32[16,128,256]{2,0,1:T(8,128)} fusion(f32[16,128,256]{2,0,1:T(8,128)} %get-tuple-element.410, f32[32,128,256]{2,1,0:T(8,128)} %fusion.98, pred[]{:T(512)S(6)} %compare.9, s32[32]{0:T(128)S(1)} %fusion.99, pred[32]{0:T(512)(128)(4,1)S(1)} %dynamic-slice_bitcast_fusion.6), kind=kOutput, calls=%fused_computation.35.clone.1 | convolution fusion | flops 202376192 | bytes 8388769 | tf_op jit(solution)/shard_map/while/body/eval_jaxpr/tr,taw->raw/dot_general | solution.py:31
  76.4 4.2 %copy.10 = f32[16,128,256]{2,1,0:T(8,128)} copy(f32[16,128,256]{2,0,1:T(8,128)} %get-tuple-element.130) | data formatting | bytes 4194304 | tf_op jit(solution)/shard_map/while | solution.py:35
  81.4 10.9 %all_gather.11 = bf16[2048,128]{1,0:T(8,128)(2,1)} all-gather(bf16[256,128]{1,0:T(8,128)(2,1)S(1)} %copy-done.2), channel_id=1, replica_groups=mesh['row'=8,'col'=4] {'row'}, dimensions={0}, use_global_device_ids=true | all-gather | bytes 589824 | tf_op jit(solution)/shard_map/all_gather | solution.py:83
  92.2 29.0 %while.35 = (s32[]{:T(128)}, f32[8,128,128]{2,0,1:T(8,128)}, s32[4,32]{1,0:T(4,128)S(1)}, pred[4,32]{1,0:T(4,128)(4,1)S(1)}, bf16[4,32,128,128]{3,2,1,0:T(8,128)...) while((s32[]{:T(128)}, f32[8,128,128]{2,0,1:T(8,128)}, ...), condition=%wide.region_7.9_spmd.clone, body=%wide.region_6.8_spmd.clone.sunk | while | flops 185337632 | bytes 9443095 | solution.py:35
  125.0 21.9 %all_gather.10 = bf16[1024,256]{1,0:T(8,128)(2,1)S(1)} all-gather(bf16[256,256]{1,0:T(8,128)(2,1)S(1)} %get-tuple-element.261), channel_id=1, replica_groups=mesh['row'=8,'col'=4] {'col'}, dimensions={0}, use_global_device_ids=true | all-gather | bytes 655360 | tf_op jit(solution)/shard_map/all_gather | solution.py:70
  147.0 50.0 %while.34 = (s32[]{:T(128)}, f32[16,128,256]{2,0,1:T(8,128)}, s32[4,32]{1,0:T(4,128)S(1)}, pred[4,32]{1,0:T(4,128)(4,1)S(1)}, bf16[4,32,128,128]{3,2,1,0:T(8,128...) while((s32[]{:T(128)}, f32[16,128,256]{2,0,1:T(8,128)}, ...), condition=%wide.region_4.6_spmd.clone, body=%wide.region_3.5_spmd.clone.sunk | while | flops 471861440 | bytes 19928724 | solution.py:35
  147.7 4.0 %fusion.104 = f32[32,128,256]{2,1,0:T(8,128)} fusion(bf16[32,128,256]{2,1,0:T(8,128)(2,1)S(1)} %gather_fusion.1, pred[32]{0:T(512)(128)(4,1)S(1)} %get-tuple-element.392, bf16[4,32,128,128]{3,2,1,0:T(8,128)(2,1)} %get-tuple-element.449, s32[]{:T(128)} %get-tuple-element.436), kind=kOutput, calls=%fused_computation.57.clone.1 | convolution fusion | flops 269484032 | bytes 7340576 | tf_op jit(solution)/shard_map/while/body/eval_jaxpr/tab,tbw->taw/dot_general | solution.py:27
  151.7 7.3 %select_add_fusion.5 = f32[16,128,256]{2,0,1:T(8,128)} fusion(f32[16,128,256]{2,0,1:T(8,128)} %get-tuple-element.437, f32[32,128,256]{2,1,0:T(8,128)} %fusion.104, pred[]{:T(512)S(6)} %compare.10, s32[32]{0:T(128)S(1)} %fusion.105, pred[32]{0:T(512)(128)(4,1)S(1)} %dynamic-slice_bitcast_fusion.7), kind=kOutput, calls=%fused_computation.59.clone.1 | convolution fusion | flops 202376192 | bytes 8388769 | tf_op jit(solution)/shard_map/while/body/eval_jaxpr/tr,taw->raw/dot_general | solution.py:31
  159.7 4.0 %fusion.104 = f32[32,128,256]{2,1,0:T(8,128)} fusion(bf16[32,128,256]{2,1,0:T(8,128)(2,1)S(1)} %gather_fusion.1, pred[32]{0:T(512)(128)(4,1)S(1)} %get-tuple-element.392, bf16[4,32,128,128]{3,2,1,0:T(8,128)(2,1)} %get-tuple-element.449, s32[]{:T(128)} %get-tuple-element.436), kind=kOutput, calls=%fused_computation.57.clone.1 | convolution fusion | flops 269484032 | bytes 7340576 | tf_op jit(solution)/shard_map/while/body/eval_jaxpr/tab,tbw->taw/dot_general | solution.py:27
  163.6 8.0 %select_add_fusion.5 = f32[16,128,256]{2,0,1:T(8,128)} fusion(f32[16,128,256]{2,0,1:T(8,128)} %get-tuple-element.437, f32[32,128,256]{2,1,0:T(8,128)} %fusion.104, pred[]{:T(512)S(6)} %compare.10, s32[32]{0:T(128)S(1)} %fusion.105, pred[32]{0:T(512)(128)(4,1)S(1)} %dynamic-slice_bitcast_fusion.7), kind=kOutput, calls=%fused_computation.59.clone.1 | convolution fusion | flops 202376192 | bytes 8388769 | tf_op jit(solution)/shard_map/while/body/eval_jaxpr/tr,taw->raw/dot_general | solution.py:31
  172.3 4.0 %fusion.104 = f32[32,128,256]{2,1,0:T(8,128)} fusion(bf16[32,128,256]{2,1,0:T(8,128)(2,1)S(1)} %gather_fusion.1, pred[32]{0:T(512)(128)(4,1)S(1)} %get-tuple-element.392, bf16[4,32,128,128]{3,2,1,0:T(8,128)(2,1)} %get-tuple-element.449, s32[]{:T(128)} %get-tuple-element.436), kind=kOutput, calls=%fused_computation.57.clone.1 | convolution fusion | flops 269484032 | bytes 7340576 | tf_op jit(solution)/shard_map/while/body/eval_jaxpr/tab,tbw->taw/dot_general | solution.py:27
  176.3 8.0 %select_add_fusion.5 = f32[16,128,256]{2,0,1:T(8,128)} fusion(f32[16,128,256]{2,0,1:T(8,128)} %get-tuple-element.437, f32[32,128,256]{2,1,0:T(8,128)} %fusion.104, pred[]{:T(512)S(6)} %compare.10, s32[32]{0:T(128)S(1)} %fusion.105, pred[32]{0:T(512)(128)(4,1)S(1)} %dynamic-slice_bitcast_fusion.7), kind=kOutput, calls=%fused_computation.59.clone.1 | convolution fusion | flops 202376192 | bytes 8388769 | tf_op jit(solution)/shard_map/while/body/eval_jaxpr/tr,taw->raw/dot_general | solution.py:31
  188.9 8.0 %select_add_fusion.5 = f32[16,128,256]{2,0,1:T(8,128)} fusion(f32[16,128,256]{2,0,1:T(8,128)} %get-tuple-element.437, f32[32,128,256]{2,1,0:T(8,128)} %fusion.104, pred[]{:T(512)S(6)} %compare.10, s32[32]{0:T(128)S(1)} %fusion.105, pred[32]{0:T(512)(128)(4,1)S(1)} %dynamic-slice_bitcast_fusion.7), kind=kOutput, calls=%fused_computation.59.clone.1 | convolution fusion | flops 202376192 | bytes 8388769 | tf_op jit(solution)/shard_map/while/body/eval_jaxpr/tr,taw->raw/dot_general | solution.py:31
  196.9 4.2 %copy.11 = f32[16,128,256]{2,1,0:T(8,128)} copy(f32[16,128,256]{2,0,1:T(8,128)} %get-tuple-element.131) | data formatting | bytes 4194304 | tf_op jit(solution)/shard_map/while | solution.py:35
  205.6 36.1 %reduce-scatter.6.cloned.1.call-done = f32[256,256]{1,0:T(8,128)} async-done(((f32[2048,256]{1,0:T(8,128)}), f32[256,256]{1,0:T(8,128)}) %reduce-scatter.6.cloned.1.call-update) | async-done | bytes 262160 | tf_op jit(solution)/shard_map/reduce_scatter | solution.py:80
  243.5 131.8 %all-reduce.3.cloned.1.call-done = (f32[256,256]{1,0:T(8,128)}, f32[256,128]{1,0:T(8,128)}) async-done(((f32[256,256]{1,0:T(8,128)}, f32[256,128]{1,0:T(8,128)}), (f32[256,256]{1,0:T(8,128)}, f32[256,128]{1,0:T(8,128)})) %all-reduce.3.cloned.1.call-update) | async-done | bytes 393232 | tf_op jit(solution)/shard_map/psum | solution.py:101
  (107 shorter events, 57.5 us)
Async XLA Ops:
  7.2 116.6 %copy-start = (bf16[256,256]{1,0:T(8,128)(2,1)S(1)}, bf16[256,256]{1,0:T(8,128)(2,1)}, u32[]{:S(2)}) copy-start(bf16[256,256]{1,0:T(8,128)(2,1)} %param.19) | copy-start | bytes 393220
  7.2 116.6 %reduce-scatter.4.cloned.1.call-start = ((), (), s32[]{:S(2)}) async-start(), calls=%async_computation.3 | async-start | bytes 2359296 | tf_op jit(solution)/shard_map/reduce_scatter | solution.py:66
  80.5 0.8 copy-start.2
  80.5 120.6 %reduce-scatter.8.cloned.1.call-start = ((), (), s32[]{:S(2)}) async-start(), calls=%async_computation.5 | async-start | bytes 655360 | tf_op jit(solution)/shard_map/reduce_scatter | solution.py:93
  123.3 118.4 %reduce-scatter.6.cloned.1.call-start = ((), (), s32[]{:S(2)}) async-start(), calls=%async_computation.4 | async-start | bytes 2359296 | tf_op jit(solution)/shard_map/reduce_scatter | solution.py:80
  201.1 2.0 copy-start.3
  201.1 3.2 copy-start.1
  201.1 174.3 %all-reduce.3.cloned.1.call-start = ((), (), s32[]{:S(2)}) async-start(), calls=%async_computation.6 | async-start | bytes 786432 | tf_op jit(solution)/shard_map/psum | solution.py:101
Sparse Core Ops, SparseCore 0:
  80.7 43.0 reduce-scatter.3
  126.1 24.4 reduce-scatter.7
  201.2 40.4 reduce-scatter.5
  247.5 127.8 all-reduce.2
where the time goes:
time: 386 us; the launch traced here: 385 us
  waiting for transfers between devices  168 us (44%)
  matrix products  123 us (32%)
  blocking collectives  50.4 us (13%)
  local copies, waits for them, and re-layouts  28.1 us (7%)
  between operations  14.5 us (4%)
    psum x1, waiting for transfers between devices, on_device(): first_grad = lax.psum(first_local, ('row', 'col'))  132 us
    dot_general x12, matrix products, add_group(): jnp.einsum('tr,taw->raw', select, products, precision=HIGHEST)  76.6 us
    dot_general x12, matrix products, add_group(): jnp.einsum(einsum_form, group_tiles, picked, preferred_element_type=jnp.f...  38.9 us
    reduce_scatter x1, waiting for transfers between devices, on_device(): lax.psum_scatter(hidden_part, 'row', scatter_dimension=0, tiled=True)  36.1 us
    all_gather x1, blocking collectives, on_device(): gathered_h = lax.all_gather(hidden_act, 'col', axis=0, tiled=True)  21.9 us
    all_gather x1, blocking collectives, on_device(): gathered_x = lax.all_gather(node_features, 'col', axis=0, tiled=True)  17.6 us
    gather x12, local copies, waits for them, and re-layouts, add_group(): picked = jnp.take(source, group_source, axis=0)  12.6 us
    all_gather x1, blocking collectives, on_device(): gathered_g = lax.all_gather(out_grad, 'row', axis=0, tiled=True)  10.9 us
  transfers between devices with their start and end apart: 4, of which 3 were waited for; matrix products, arithmetic and copies ran while one was open for 24% of the time, Pallas kernels for 0%

commit v1 on v0

v1 whole, which is shorter than its diff:
```python
import functools
import math

import jax
import jax.numpy as jnp
from jax import lax
from jax.experimental import pallas as pl
from jax.experimental.pallas import tpu as pltpu
from jax.sharding import PartitionSpec as P

BF16 = jnp.bfloat16
F32 = jnp.float32


def assemble_kernel(places_ref, count_ref, tiles_ref, dense_ref, sems):
    slots, edge = tiles_ref.shape[0], tiles_ref.shape[1]
    live = count_ref[0]
    strip = min(dense_ref.shape[1], 256)

    def clear(step, carry):
        rows = pl.ds(pl.multiple_of(step * strip, strip), strip)
        for half in range(2):
            dense_ref[half, rows, :] = jnp.zeros((strip, dense_ref.shape[2]), BF16)
        return carry

    lax.fori_loop(0, dense_ref.shape[1] // strip, clear, 0)

    def tile_copy(slot):
        rows = pl.ds(pl.multiple_of(places_ref[1, slot] * edge, edge), edge)
        cols = pl.ds(pl.multiple_of(places_ref[2, slot] * edge, edge), edge)
        return pltpu.make_async_copy(
            tiles_ref.at[slot], dense_ref.at[places_ref[0, slot], rows, cols], sems.at[slot]
        )

    def begin(slot, carry):
        @pl.when(slot < live)
        def _():
            tile_copy(slot).start()

        return carry

    def finish(slot, carry):
        @pl.when(slot < live)
        def _():
            tile_copy(slot).wait()

        return carry

    lax.fori_loop(0, slots, begin, 0)
    lax.fori_loop(0, slots, finish, 0)


def assemble(tiles, places, count, rows, cols):
    slots = tiles.shape[0]
    return pl.pallas_call(
        assemble_kernel,
        out_shape=jax.ShapeDtypeStruct((2, rows // 2, cols), BF16),
        in_specs=[
            pl.BlockSpec(memory_space=pltpu.SMEM),
            pl.BlockSpec(memory_space=pltpu.SMEM),
            pl.BlockSpec(memory_space=pl.ANY),
        ],
        out_specs=pl.BlockSpec(memory_space=pltpu.VMEM),
        scratch_shapes=[pltpu.SemaphoreType.DMA((slots,))],
        compiler_params=pltpu.CompilerParams(vmem_limit_bytes=rows * cols * 2 + (8 << 20)),
        cost_estimate=pl.CostEstimate(
            flops=0, bytes_accessed=2 * rows * cols * 2, transcendentals=0
        ),
    )(places, count, tiles)


def tree_sum(parts):
    parts = [part.astype(F32) for part in parts]
    while len(parts) > 1:
        parts = [parts[i] + parts[i + 1] for i in range(0, len(parts), 2)]
    return parts[0]


def swap(value, axis, offset):
    size = lax.axis_size(axis)
    return lax.ppermute(value, axis, [(i, i ^ offset) for i in range(size)])


def matmul(left, right, left_dim=1, right_dim=0):
    return lax.dot_general(
        left, right, (((left_dim,), (right_dim,)), ((), ())), preferred_element_type=F32
    )


def on_device(
    node_features, tile_values, tile_coords, tile_counts, first_weight, second_weight, out_grad
):
    node_rows = node_features.shape[0]
    edge = tile_values.shape[-1]
    slots = tile_values.shape[2]
    grid_rows = lax.axis_size("row")
    grid_cols = lax.axis_size("col")
    chips = grid_rows // 2
    per_node = node_rows // edge
    me_row = lax.axis_index("row")
    me_col = lax.axis_index("col")
    me_core = me_row % 2

    def gather_col(value):
        return jnp.concatenate(
            [value] + [swap(value, "col", k) for k in range(1, grid_cols)], axis=0
        )

    def gather_plane(value):
        return jnp.concatenate(
            [value] + [swap(value, "row", 2 * i) for i in range(1, chips)], axis=0
        )

    coords = tile_coords.reshape(slots, 2)
    tile_row, tile_col = coords[:, 0], coords[:, 1]
    offset = (tile_row // per_node) ^ me_row
    places = jnp.stack(
        [
            offset % 2,
            (offset // 2) * per_node + tile_row % per_node,
            ((tile_col // per_node) ^ me_col) * per_node + tile_col % per_node,
        ]
    )
    gathered_x = gather_col(node_features)
    grad_own = gather_plane(out_grad)
    grad_other = swap(grad_own, "row", 1)
    dense = assemble(
        tile_values.reshape(slots, edge, edge),
        places,
        tile_counts.reshape(1),
        grid_rows * node_rows,
        grid_cols * node_rows,
    )
    dense_own, dense_other = dense[0], dense[1]

    def reduce_plane(source):
        other = matmul(dense_other, source).astype(BF16)
        arrived = swap(other, "row", 1)
        chip_sum = matmul(dense_own, source) + arrived.astype(F32)
        blocks = chip_sum.reshape(chips, node_rows, -1)
        sent = [swap(blocks[i].astype(BF16), "row", 2 * i) for i in range(1, chips)]
        return tree_sum([blocks[0]] + sent)

    back_part = matmul(dense_own, grad_own, 0) + matmul(dense_other, grad_other, 0)
    back_blocks = back_part.reshape(grid_cols, node_rows, -1)
    back_sum = tree_sum(
        [back_blocks[0]]
        + [swap(back_blocks[k].astype(BF16), "col", k) for k in range(1, grid_cols)]
    )
    hidden_grad = matmul(back_sum.astype(BF16), second_weight, 1, 1)

    first_mean = reduce_plane(gathered_x)
    first_pre = matmul(first_mean.astype(BF16), first_weight)
    sigma = jax.nn.sigmoid(first_pre)
    hidden_act = (first_pre * sigma).astype(BF16)
    projected = matmul(hidden_act, second_weight).astype(BF16)
    output = reduce_plane(gather_col(projected)).astype(BF16)

    pre_grad = hidden_grad * (sigma * (1.0 + first_pre * (1.0 - sigma)))
    scale = 1.0 / math.sqrt(node_rows * grid_rows * grid_cols)
    first_local = matmul(first_mean.astype(BF16), pre_grad.astype(BF16), 0)
    second_local = matmul(hidden_act, back_sum.astype(BF16), 0)
    grads = jnp.concatenate([first_local, second_local], axis=1) * scale
    half = grads.shape[0] // 2
    low, high = grads[:half], grads[half:]
    mine = jnp.where(me_core == 0, low, high)
    theirs = jnp.where(me_core == 0, high, low)
    mine = (mine + swap(theirs.astype(BF16), "row", 1).astype(F32)).astype(BF16)
    mine = tree_sum([mine] + [swap(mine, "row", 2 * i) for i in range(1, chips)]).astype(BF16)
    mine = tree_sum([mine] + [swap(mine, "col", k) for k in range(1, grid_cols)])
    theirs = swap(mine, "row", 1)
    low = jnp.where(me_core == 0, mine, theirs)
    high = jnp.where(me_core == 0, theirs, mine)
    grads = jnp.concatenate([low, high], axis=0)
    width = first_weight.shape[1]
    return (output, grads[:, :width], grads[:, width:])


def solution(mesh):
    return jax.shard_map(
        on_device,
        mesh=mesh,
        in_specs=(
            P(("row", "col"), None),
            P("row", "col", None, None, None),
            P("row", "col", None, None),
            P("row", "col"),
            P(),
            P(),
            P(("row", "col"), None),
        ),
        out_specs=(P(("row", "col"), None), P(), P()),
        check_vma=False,
    )
```

time: 386 us -> 70.7 us (0.18)
  waiting for transfers between devices: 168 us -> 14.5 us
  matrix products: 123 us -> 6.98 us
  blocking collectives: 50.4 us -> 0 us
  starting transfers between devices: 0.16 us -> 35.3 us
  local copies, waits for them, and re-layouts: 28.1 us -> 4.85 us
  between operations: 14.5 us -> 1.69 us
  Pallas kernels: 0 us -> 4.59 us
    psum x1 -> x0, waiting for transfers between devices: 132 us -> none  [on_device(): first_grad = lax.psum(first_local, ('row', 'col'))]
    dot_general x29 -> x10, matrix products: 123 us -> 6.98 us  [matmul(): lax.dot_general(left, right, (((left_dim,), (right_dim,)), ((), ())), pre...]
    all_gather x3 -> x0, blocking collectives: 50.4 us -> none  [the longest x1 21.9 us: on_device(): gathered_h = lax.all_gather(hidden_act, 'col', axis=0, tiled=True)]
    reduce_scatter x3 -> x0, waiting for transfers between devices: 36.5 us -> none  [the longest x1 36.1 us: on_device(): lax.psum_scatter(hidden_part, 'row', scatter_dimension=0, tiled=True)]
    ppermute x0 -> x29, starting transfers between devices: none -> 35.3 us  [swap(): return lax.ppermute(value, axis, [(i, i ^ offset) for i in range(size)])]
    ppermute x0 -> x29, waiting for transfers between devices: none -> 14.5 us  [swap(): return lax.ppermute(value, axis, [(i, i ^ offset) for i in range(size)])]
    gather x12 -> x0, local copies, waits for them, and re-layouts: 12.6 us -> none  [add_group(): picked = jnp.take(source, group_source, axis=0)]
    while x3 -> x0, local copies, waits for them, and re-layouts: 10.3 us -> none  [tile_sum(): lax.scan(add_group, start_sum, (grouped_tiles, grouped_dest, grouped_sour...]
  transfers between devices with their start and end apart: 4 -> 29, of which waited for: 3 -> 8; matrix products, arithmetic and copies ran while one was open for 24% -> 13% of each run, Pallas kernels for 0% -> 7%
where the time goes in v1:
time: 70.7 us; the launch traced here: 70.5 us
  starting transfers between devices  35.3 us (50%)
  waiting for transfers between devices  14.5 us (21%)
  matrix products  6.98 us (10%)
  local copies, waits for them, and re-layouts  4.85 us (7%)
  Pallas kernels  4.59 us (6%)
  other arithmetic  2.52 us (4%)
  between operations  1.69 us (2%)
    ppermute x29, starting transfers between devices, swap(): return lax.ppermute(value, axis, [(i, i ^ offset) for i in range(size)])  35.3 us
    ppermute x29, waiting for transfers between devices, swap(): return lax.ppermute(value, axis, [(i, i ^ offset) for i in range(size)])  14.5 us
    dot_general x10, matrix products, matmul(): lax.dot_general(left, right, (((left_dim,), (right_dim,)), ((), ())), pre...  6.98 us
    unnamed x20, local copies, waits for them, and re-layouts  4.77 us
    pallas_call x1, Pallas kernels, assemble(): pl.pallas_call(assemble_kernel, out_shape=jax.ShapeDtypeStruct((2, rows /...  4.59 us
  transfers between devices with their start and end apart: 29, of which 8 were waited for; matrix products, arithmetic and copies ran while one was open for 13% of the time, Pallas kernels for 7%

profile of v1, /device:TPU:0, one launch (start us, length us, event | category | flops | bytes accessed | tf_op | source)
XLA Modules:
  0.0 70.5 jit_solution(11893646989624613517)
XLA Ops:
  0.6 3.1 %collective-permute-start = (bf16[256,256]{1,0:T(8,128)(2,1)}, bf16[256,256]{1,0:T(8,128)(2,1)S(1)}, u32[]{:S(2)}, u32[]{:S(2)}) collective-permute-start(bf16[256,256]{1,0:T(8,128)(2,1)} %param.7), channel_id=1, source_target_pairs={{0,1},{1,0},{2,3},{3,2},{4,5},{5,4},{6,7},{7,6},{8,9},{9,8},{10,11... | collective-permute-start | bytes 393224 | tf_op jit(solution)/shard_map/ppermute | solution.py:81
  3.7 2.6 %collective-permute-start.1 = (bf16[256,256]{1,0:T(8,128)(2,1)}, bf16[256,256]{1,0:T(8,128)(2,1)S(1)}, u32[]{:S(2)}, u32[]{:S(2)}) collective-permute-start(bf16[256,256]{1,0:T(8,128)(2,1)} %param.7), channel_id=1, source_target_pairs={{0,2},{1,3},{2,0},{3,1},{4,6},{5,7},{6,4},{7,5},{8,10},{9,11},{10,... | collective-permute-start | bytes 393224 | tf_op jit(solution)/shard_map/ppermute | solution.py:81
  6.3 1.7 %collective-permute-start.14 = (bf16[256,128]{1,0:T(8,128)(2,1)}, bf16[256,128]{1,0:T(8,128)(2,1)S(1)}, u32[]{:S(2)}, u32[]{:S(2)}) collective-permute-start(bf16[256,128]{1,0:T(8,128)(2,1)} %param.13), channel_id=1, source_target_pairs={{0,8},{4,12},{8,0},{12,4},{16,24},{20,28},{24,16},{28,20},{1,9},{5... | collective-permute-start | bytes 196616 | tf_op jit(solution)/shard_map/ppermute | solution.py:81
  8.0 1.5 %collective-permute-start.15 = (bf16[256,128]{1,0:T(8,128)(2,1)}, bf16[256,128]{1,0:T(8,128)(2,1)S(1)}, u32[]{:S(2)}, u32[]{:S(2)}) collective-permute-start(bf16[256,128]{1,0:T(8,128)(2,1)} %param.13), channel_id=1, source_target_pairs={{0,16},{4,20},{8,24},{12,28},{16,0},{20,4},{24,8},{28,12},{1,17},{... | collective-permute-start | bytes 196616 | tf_op jit(solution)/shard_map/ppermute | solution.py:81
  12.6 2.2 %copy-done.3 = bf16[1,1,128,128,128]{4,3,2,1,0:T(8,128)(2,1)S(1)} copy-done((bf16[1,1,128,128,128]{4,3,2,1,0:T(8,128)(2,1)S(1)}, bf16[1,1,128,128,128]{4,3,2,1,0:T(8,128)(2,1)}, u32[]{:S(2)}) %copy-start.3) | copy-done | bytes 4194328
  14.8 4.6 %shard_map.94 = bf16[2,1024,1024]{2,1,0:T(8,128)(2,1)S(1)} custom-call(s32[3,128]{1,0:T(4,128)S(1)} %pad_add_fusion.places_ref, s32[1]{0:T(128)} %bitcast.73.count_ref, bf16[128,128,128]{2,1,0:T(8,128)(2,1)S(1)} %bitcast.74), custom_call_target="tpu_custom_call" | custom-call | bytes 8388608 | tf_op jit(solution)/shard_map/pallas_call | solution.py:55
  19.5 1.2 %collective-permute-start.16 = (bf16[256,128]{1,0:T(8,128)(2,1)S(1)}, bf16[256,128]{1,0:T(8,128)(2,1)S(1)}, u32[]{:S(2)}, u32[]{:S(2)}) collective-permute-start(bf16[256,128]{1,0:T(8,128)(2,1)S(1)} %copy-done.4), channel_id=1, source_target_pairs={{0,24},{4,28},{8,16},{12,20},{16,8},{20,12},{24,0},{28,4},{1,25},{... | collective-permute-start | bytes 196616 | tf_op jit(solution)/shard_map/ppermute | solution.py:81
  20.7 4.0 %collective-permute-done.16 = bf16[256,128]{1,0:T(8,128)(2,1)S(1)} collective-permute-done((bf16[256,128]{1,0:T(8,128)(2,1)S(1)}, bf16[256,128]{1,0:T(8,128)(2,1)S(1)}, u32[]{:S(2)}, u32[]{:S(2)}) %collective-permute-start.16) | collective-permute-done | bytes 65568 | tf_op jit(solution)/shard_map/ppermute | solution.py:81
  27.8 3.9 %collective-permute-start.20 = (bf16[256,128]{1,0:T(8,128)(2,1)S(1)}, bf16[256,128]{1,0:T(8,128)(2,1)S(1)}, u32[]{:S(2)}, u32[]{:S(2)}) collective-permute-start(bf16[256,128]{1,0:T(8,128)(2,1)S(1)} %get-tuple-element.14), channel_id=1, source_target_pairs={{0,3},{1,2},{2,1},{3,0},{4,7},{5,6},{6,5},{7,4},{8,11},{9,10},{10,... | collective-permute-start | bytes 196616 | tf_op jit(solution)/shard_map/ppermute | solution.py:81
  33.1 1.1 %collective-permute-start.6 = (bf16[256,256]{1,0:T(8,128)(2,1)S(1)}, bf16[256,256]{1,0:T(8,128)(2,1)S(1)}, u32[]{:S(2)}, u32[]{:S(2)}) collective-permute-start(bf16[256,256]{1,0:T(8,128)(2,1)S(1)} %get-tuple-element.9), channel_id=1, source_target_pairs={{0,24},{4,28},{8,16},{12,20},{16,8},{20,12},{24,0},{28,4},{1,25},{... | collective-permute-start | bytes 393224 | tf_op jit(solution)/shard_map/ppermute | solution.py:81
  34.2 1.5 %collective-permute-start.5 = (bf16[256,256]{1,0:T(8,128)(2,1)S(1)}, bf16[256,256]{1,0:T(8,128)(2,1)S(1)}, u32[]{:S(2)}, u32[]{:S(2)}) collective-permute-start(bf16[256,256]{1,0:T(8,128)(2,1)S(1)} %get-tuple-element.10), channel_id=1, source_target_pairs={{0,16},{4,20},{8,24},{12,28},{16,0},{20,4},{24,8},{28,12},{1,17},{... | collective-permute-start | bytes 393224 | tf_op jit(solution)/shard_map/ppermute | solution.py:81
  35.7 1.0 %collective-permute-start.4 = (bf16[256,256]{1,0:T(8,128)(2,1)S(1)}, bf16[256,256]{1,0:T(8,128)(2,1)S(1)}, u32[]{:S(2)}, u32[]{:S(2)}) collective-permute-start(bf16[256,256]{1,0:T(8,128)(2,1)S(1)} %get-tuple-element.8), channel_id=1, source_target_pairs={{0,8},{4,12},{8,0},{12,4},{16,24},{20,28},{24,16},{28,20},{1,9},{5... | collective-permute-start | bytes 393224 | tf_op jit(solution)/shard_map/ppermute | solution.py:81
  37.4 3.1 %collective-permute-done.6 = bf16[256,256]{1,0:T(8,128)(2,1)S(1)} collective-permute-done((bf16[256,256]{1,0:T(8,128)(2,1)S(1)}, bf16[256,256]{1,0:T(8,128)(2,1)S(1)}, u32[]{:S(2)}, u32[]{:S(2)}) %collective-permute-start.6) | collective-permute-done | bytes 131104 | tf_op jit(solution)/shard_map/ppermute | solution.py:81
  40.5 1.0 %collective-permute-done.5 = bf16[256,256]{1,0:T(8,128)(2,1)S(1)} collective-permute-done((bf16[256,256]{1,0:T(8,128)(2,1)S(1)}, bf16[256,256]{1,0:T(8,128)(2,1)S(1)}, u32[]{:S(2)}, u32[]{:S(2)}) %collective-permute-start.5) | collective-permute-done | bytes 131104 | tf_op jit(solution)/shard_map/ppermute | solution.py:81
  42.9 3.5 %collective-permute-start.9 = (bf16[256,128]{1,0:T(8,128)(2,1)S(1)}, bf16[256,128]{1,0:T(8,128)(2,1)S(1)}, u32[]{:S(2)}, u32[]{:S(2)}) collective-permute-start(bf16[256,128]{1,0:T(8,128)(2,1)S(1)} %convolution_convert_fusion), channel_id=1, source_target_pairs={{0,3},{1,2},{2,1},{3,0},{4,7},{5,6},{6,5},{7,4},{8,11},{9,10},{10,... | collective-permute-start | bytes 196616 | tf_op jit(solution)/shard_map/ppermute | solution.py:81
  47.4 1.5 %collective-permute-start.24 = (bf16[128,384]{0,1:T(8,128)(2,1)S(1)}, bf16[128,384]{0,1:T(8,128)(2,1)S(1)}, u32[]{:S(2)}, u32[]{:S(2)}) collective-permute-start(bf16[128,384]{0,1:T(8,128)(2,1)S(1)} %add_convert_fusion.1), channel_id=1, source_target_pairs={{0,24},{4,28},{8,16},{12,20},{16,8},{20,12},{24,0},{28,4},{1,25},{... | collective-permute-start | bytes 294920 | tf_op jit(solution)/shard_map/ppermute | solution.py:81
  48.8 1.5 %collective-permute-start.23 = (bf16[128,384]{0,1:T(8,128)(2,1)S(1)}, bf16[128,384]{0,1:T(8,128)(2,1)S(1)}, u32[]{:S(2)}, u32[]{:S(2)}) collective-permute-start(bf16[128,384]{0,1:T(8,128)(2,1)S(1)} %add_convert_fusion.1), channel_id=1, source_target_pairs={{0,16},{4,20},{8,24},{12,28},{16,0},{20,4},{24,8},{28,12},{1,17},{... | collective-permute-start | bytes 294920 | tf_op jit(solution)/shard_map/ppermute | solution.py:81
  51.1 1.4 %collective-permute-done.8 = bf16[256,128]{1,0:T(8,128)(2,1)S(1)} collective-permute-done((bf16[256,128]{1,0:T(8,128)(2,1)S(1)}, bf16[256,128]{1,0:T(8,128)(2,1)S(1)}, u32[]{:S(2)}, u32[]{:S(2)}) %collective-permute-start.8) | collective-permute-done | bytes 65568 | tf_op jit(solution)/shard_map/ppermute | solution.py:81
  52.5 2.3 %fusion.10 = bf16[1024,128]{1,0:T(8,128)(2,1)S(1)} fusion(bf16[2,1024,1024]{2,1,0:T(8,128)(2,1)} %copy-done.1, bf16[256,128]{1,0:T(8,128)(2,1)S(1)} %collective-permute-done.9, bf16[256,128]{1,0:T(8,128)(2,1)S(1)} %collective-permute-done.8, bf16[256,128]{1,0:T(8,128)(2,1)S(1)} %collective-permute-done.7, bf16[256,128]{1,0:T(8,128)(2,1)S(1)} %convolution_convert_fusion), kind=kOutput, calls=%fused_computation.12 | convolution fusion | flops 269615104 | bytes 2621440 | tf_op jit(solution)/shard_map/dot_general | solution.py:85
  55.0 3.5 %collective-permute-start.27 = (bf16[128,384]{0,1:T(8,128)(2,1)S(1)}, bf16[128,384]{0,1:T(8,128)(2,1)S(1)}, u32[]{:S(2)}, u32[]{:S(2)}) collective-permute-start(bf16[128,384]{0,1:T(8,128)(2,1)S(1)} %add_convert_fusion), channel_id=1, source_target_pairs={{0,3},{1,2},{2,1},{3,0},{4,7},{5,6},{6,5},{7,4},{8,11},{9,10},{10,... | collective-permute-start | bytes 294920 | tf_op jit(solution)/shard_map/ppermute | solution.py:81
  58.5 0.9 %collective-permute-start.25 = (bf16[128,384]{0,1:T(8,128)(2,1)S(1)}, bf16[128,384]{0,1:T(8,128)(2,1)S(1)}, u32[]{:S(2)}, u32[]{:S(2)}) collective-permute-start(bf16[128,384]{0,1:T(8,128)(2,1)S(1)} %add_convert_fusion), channel_id=1, source_target_pairs={{0,1},{1,0},{2,3},{3,2},{4,5},{5,4},{6,7},{7,6},{8,9},{9,8},{10,11... | collective-permute-start | bytes 294920 | tf_op jit(solution)/shard_map/ppermute | solution.py:81
  60.2 1.5 %collective-permute-start.13 = (bf16[256,128]{1,0:T(8,128)(2,1)S(1)}, bf16[256,128]{1,0:T(8,128)(2,1)S(1)}, u32[]{:S(2)}, u32[]{:S(2)}) collective-permute-start(bf16[256,128]{1,0:T(8,128)(2,1)S(1)} %get-tuple-element.17), channel_id=1, source_target_pairs={{0,24},{4,28},{8,16},{12,20},{16,8},{20,12},{24,0},{28,4},{1,25},{... | collective-permute-start | bytes 196616 | tf_op jit(solution)/shard_map/ppermute | solution.py:81
  61.7 1.4 %collective-permute-start.12 = (bf16[256,128]{1,0:T(8,128)(2,1)S(1)}, bf16[256,128]{1,0:T(8,128)(2,1)S(1)}, u32[]{:S(2)}, u32[]{:S(2)}) collective-permute-start(bf16[256,128]{1,0:T(8,128)(2,1)S(1)} %get-tuple-element.18), channel_id=1, source_target_pairs={{0,16},{4,20},{8,24},{12,28},{16,0},{20,4},{24,8},{28,12},{1,17},{... | collective-permute-start | bytes 196616 | tf_op jit(solution)/shard_map/ppermute | solution.py:81
  63.9 3.3 %collective-permute-done.26 = bf16[128,384]{0,1:T(8,128)(2,1)S(1)} collective-permute-done((bf16[128,384]{0,1:T(8,128)(2,1)S(1)}, bf16[128,384]{0,1:T(8,128)(2,1)S(1)}, u32[]{:S(2)}, u32[]{:S(2)}) %collective-permute-start.26) | collective-permute-done | bytes 98336 | tf_op jit(solution)/shard_map/ppermute | solution.py:81
  (84 shorter events, 15.6 us)
Async XLA Ops:
  0.6 24.1 %collective-permute-start = (bf16[256,256]{1,0:T(8,128)(2,1)}, bf16[256,256]{1,0:T(8,128)(2,1)S(1)}, u32[]{:S(2)}, u32[]{:S(2)}) collective-permute-start(bf16[256,256]{1,0:T(8,128)(2,1)} %param.7), channel_id=1, source_target_pairs={{0,1},{1,0},{2,3},{3,2},{4,5},{5,4},{6,7},{7,6},{8,9},{9,8},{10,11... | collective-permute-start | bytes 393224 | tf_op jit(solution)/shard_map/ppermute | solution.py:81
  3.7 21.1 %collective-permute-start.1 = (bf16[256,256]{1,0:T(8,128)(2,1)}, bf16[256,256]{1,0:T(8,128)(2,1)S(1)}, u32[]{:S(2)}, u32[]{:S(2)}) collective-permute-start(bf16[256,256]{1,0:T(8,128)(2,1)} %param.7), channel_id=1, source_target_pairs={{0,2},{1,3},{2,0},{3,1},{4,6},{5,7},{6,4},{7,5},{8,10},{9,11},{10,... | collective-permute-start | bytes 393224 | tf_op jit(solution)/shard_map/ppermute | solution.py:81
  6.3 18.5 %collective-permute-start.2 = (bf16[256,256]{1,0:T(8,128)(2,1)}, bf16[256,256]{1,0:T(8,128)(2,1)S(1)}, u32[]{:S(2)}, u32[]{:S(2)}) collective-permute-start(bf16[256,256]{1,0:T(8,128)(2,1)} %param.7), channel_id=1, source_target_pairs={{0,3},{1,2},{2,1},{3,0},{4,7},{5,6},{6,5},{7,4},{8,11},{9,10},{10,... | collective-permute-start | bytes 393224 | tf_op jit(solution)/shard_map/ppermute | solution.py:81
  6.3 13.1 %collective-permute-start.14 = (bf16[256,128]{1,0:T(8,128)(2,1)}, bf16[256,128]{1,0:T(8,128)(2,1)S(1)}, u32[]{:S(2)}, u32[]{:S(2)}) collective-permute-start(bf16[256,128]{1,0:T(8,128)(2,1)} %param.13), channel_id=1, source_target_pairs={{0,8},{4,12},{8,0},{12,4},{16,24},{20,28},{24,16},{28,20},{1,9},{5... | collective-permute-start | bytes 196616 | tf_op jit(solution)/shard_map/ppermute | solution.py:81
  8.0 12.6 %collective-permute-start.15 = (bf16[256,128]{1,0:T(8,128)(2,1)}, bf16[256,128]{1,0:T(8,128)(2,1)S(1)}, u32[]{:S(2)}, u32[]{:S(2)}) collective-permute-start(bf16[256,128]{1,0:T(8,128)(2,1)} %param.13), channel_id=1, source_target_pairs={{0,16},{4,20},{8,24},{12,28},{16,0},{20,4},{24,8},{28,12},{1,17},{... | collective-permute-start | bytes 196616 | tf_op jit(solution)/shard_map/ppermute | solution.py:81
  19.5 5.2 %collective-permute-start.16 = (bf16[256,128]{1,0:T(8,128)(2,1)S(1)}, bf16[256,128]{1,0:T(8,128)(2,1)S(1)}, u32[]{:S(2)}, u32[]{:S(2)}) collective-permute-start(bf16[256,128]{1,0:T(8,128)(2,1)S(1)} %copy-done.4), channel_id=1, source_target_pairs={{0,24},{4,28},{8,16},{12,20},{16,8},{20,12},{24,0},{28,4},{1,25},{... | collective-permute-start | bytes 196616 | tf_op jit(solution)/shard_map/ppermute | solution.py:81
  25.6 6.8 %collective-permute-start.3 = (bf16[1024,256]{1,0:T(8,128)(2,1)S(1)}, bf16[1024,256]{1,0:T(8,128)(2,1)S(1)}, u32[]{:S(2)}, u32[]{:S(2)}) collective-permute-start(bf16[1024,256]{1,0:T(8,128)(2,1)S(1)} %fusion.7), channel_id=1, source_target_pairs={{0,4},{4,0},{8,12},{12,8},{16,20},{20,16},{24,28},{28,24},{1,5},{5... | collective-permute-start | bytes 1572872 | tf_op jit(solution)/shard_map/ppermute | solution.py:81
  27.8 7.9 %collective-permute-start.20 = (bf16[256,128]{1,0:T(8,128)(2,1)S(1)}, bf16[256,128]{1,0:T(8,128)(2,1)S(1)}, u32[]{:S(2)}, u32[]{:S(2)}) collective-permute-start(bf16[256,128]{1,0:T(8,128)(2,1)S(1)} %get-tuple-element.14), channel_id=1, source_target_pairs={{0,3},{1,2},{2,1},{3,0},{4,7},{5,6},{6,5},{7,4},{8,11},{9,10},{10,... | collective-permute-start | bytes 196616 | tf_op jit(solution)/shard_map/ppermute | solution.py:81
  31.7 5.7 %collective-permute-start.19 = (bf16[256,128]{1,0:T(8,128)(2,1)S(1)}, bf16[256,128]{1,0:T(8,128)(2,1)S(1)}, u32[]{:S(2)}, u32[]{:S(2)}) collective-permute-start(bf16[256,128]{1,0:T(8,128)(2,1)S(1)} %get-tuple-element.15), channel_id=1, source_target_pairs={{0,2},{1,3},{2,0},{3,1},{4,6},{5,7},{6,4},{7,5},{8,10},{9,11},{10,... | collective-permute-start | bytes 196616 | tf_op jit(solution)/shard_map/ppermute | solution.py:81
  31.7 5.7 %collective-permute-start.18 = (bf16[256,128]{1,0:T(8,128)(2,1)S(1)}, bf16[256,128]{1,0:T(8,128)(2,1)S(1)}, u32[]{:S(2)}, u32[]{:S(2)}) collective-permute-start(bf16[256,128]{1,0:T(8,128)(2,1)S(1)} %get-tuple-element.13), channel_id=1, source_target_pairs={{0,1},{1,0},{2,3},{3,2},{4,5},{5,4},{6,7},{7,6},{8,9},{9,8},{10,11... | collective-permute-start | bytes 196616 | tf_op jit(solution)/shard_map/ppermute | solution.py:81
  33.1 7.4 %collective-permute-start.6 = (bf16[256,256]{1,0:T(8,128)(2,1)S(1)}, bf16[256,256]{1,0:T(8,128)(2,1)S(1)}, u32[]{:S(2)}, u32[]{:S(2)}) collective-permute-start(bf16[256,256]{1,0:T(8,128)(2,1)S(1)} %get-tuple-element.9), channel_id=1, source_target_pairs={{0,24},{4,28},{8,16},{12,20},{16,8},{20,12},{24,0},{28,4},{1,25},{... | collective-permute-start | bytes 393224 | tf_op jit(solution)/shard_map/ppermute | solution.py:81
  34.2 7.3 %collective-permute-start.5 = (bf16[256,256]{1,0:T(8,128)(2,1)S(1)}, bf16[256,256]{1,0:T(8,128)(2,1)S(1)}, u32[]{:S(2)}, u32[]{:S(2)}) collective-permute-start(bf16[256,256]{1,0:T(8,128)(2,1)S(1)} %get-tuple-element.10), channel_id=1, source_target_pairs={{0,16},{4,20},{8,24},{12,28},{16,0},{20,4},{24,8},{28,12},{1,17},{... | collective-permute-start | bytes 393224 | tf_op jit(solution)/shard_map/ppermute | solution.py:81
  35.7 5.8 %collective-permute-start.4 = (bf16[256,256]{1,0:T(8,128)(2,1)S(1)}, bf16[256,256]{1,0:T(8,128)(2,1)S(1)}, u32[]{:S(2)}, u32[]{:S(2)}) collective-permute-start(bf16[256,256]{1,0:T(8,128)(2,1)S(1)} %get-tuple-element.8), channel_id=1, source_target_pairs={{0,8},{4,12},{8,0},{12,4},{16,24},{20,28},{24,16},{28,20},{1,9},{5... | collective-permute-start | bytes 393224 | tf_op jit(solution)/shard_map/ppermute | solution.py:81
  42.6 4.7 %collective-permute-start.21 = (bf16[128,384]{0,1:T(8,128)(2,1)S(1)}, bf16[128,384]{0,1:T(8,128)(2,1)S(1)}, u32[]{:S(2)}, u32[]{:S(2)}) collective-permute-start(bf16[128,384]{0,1:T(8,128)(2,1)S(1)} %select_convert_fusion), channel_id=1, source_target_pairs={{0,4},{4,0},{8,12},{12,8},{16,20},{20,16},{24,28},{28,24},{1,5},{5... | collective-permute-start | bytes 294920 | tf_op jit(solution)/shard_map/ppermute | solution.py:81
  42.9 7.4 %collective-permute-start.9 = (bf16[256,128]{1,0:T(8,128)(2,1)S(1)}, bf16[256,128]{1,0:T(8,128)(2,1)S(1)}, u32[]{:S(2)}, u32[]{:S(2)}) collective-permute-start(bf16[256,128]{1,0:T(8,128)(2,1)S(1)} %convolution_convert_fusion), channel_id=1, source_target_pairs={{0,3},{1,2},{2,1},{3,0},{4,7},{5,6},{6,5},{7,4},{8,11},{9,10},{10,... | collective-permute-start | bytes 196616 | tf_op jit(solution)/shard_map/ppermute | solution.py:81
  46.4 6.1 %collective-permute-start.8 = (bf16[256,128]{1,0:T(8,128)(2,1)S(1)}, bf16[256,128]{1,0:T(8,128)(2,1)S(1)}, u32[]{:S(2)}, u32[]{:S(2)}) collective-permute-start(bf16[256,128]{1,0:T(8,128)(2,1)S(1)} %convolution_convert_fusion), channel_id=1, source_target_pairs={{0,2},{1,3},{2,0},{3,1},{4,6},{5,7},{6,4},{7,5},{8,10},{9,11},{10,... | collective-permute-start | bytes 196616 | tf_op jit(solution)/shard_map/ppermute | solution.py:81
  46.4 6.1 %collective-permute-start.7 = (bf16[256,128]{1,0:T(8,128)(2,1)S(1)}, bf16[256,128]{1,0:T(8,128)(2,1)S(1)}, u32[]{:S(2)}, u32[]{:S(2)}) collective-permute-start(bf16[256,128]{1,0:T(8,128)(2,1)S(1)} %convolution_convert_fusion), channel_id=1, source_target_pairs={{0,1},{1,0},{2,3},{3,2},{4,5},{5,4},{6,7},{7,6},{8,9},{9,8},{10,11... | collective-permute-start | bytes 196616 | tf_op jit(solution)/shard_map/ppermute | solution.py:81
  47.4 7.5 %collective-permute-start.24 = (bf16[128,384]{0,1:T(8,128)(2,1)S(1)}, bf16[128,384]{0,1:T(8,128)(2,1)S(1)}, u32[]{:S(2)}, u32[]{:S(2)}) collective-permute-start(bf16[128,384]{0,1:T(8,128)(2,1)S(1)} %add_convert_fusion.1), channel_id=1, source_target_pairs={{0,24},{4,28},{8,16},{12,20},{16,8},{20,12},{24,0},{28,4},{1,25},{... | collective-permute-start | bytes 294920 | tf_op jit(solution)/shard_map/ppermute | solution.py:81
  48.8 6.0 %collective-permute-start.23 = (bf16[128,384]{0,1:T(8,128)(2,1)S(1)}, bf16[128,384]{0,1:T(8,128)(2,1)S(1)}, u32[]{:S(2)}, u32[]{:S(2)}) collective-permute-start(bf16[128,384]{0,1:T(8,128)(2,1)S(1)} %add_convert_fusion.1), channel_id=1, source_target_pairs={{0,16},{4,20},{8,24},{12,28},{16,0},{20,4},{24,8},{28,12},{1,17},{... | collective-permute-start | bytes 294920 | tf_op jit(solution)/shard_map/ppermute | solution.py:81
  55.0 8.1 %collective-permute-start.27 = (bf16[128,384]{0,1:T(8,128)(2,1)S(1)}, bf16[128,384]{0,1:T(8,128)(2,1)S(1)}, u32[]{:S(2)}, u32[]{:S(2)}) collective-permute-start(bf16[128,384]{0,1:T(8,128)(2,1)S(1)} %add_convert_fusion), channel_id=1, source_target_pairs={{0,3},{1,2},{2,1},{3,0},{4,7},{5,6},{6,5},{7,4},{8,11},{9,10},{10,... | collective-permute-start | bytes 294920 | tf_op jit(solution)/shard_map/ppermute | solution.py:81
  58.5 8.7 %collective-permute-start.26 = (bf16[128,384]{0,1:T(8,128)(2,1)S(1)}, bf16[128,384]{0,1:T(8,128)(2,1)S(1)}, u32[]{:S(2)}, u32[]{:S(2)}) collective-permute-start(bf16[128,384]{0,1:T(8,128)(2,1)S(1)} %add_convert_fusion), channel_id=1, source_target_pairs={{0,2},{1,3},{2,0},{3,1},{4,6},{5,7},{6,4},{7,5},{8,10},{9,11},{10,... | collective-permute-start | bytes 294920 | tf_op jit(solution)/shard_map/ppermute | solution.py:81
  58.5 8.7 %collective-permute-start.25 = (bf16[128,384]{0,1:T(8,128)(2,1)S(1)}, bf16[128,384]{0,1:T(8,128)(2,1)S(1)}, u32[]{:S(2)}, u32[]{:S(2)}) collective-permute-start(bf16[128,384]{0,1:T(8,128)(2,1)S(1)} %add_convert_fusion), channel_id=1, source_target_pairs={{0,1},{1,0},{2,3},{3,2},{4,5},{5,4},{6,7},{7,6},{8,9},{9,8},{10,11... | collective-permute-start | bytes 294920 | tf_op jit(solution)/shard_map/ppermute | solution.py:81
  60.2 7.2 %collective-permute-start.13 = (bf16[256,128]{1,0:T(8,128)(2,1)S(1)}, bf16[256,128]{1,0:T(8,128)(2,1)S(1)}, u32[]{:S(2)}, u32[]{:S(2)}) collective-permute-start(bf16[256,128]{1,0:T(8,128)(2,1)S(1)} %get-tuple-element.17), channel_id=1, source_target_pairs={{0,24},{4,28},{8,16},{12,20},{16,8},{20,12},{24,0},{28,4},{1,25},{... | collective-permute-start | bytes 196616 | tf_op jit(solution)/shard_map/ppermute | solution.py:81
  61.7 5.7 %collective-permute-start.12 = (bf16[256,128]{1,0:T(8,128)(2,1)S(1)}, bf16[256,128]{1,0:T(8,128)(2,1)S(1)}, u32[]{:S(2)}, u32[]{:S(2)}) collective-permute-start(bf16[256,128]{1,0:T(8,128)(2,1)S(1)} %get-tuple-element.18), channel_id=1, source_target_pairs={{0,16},{4,20},{8,24},{12,28},{16,0},{20,4},{24,8},{28,12},{1,17},{... | collective-permute-start | bytes 196616 | tf_op jit(solution)/shard_map/ppermute | solution.py:81
  (11 other events, 104.7 us)

commit v2 on v1

v2 whole, which is shorter than its diff:
```python
import math

import jax
import jax.numpy as jnp
from jax import lax
from jax.experimental import pallas as pl
from jax.experimental.pallas import tpu as pltpu
from jax.sharding import PartitionSpec as P

BF16 = jnp.bfloat16
F32 = jnp.float32


def dot_parts(left, right, left_dim=1, right_dim=0):
    def parts(value):
        if value.dtype == BF16:
            return [value]
        high = lax.reduce_precision(value, 8, 7)
        return [high.astype(BF16), (value - high).astype(BF16)]

    lefts, rights = parts(left), parts(right)
    total = None
    for i, one in enumerate(lefts):
        for j, other in enumerate(rights):
            if i + j < 2:
                term = lax.dot_general(
                    one, other, (((left_dim,), (right_dim,)), ((), ())), preferred_element_type=F32
                )
                total = term if total is None else total + term
    return total


def tree_sum(parts):
    parts = [part.astype(F32) for part in parts]
    while len(parts) > 1:
        parts = [parts[i] + parts[i + 1] for i in range(0, len(parts), 2)]
    return parts[0]


def assemble_kernel(per_node, coords_ref, count_ref, tiles_ref, dense_ref, sem):
    slots, edge = tiles_ref.shape[0], tiles_ref.shape[1]
    halves, rows, cols = dense_ref.shape
    me_row, me_col = lax.axis_index("row"), lax.axis_index("col")
    live = count_ref[0]
    strip = math.gcd(rows, 256)
    shift = per_node.bit_length() - 1

    @pl.when(live * edge * edge < halves * rows * cols)
    def _():
        def clear(step, carry):
            place = pl.ds(pl.multiple_of(step * strip, strip), strip)
            for half in range(halves):
                dense_ref[half, place, :] = jnp.zeros((strip, cols), BF16)
            return carry

        lax.fori_loop(0, rows // strip, clear, 0)

    def begin(slot):
        row, col = coords_ref[0, slot], coords_ref[1, slot]
        offset = (row >> shift) ^ me_row
        row_place = ((offset >> 1) << shift) + (row & (per_node - 1))
        col_place = (((col >> shift) ^ me_col) << shift) + (col & (per_node - 1))
        pltpu.make_async_copy(
            tiles_ref.at[slot],
            dense_ref.at[
                offset & 1,
                pl.ds(pl.multiple_of(row_place * edge, edge), edge),
                pl.ds(pl.multiple_of(col_place * edge, edge), edge),
            ],
            sem,
        ).start()

    def begin_group(step, carry):
        for i in range(8):
            begin(step * 8 + i)
        return carry

    def begin_one(slot, carry):
        begin(slot)
        return carry

    groups = live >> 3
    lax.fori_loop(0, groups, begin_group, 0)
    lax.fori_loop(groups << 3, live, begin_one, 0)
    size = 1
    while size <= slots:

        @pl.when((live & size) != 0)
        def _(size=size):
            some = tiles_ref.at[pl.ds(0, size)]
            pltpu.make_async_copy(some, some, sem).wait()

        size *= 2


def assemble(tiles, coords, count, rows, cols, per_node):
    def kernel(*refs):
        assemble_kernel(per_node, *refs)

    return pl.pallas_call(
        kernel,
        out_shape=jax.ShapeDtypeStruct((2, rows // 2, cols), BF16),
        in_specs=[
            pl.BlockSpec(memory_space=pltpu.SMEM),
            pl.BlockSpec(memory_space=pltpu.SMEM),
            pl.BlockSpec(memory_space=pltpu.HBM),
        ],
        out_specs=pl.BlockSpec(memory_space=pltpu.VMEM),
        scratch_shapes=[pltpu.SemaphoreType.DMA],
        compiler_params=pltpu.CompilerParams(vmem_limit_bytes=rows * cols * 2 + (2 << 20)),
        cost_estimate=pl.CostEstimate(
            flops=0, bytes_accessed=2 * rows * cols * 2, transcendentals=0
        ),
        name="assemble",
    )(coords, count, tiles)


def local_grads_kernel(scale, grid_cols, *refs):
    mean_ref, pre_ref, back_ref = refs[:3]
    arrived_refs = refs[3 : 2 + grid_cols]
    weight_ref, mine_ref, theirs_ref = refs[2 + grid_cols :]
    back_sum = tree_sum([back_ref[: mean_ref.shape[0], :]] + [ref[...] for ref in arrived_refs])
    hidden_grad = dot_parts(back_sum, weight_ref[...], 1, 1)
    first_pre = pre_ref[...]
    sigma = jax.nn.sigmoid(first_pre)
    hidden_act = (first_pre * sigma).astype(BF16)
    pre_grad = hidden_grad * (sigma * (1.0 + first_pre * (1.0 - sigma)))
    first = dot_parts(mean_ref[...], pre_grad, 0, 0) * scale
    second = dot_parts(hidden_act, back_sum, 0, 0) * scale
    half, width = mine_ref.shape[0], first.shape[1]
    low_core = lax.axis_index("row") % 2 == 0
    for value, place in ((first, slice(0, width)), (second, slice(width, None))):
        low, high = value[:half], value[half:]
        mine_ref[:, place] = jnp.where(low_core, low, high)
        theirs_ref[:, place] = jnp.where(low_core, high, low).astype(BF16)


def local_grads(mean, pre, back, arrived, weight, scale):
    grid_cols = len(arrived) + 1
    half = mean.shape[1] // 2
    width = pre.shape[1] + weight.shape[1]

    def kernel(*refs):
        local_grads_kernel(scale, grid_cols, *refs)

    vmem = pl.BlockSpec(memory_space=pltpu.VMEM)
    return pl.pallas_call(
        kernel,
        out_shape=(
            jax.ShapeDtypeStruct((half, width), F32),
            jax.ShapeDtypeStruct((half, width), BF16),
        ),
        in_specs=[vmem] * (4 + len(arrived)),
        out_specs=(vmem, vmem),
        compiler_params=pltpu.CompilerParams(vmem_limit_bytes=6 << 20),
        cost_estimate=pl.CostEstimate(
            flops=2 * 256 * 256 * 384 * 3, bytes_accessed=1 << 20, transcendentals=1 << 16
        ),
        name="local_grads",
    )(mean, pre, back, *arrived, weight)


def join_kernel(mine_ref, theirs_ref, first_ref, second_ref):
    half, width = mine_ref.shape[0], first_ref.shape[1]
    low_core = lax.axis_index("row") % 2 == 0
    for ref, place in ((first_ref, slice(0, width)), (second_ref, slice(width, None))):
        mine, theirs = mine_ref[:, place], theirs_ref[:, place]
        ref[:half, :] = jnp.where(low_core, mine, theirs)
        ref[half:, :] = jnp.where(low_core, theirs, mine)


def join(mine, theirs, width):
    vmem = pl.BlockSpec(memory_space=pltpu.VMEM)
    rows = 2 * mine.shape[0]
    return pl.pallas_call(
        join_kernel,
        out_shape=(
            jax.ShapeDtypeStruct((rows, width), F32),
            jax.ShapeDtypeStruct((rows, mine.shape[1] - width), F32),
        ),
        in_specs=[vmem, vmem],
        out_specs=(vmem, vmem),
        compiler_params=pltpu.CompilerParams(vmem_limit_bytes=2 << 20),
        name="join_grads",
    )(mine, theirs)


def swap(value, axis, offset):
    size = lax.axis_size(axis)
    return lax.ppermute(value, axis, [(i, i ^ offset) for i in range(size)])


def on_device(
    node_features, tile_values, tile_coords, tile_counts, first_weight, second_weight, out_grad
):
    node_rows = node_features.shape[0]
    edge = tile_values.shape[-1]
    slots = tile_values.shape[2]
    grid_rows = lax.axis_size("row")
    grid_cols = lax.axis_size("col")
    chips = grid_rows // 2
    per_node = node_rows // edge

    def gather_col(value):
        return jnp.concatenate(
            [value] + [swap(value, "col", k) for k in range(1, grid_cols)], axis=0
        )

    gathered_x = gather_col(node_features)
    dense = assemble(
        tile_values.reshape(slots, edge, edge),
        tile_coords.reshape(slots, 2).T,
        tile_counts.reshape(1),
        grid_rows * node_rows,
        grid_cols * node_rows,
        per_node,
    )
    dense_own, dense_other = dense[0], dense[1]
    grad_own = jnp.concatenate(
        [out_grad] + [swap(out_grad, "row", 2 * i) for i in range(1, chips)], axis=0
    )

    def chip_blocks(source):
        other = dot_parts(dense_other, source).astype(BF16)
        arrived = swap(other, "row", 1)
        chip_sum = dot_parts(dense_own, source) + arrived.astype(F32)
        return chip_sum.reshape(chips, node_rows, -1)

    def plane_sum(blocks):
        return tree_sum(
            [blocks[0]]
            + [swap(blocks[i].astype(BF16), "row", 2 * i) for i in range(1, chips)]
        )

    gathered_x, grad_own = lax.optimization_barrier((gathered_x, grad_own))
    grad_other = swap(grad_own, "row", 1)
    first_blocks = chip_blocks(gathered_x)

    first_blocks, grad_own, grad_other = lax.optimization_barrier(
        (first_blocks, grad_own, grad_other)
    )
    first_mean = plane_sum(first_blocks)
    back_part = dot_parts(dense_own, grad_own, 0) + dot_parts(dense_other, grad_other, 0)
    back_blocks = back_part.reshape(grid_cols, node_rows, -1)
    back_arrived = [swap(back_blocks[k].astype(BF16), "col", k) for k in range(1, grid_cols)]

    first_pre = dot_parts(first_mean, first_weight)
    projected = dot_parts(first_pre * jax.nn.sigmoid(first_pre), second_weight).astype(BF16)
    output = plane_sum(chip_blocks(gather_col(projected))).astype(BF16)

    scale = 1.0 / math.sqrt(node_rows * grid_rows * grid_cols)
    mine, theirs = local_grads(
        first_mean, first_pre, back_part, back_arrived, second_weight, scale
    )
    mine = (mine + swap(theirs, "row", 1).astype(F32)).astype(BF16)
    mine = tree_sum([mine] + [swap(mine, "row", 2 * i) for i in range(1, chips)]).astype(BF16)
    mine = tree_sum([mine] + [swap(mine, "col", k) for k in range(1, grid_cols)])
    first_grad, second_grad = join(mine, swap(mine, "row", 1), first_weight.shape[1])
    return (output, first_grad, second_grad)


def solution(mesh):
    return jax.shard_map(
        on_device,
        mesh=mesh,
        in_specs=(
            P(("row", "col"), None),
            P("row", "col", None, None, None),
            P("row", "col", None, None),
            P("row", "col"),
            P(),
            P(),
            P(("row", "col"), None),
        ),
        out_specs=(P(("row", "col"), None), P(), P()),
        check_vma=False,
    )
```

time: 70.7 us -> 65.3 us (0.924)
  waiting for transfers between devices: 14.5 us -> 17.1 us
  local copies, waits for them, and re-layouts: 4.85 us -> 2.94 us
  matrix products: 6.98 us -> 5.13 us
  Pallas kernels: 4.59 us -> 2.86 us
  other arithmetic: 2.52 us -> 0.95 us
    ppermute x29, waiting for transfers between devices: 14.5 us -> 17.1 us  [swap(): return lax.ppermute(value, axis, [(i, i ^ offset) for i in range(size)])]
    unnamed x20 -> x12, local copies, waits for them, and re-layouts: 4.77 us -> 2.88 us
    dot_general x10, matrix products: 6.98 us -> 5.13 us  [dot_parts(): lax.dot_general(one, other, (((left_dim,), (right_dim,)), ((), ())), pref...]
    pallas_call x1 -> x3, Pallas kernels: 4.59 us -> 2.86 us  [the longest x1 1.41 us: assemble(): pl.pallas_call(kernel, out_shape=jax.ShapeDtypeStruct((2, rows // 2, cols...]
    add x1 -> x0, other arithmetic: 0.77 us -> none  [on_device(): offset // 2 * per_node + tile_row % per_node]
    select_n x2 -> x0, other arithmetic: 0.73 us -> none  [the longest x1 0.7 us: on_device(): offset % 2]
    ppermute x29, starting transfers between devices: 35.3 us -> 34.6 us  [swap(): return lax.ppermute(value, axis, [(i, i ^ offset) for i in range(size)])]
  transfers between devices with their start and end apart: 29 -> 29, of which waited for: 8 -> 8; matrix products, arithmetic and copies ran while one was open for 13% -> 8% of each run, Pallas kernels for 7% -> 2%
where the time goes in v2:
time: 65.3 us; the launch traced here: 65.1 us
  starting transfers between devices  34.6 us (53%)
  waiting for transfers between devices  17.1 us (26%)
  matrix products  5.13 us (8%)
  local copies, waits for them, and re-layouts  2.94 us (5%)
  Pallas kernels  2.86 us (4%)
  between operations  1.58 us (2%)
  other arithmetic  0.95 us (1%)
    ppermute x29, starting transfers between devices, swap(): return lax.ppermute(value, axis, [(i, i ^ offset) for i in range(size)])  34.6 us
    ppermute x29, waiting for transfers between devices, swap(): return lax.ppermute(value, axis, [(i, i ^ offset) for i in range(size)])  17.1 us
    dot_general x10, matrix products, dot_parts(): lax.dot_general(one, other, (((left_dim,), (right_dim,)), ((), ())), pref...  5.13 us
    unnamed x12, local copies, waits for them, and re-layouts  2.88 us
    pallas_call x1, Pallas kernels, assemble(): pl.pallas_call(kernel, out_shape=jax.ShapeDtypeStruct((2, rows // 2, cols...  1.41 us
  transfers between devices with their start and end apart: 29, of which 8 were waited for; matrix products, arithmetic and copies ran while one was open for 8% of the time, Pallas kernels for 2%

profile of v2, /device:TPU:0, one launch (start us, length us, event | category | flops | bytes accessed | tf_op | source)
XLA Modules:
  0.0 65.1 jit_solution(4141998539793604439)
XLA Ops:
  0.6 3.0 %collective-permute-start.3 = (bf16[256,128]{1,0:T(8,128)(2,1)}, bf16[256,128]{1,0:T(8,128)(2,1)S(1)}, u32[]{:S(2)}, u32[]{:S(2)}) collective-permute-start(bf16[256,128]{1,0:T(8,128)(2,1)} %param.13), channel_id=1, source_target_pairs={{0,8},{4,12},{8,0},{12,4},{16,24},{20,28},{24,16},{28,20},{1,9},{5... | collective-permute-start | bytes 196616 | tf_op jit(solution)/shard_map/ppermute | solution.py:190
  3.7 1.5 %collective-permute-start.4 = (bf16[256,128]{1,0:T(8,128)(2,1)}, bf16[256,128]{1,0:T(8,128)(2,1)S(1)}, u32[]{:S(2)}, u32[]{:S(2)}) collective-permute-start(bf16[256,128]{1,0:T(8,128)(2,1)} %param.13), channel_id=1, source_target_pairs={{0,16},{4,20},{8,24},{12,28},{16,0},{20,4},{24,8},{28,12},{1,17},{... | collective-permute-start | bytes 196616 | tf_op jit(solution)/shard_map/ppermute | solution.py:190
  5.2 2.0 %collective-permute-start = (bf16[256,256]{1,0:T(8,128)(2,1)}, bf16[256,256]{1,0:T(8,128)(2,1)S(1)}, u32[]{:S(2)}, u32[]{:S(2)}) collective-permute-start(bf16[256,256]{1,0:T(8,128)(2,1)} %param.7), channel_id=1, source_target_pairs={{0,1},{1,0},{2,3},{3,2},{4,5},{5,4},{6,7},{7,6},{8,9},{9,8},{10,11... | collective-permute-start | bytes 393224 | tf_op jit(solution)/shard_map/ppermute | solution.py:190
  7.2 2.6 %collective-permute-start.1 = (bf16[256,256]{1,0:T(8,128)(2,1)}, bf16[256,256]{1,0:T(8,128)(2,1)S(1)}, u32[]{:S(2)}, u32[]{:S(2)}) collective-permute-start(bf16[256,256]{1,0:T(8,128)(2,1)} %param.7), channel_id=1, source_target_pairs={{0,2},{1,3},{2,0},{3,1},{4,6},{5,7},{6,4},{7,5},{8,10},{9,11},{10,... | collective-permute-start | bytes 393224 | tf_op jit(solution)/shard_map/ppermute | solution.py:190
  10.9 2.2 %copy-done.1 = bf16[1,1,128,128,128]{4,3,2,1,0:T(8,128)(2,1)S(1)} copy-done((bf16[1,1,128,128,128]{4,3,2,1,0:T(8,128)(2,1)S(1)}, bf16[1,1,128,128,128]{4,3,2,1,0:T(8,128)(2,1)}, u32[]{:S(2)}) %copy-start.1) | copy-done | bytes 4194328
  13.8 1.4 %assemble.1 = bf16[2,1024,1024]{2,1,0:T(8,128)(2,1)S(1)} custom-call(s32[2,128]{1,0:T(2,128)S(1)} %bitcast.50, s32[1]{0:T(128)} %bitcast.48.refs_1_, bf16[128,128,128]{2,1,0:T(8,128)(2,1)S(1)} %bitcast.49), custom_call_target="tpu_custom_call" | custom-call | bytes 8388608 | tf_op jit(solution)/shard_map/assemble/pallas_call | solution.py:100
  15.2 4.3 %collective-permute-done.1 = bf16[256,256]{1,0:T(8,128)(2,1)S(1)} collective-permute-done((bf16[256,256]{1,0:T(8,128)(2,1)}, bf16[256,256]{1,0:T(8,128)(2,1)S(1)}, u32[]{:S(2)}, u32[]{:S(2)}) %collective-permute-start.1) | collective-permute-done | bytes 131104 | tf_op jit(solution)/shard_map/ppermute | solution.py:190
  20.9 1.4 %collective-permute-done.6 = bf16[1024,256]{1,0:T(8,128)(2,1)S(1)} collective-permute-done((bf16[1024,256]{1,0:T(8,128)(2,1)S(1)}, bf16[1024,256]{1,0:T(8,128)(2,1)S(1)}, u32[]{:S(2)}, u32[]{:S(2)}) %collective-permute-start.6) | collective-permute-done | bytes 524320 | tf_op jit(solution)/shard_map/ppermute | solution.py:190
  23.1 2.5 %collective-permute-start.10 = (bf16[256,256]{1,0:T(8,128)(2,1)S(1)}, bf16[256,256]{1,0:T(8,128)(2,1)S(1)}, u32[]{:S(2)}, u32[]{:S(2)}) collective-permute-start(bf16[256,256]{1,0:T(8,128)(2,1)S(1)} %get-tuple-element.22), channel_id=1, source_target_pairs={{0,24},{4,28},{8,16},{12,20},{16,8},{20,12},{24,0},{28,4},{1,25},{... | collective-permute-start | bytes 393224 | tf_op jit(solution)/shard_map/ppermute | solution.py:190
  28.2 2.0 %collective-permute-start.18 = (bf16[256,128]{1,0:T(8,128)(2,1)S(1)}, bf16[256,128]{1,0:T(8,128)(2,1)S(1)}, u32[]{:S(2)}, u32[]{:S(2)}) collective-permute-start(bf16[256,128]{1,0:T(8,128)(2,1)S(1)} %get-tuple-element.26), channel_id=1, source_target_pairs={{0,1},{1,0},{2,3},{3,2},{4,5},{5,4},{6,7},{7,6},{8,9},{9,8},{10,11... | collective-permute-start | bytes 196616 | tf_op jit(solution)/shard_map/ppermute | solution.py:190
  31.3 1.6 %collective-permute-start.20 = (bf16[256,128]{1,0:T(8,128)(2,1)S(1)}, bf16[256,128]{1,0:T(8,128)(2,1)S(1)}, u32[]{:S(2)}, u32[]{:S(2)}) collective-permute-start(bf16[256,128]{1,0:T(8,128)(2,1)S(1)} %get-tuple-element.24), channel_id=1, source_target_pairs={{0,3},{1,2},{2,1},{3,0},{4,7},{5,6},{6,5},{7,4},{8,11},{9,10},{10,... | collective-permute-start | bytes 196616 | tf_op jit(solution)/shard_map/ppermute | solution.py:190
  33.6 4.1 %collective-permute-done.19.refs_4_ = bf16[256,128]{1,0:T(8,128)(2,1)S(1)} collective-permute-done((bf16[256,128]{1,0:T(8,128)(2,1)S(1)}, bf16[256,128]{1,0:T(8,128)(2,1)S(1)}, u32[]{:S(2)}, u32[]{:S(2)}) %collective-permute-start.19) | collective-permute-done | bytes 65568 | tf_op jit(solution)/shard_map/ppermute | solution.py:190
  38.6 1.3 %collective-permute-start.11 = (bf16[256,128]{1,0:T(8,128)(2,1)S(1)}, bf16[256,128]{1,0:T(8,128)(2,1)S(1)}, u32[]{:S(2)}, u32[]{:S(2)}) collective-permute-start(bf16[256,128]{1,0:T(8,128)(2,1)S(1)} %fusion.10), channel_id=1, source_target_pairs={{0,1},{1,0},{2,3},{3,2},{4,5},{5,4},{6,7},{7,6},{8,9},{9,8},{10,11... | collective-permute-start | bytes 196616 | tf_op jit(solution)/shard_map/ppermute | solution.py:190
  39.9 1.6 %collective-permute-start.12 = (bf16[256,128]{1,0:T(8,128)(2,1)S(1)}, bf16[256,128]{1,0:T(8,128)(2,1)S(1)}, u32[]{:S(2)}, u32[]{:S(2)}) collective-permute-start(bf16[256,128]{1,0:T(8,128)(2,1)S(1)} %fusion.10), channel_id=1, source_target_pairs={{0,2},{1,3},{2,0},{3,1},{4,6},{5,7},{6,4},{7,5},{8,10},{9,11},{10,... | collective-permute-start | bytes 196616 | tf_op jit(solution)/shard_map/ppermute | solution.py:190
  41.5 1.6 %collective-permute-start.13 = (bf16[256,128]{1,0:T(8,128)(2,1)S(1)}, bf16[256,128]{1,0:T(8,128)(2,1)S(1)}, u32[]{:S(2)}, u32[]{:S(2)}) collective-permute-start(bf16[256,128]{1,0:T(8,128)(2,1)S(1)} %fusion.10), channel_id=1, source_target_pairs={{0,3},{1,2},{2,1},{3,0},{4,7},{5,6},{6,5},{7,4},{8,11},{9,10},{10,... | collective-permute-start | bytes 196616 | tf_op jit(solution)/shard_map/ppermute | solution.py:190
  43.1 1.6 %collective-permute-start.22 = (bf16[128,384]{1,0:T(8,128)(2,1)S(1)}, bf16[128,384]{1,0:T(8,128)(2,1)S(1)}, u32[]{:S(2)}, u32[]{:S(2)}) collective-permute-start(bf16[128,384]{1,0:T(8,128)(2,1)S(1)} %add_convert_fusion.1), channel_id=1, source_target_pairs={{0,8},{4,12},{8,0},{12,4},{16,24},{20,28},{24,16},{28,20},{1,9},{5... | collective-permute-start | bytes 294920 | tf_op jit(solution)/shard_map/ppermute | solution.py:190
  44.7 1.5 %collective-permute-start.23 = (bf16[128,384]{1,0:T(8,128)(2,1)S(1)}, bf16[128,384]{1,0:T(8,128)(2,1)S(1)}, u32[]{:S(2)}, u32[]{:S(2)}) collective-permute-start(bf16[128,384]{1,0:T(8,128)(2,1)S(1)} %add_convert_fusion.1), channel_id=1, source_target_pairs={{0,16},{4,20},{8,24},{12,28},{16,0},{20,4},{24,8},{28,12},{1,17},{... | collective-permute-start | bytes 294920 | tf_op jit(solution)/shard_map/ppermute | solution.py:190
  46.7 1.8 %collective-permute-done.12 = bf16[256,128]{1,0:T(8,128)(2,1)S(1)} collective-permute-done((bf16[256,128]{1,0:T(8,128)(2,1)S(1)}, bf16[256,128]{1,0:T(8,128)(2,1)S(1)}, u32[]{:S(2)}, u32[]{:S(2)}) %collective-permute-start.12) | collective-permute-done | bytes 65568 | tf_op jit(solution)/shard_map/ppermute | solution.py:190
  50.3 1.4 %collective-permute-done.24 = bf16[128,384]{1,0:T(8,128)(2,1)S(1)} collective-permute-done((bf16[128,384]{1,0:T(8,128)(2,1)S(1)}, bf16[128,384]{1,0:T(8,128)(2,1)S(1)}, u32[]{:S(2)}, u32[]{:S(2)}) %collective-permute-start.24) | collective-permute-done | bytes 98336 | tf_op jit(solution)/shard_map/ppermute | solution.py:190
  52.2 2.5 %collective-permute-start.26 = (bf16[128,384]{1,0:T(8,128)(2,1)S(1)}, bf16[128,384]{1,0:T(8,128)(2,1)S(1)}, u32[]{:S(2)}, u32[]{:S(2)}) collective-permute-start(bf16[128,384]{1,0:T(8,128)(2,1)S(1)} %add_convert_fusion), channel_id=1, source_target_pairs={{0,2},{1,3},{2,0},{3,1},{4,6},{5,7},{6,4},{7,5},{8,10},{9,11},{10,... | collective-permute-start | bytes 294920 | tf_op jit(solution)/shard_map/ppermute | solution.py:190
  54.6 1.6 %collective-permute-start.27 = (bf16[128,384]{1,0:T(8,128)(2,1)S(1)}, bf16[128,384]{1,0:T(8,128)(2,1)S(1)}, u32[]{:S(2)}, u32[]{:S(2)}) collective-permute-start(bf16[128,384]{1,0:T(8,128)(2,1)S(1)} %add_convert_fusion), channel_id=1, source_target_pairs={{0,3},{1,2},{2,1},{3,0},{4,7},{5,6},{6,5},{7,4},{8,11},{9,10},{10,... | collective-permute-start | bytes 294920 | tf_op jit(solution)/shard_map/ppermute | solution.py:190
  58.5 2.0 %collective-permute-start.17 = (bf16[256,128]{1,0:T(8,128)(2,1)S(1)}, bf16[256,128]{1,0:T(8,128)(2,1)S(1)}, u32[]{:S(2)}, u32[]{:S(2)}) collective-permute-start(bf16[256,128]{1,0:T(8,128)(2,1)S(1)} %get-tuple-element.28), channel_id=1, source_target_pairs={{0,24},{4,28},{8,16},{12,20},{16,8},{20,12},{24,0},{28,4},{1,25},{... | collective-permute-start | bytes 196616 | tf_op jit(solution)/shard_map/ppermute | solution.py:190
  60.5 1.3 %collective-permute-done.26 = bf16[128,384]{1,0:T(8,128)(2,1)S(1)} collective-permute-done((bf16[128,384]{1,0:T(8,128)(2,1)S(1)}, bf16[128,384]{1,0:T(8,128)(2,1)S(1)}, u32[]{:S(2)}, u32[]{:S(2)}) %collective-permute-start.26) | collective-permute-done | bytes 98336 | tf_op jit(solution)/shard_map/ppermute | solution.py:190
  62.0 1.7 %collective-permute-done.17 = bf16[256,128]{1,0:T(8,128)(2,1)S(1)} collective-permute-done((bf16[256,128]{1,0:T(8,128)(2,1)S(1)}, bf16[256,128]{1,0:T(8,128)(2,1)S(1)}, u32[]{:S(2)}, u32[]{:S(2)}) %collective-permute-start.17) | collective-permute-done | bytes 65568 | tf_op jit(solution)/shard_map/ppermute | solution.py:190
  (70 shorter events, 15.2 us)
Async XLA Ops:
  0.6 9.2 %collective-permute-start.3 = (bf16[256,128]{1,0:T(8,128)(2,1)}, bf16[256,128]{1,0:T(8,128)(2,1)S(1)}, u32[]{:S(2)}, u32[]{:S(2)}) collective-permute-start(bf16[256,128]{1,0:T(8,128)(2,1)} %param.13), channel_id=1, source_target_pairs={{0,8},{4,12},{8,0},{12,4},{16,24},{20,28},{24,16},{28,20},{1,9},{5... | collective-permute-start | bytes 196616 | tf_op jit(solution)/shard_map/ppermute | solution.py:190
  3.7 11.5 %collective-permute-start.4 = (bf16[256,128]{1,0:T(8,128)(2,1)}, bf16[256,128]{1,0:T(8,128)(2,1)S(1)}, u32[]{:S(2)}, u32[]{:S(2)}) collective-permute-start(bf16[256,128]{1,0:T(8,128)(2,1)} %param.13), channel_id=1, source_target_pairs={{0,16},{4,20},{8,24},{12,28},{16,0},{20,4},{24,8},{28,12},{1,17},{... | collective-permute-start | bytes 196616 | tf_op jit(solution)/shard_map/ppermute | solution.py:190
  5.2 10.0 %collective-permute-start.5 = (bf16[256,128]{1,0:T(8,128)(2,1)}, bf16[256,128]{1,0:T(8,128)(2,1)S(1)}, u32[]{:S(2)}, u32[]{:S(2)}) collective-permute-start(bf16[256,128]{1,0:T(8,128)(2,1)} %param.13), channel_id=1, source_target_pairs={{0,24},{4,28},{8,16},{12,20},{16,8},{20,12},{24,0},{28,4},{1,25},{... | collective-permute-start | bytes 196616 | tf_op jit(solution)/shard_map/ppermute | solution.py:190
  5.2 10.0 %collective-permute-start = (bf16[256,256]{1,0:T(8,128)(2,1)}, bf16[256,256]{1,0:T(8,128)(2,1)S(1)}, u32[]{:S(2)}, u32[]{:S(2)}) collective-permute-start(bf16[256,256]{1,0:T(8,128)(2,1)} %param.7), channel_id=1, source_target_pairs={{0,1},{1,0},{2,3},{3,2},{4,5},{5,4},{6,7},{7,6},{8,9},{9,8},{10,11... | collective-permute-start | bytes 393224 | tf_op jit(solution)/shard_map/ppermute | solution.py:190
  7.2 12.3 %collective-permute-start.1 = (bf16[256,256]{1,0:T(8,128)(2,1)}, bf16[256,256]{1,0:T(8,128)(2,1)S(1)}, u32[]{:S(2)}, u32[]{:S(2)}) collective-permute-start(bf16[256,256]{1,0:T(8,128)(2,1)} %param.7), channel_id=1, source_target_pairs={{0,2},{1,3},{2,0},{3,1},{4,6},{5,7},{6,4},{7,5},{8,10},{9,11},{10,... | collective-permute-start | bytes 393224 | tf_op jit(solution)/shard_map/ppermute | solution.py:190
  9.8 9.7 %collective-permute-start.2 = (bf16[256,256]{1,0:T(8,128)(2,1)}, bf16[256,256]{1,0:T(8,128)(2,1)S(1)}, u32[]{:S(2)}, u32[]{:S(2)}) collective-permute-start(bf16[256,256]{1,0:T(8,128)(2,1)} %param.7), channel_id=1, source_target_pairs={{0,3},{1,2},{2,1},{3,0},{4,7},{5,6},{6,5},{7,4},{8,11},{9,10},{10,... | collective-permute-start | bytes 393224 | tf_op jit(solution)/shard_map/ppermute | solution.py:190
  23.1 8.2 %collective-permute-start.10 = (bf16[256,256]{1,0:T(8,128)(2,1)S(1)}, bf16[256,256]{1,0:T(8,128)(2,1)S(1)}, u32[]{:S(2)}, u32[]{:S(2)}) collective-permute-start(bf16[256,256]{1,0:T(8,128)(2,1)S(1)} %get-tuple-element.22), channel_id=1, source_target_pairs={{0,24},{4,28},{8,16},{12,20},{16,8},{20,12},{24,0},{28,4},{1,25},{... | collective-permute-start | bytes 393224 | tf_op jit(solution)/shard_map/ppermute | solution.py:190
  25.6 7.3 %collective-permute-start.8 = (bf16[256,256]{1,0:T(8,128)(2,1)S(1)}, bf16[256,256]{1,0:T(8,128)(2,1)S(1)}, u32[]{:S(2)}, u32[]{:S(2)}) collective-permute-start(bf16[256,256]{1,0:T(8,128)(2,1)S(1)} %get-tuple-element.21), channel_id=1, source_target_pairs={{0,8},{4,12},{8,0},{12,4},{16,24},{20,28},{24,16},{28,20},{1,9},{5... | collective-permute-start | bytes 393224 | tf_op jit(solution)/shard_map/ppermute | solution.py:190
  26.2 6.7 %collective-permute-start.9 = (bf16[256,256]{1,0:T(8,128)(2,1)S(1)}, bf16[256,256]{1,0:T(8,128)(2,1)S(1)}, u32[]{:S(2)}, u32[]{:S(2)}) collective-permute-start(bf16[256,256]{1,0:T(8,128)(2,1)S(1)} %get-tuple-element.23), channel_id=1, source_target_pairs={{0,16},{4,20},{8,24},{12,28},{16,0},{20,4},{24,8},{28,12},{1,17},{... | collective-permute-start | bytes 393224 | tf_op jit(solution)/shard_map/ppermute | solution.py:190
  28.2 5.4 %collective-permute-start.18 = (bf16[256,128]{1,0:T(8,128)(2,1)S(1)}, bf16[256,128]{1,0:T(8,128)(2,1)S(1)}, u32[]{:S(2)}, u32[]{:S(2)}) collective-permute-start(bf16[256,128]{1,0:T(8,128)(2,1)S(1)} %get-tuple-element.26), channel_id=1, source_target_pairs={{0,1},{1,0},{2,3},{3,2},{4,5},{5,4},{6,7},{7,6},{8,9},{9,8},{10,11... | collective-permute-start | bytes 196616 | tf_op jit(solution)/shard_map/ppermute | solution.py:190
  30.2 7.4 %collective-permute-start.19 = (bf16[256,128]{1,0:T(8,128)(2,1)S(1)}, bf16[256,128]{1,0:T(8,128)(2,1)S(1)}, u32[]{:S(2)}, u32[]{:S(2)}) collective-permute-start(bf16[256,128]{1,0:T(8,128)(2,1)S(1)} %get-tuple-element.25), channel_id=1, source_target_pairs={{0,2},{1,3},{2,0},{3,1},{4,6},{5,7},{6,4},{7,5},{8,10},{9,11},{10,... | collective-permute-start | bytes 196616 | tf_op jit(solution)/shard_map/ppermute | solution.py:190
  31.3 6.3 %collective-permute-start.20 = (bf16[256,128]{1,0:T(8,128)(2,1)S(1)}, bf16[256,128]{1,0:T(8,128)(2,1)S(1)}, u32[]{:S(2)}, u32[]{:S(2)}) collective-permute-start(bf16[256,128]{1,0:T(8,128)(2,1)S(1)} %get-tuple-element.24), channel_id=1, source_target_pairs={{0,3},{1,2},{2,1},{3,0},{4,7},{5,6},{6,5},{7,4},{8,11},{9,10},{10,... | collective-permute-start | bytes 196616 | tf_op jit(solution)/shard_map/ppermute | solution.py:190
  38.6 7.6 %collective-permute-start.11 = (bf16[256,128]{1,0:T(8,128)(2,1)S(1)}, bf16[256,128]{1,0:T(8,128)(2,1)S(1)}, u32[]{:S(2)}, u32[]{:S(2)}) collective-permute-start(bf16[256,128]{1,0:T(8,128)(2,1)S(1)} %fusion.10), channel_id=1, source_target_pairs={{0,1},{1,0},{2,3},{3,2},{4,5},{5,4},{6,7},{7,6},{8,9},{9,8},{10,11... | collective-permute-start | bytes 196616 | tf_op jit(solution)/shard_map/ppermute | solution.py:190
  39.9 8.5 %collective-permute-start.12 = (bf16[256,128]{1,0:T(8,128)(2,1)S(1)}, bf16[256,128]{1,0:T(8,128)(2,1)S(1)}, u32[]{:S(2)}, u32[]{:S(2)}) collective-permute-start(bf16[256,128]{1,0:T(8,128)(2,1)S(1)} %fusion.10), channel_id=1, source_target_pairs={{0,2},{1,3},{2,0},{3,1},{4,6},{5,7},{6,4},{7,5},{8,10},{9,11},{10,... | collective-permute-start | bytes 196616 | tf_op jit(solution)/shard_map/ppermute | solution.py:190
  41.5 6.9 %collective-permute-start.13 = (bf16[256,128]{1,0:T(8,128)(2,1)S(1)}, bf16[256,128]{1,0:T(8,128)(2,1)S(1)}, u32[]{:S(2)}, u32[]{:S(2)}) collective-permute-start(bf16[256,128]{1,0:T(8,128)(2,1)S(1)} %fusion.10), channel_id=1, source_target_pairs={{0,3},{1,2},{2,1},{3,0},{4,7},{5,6},{6,5},{7,4},{8,11},{9,10},{10,... | collective-permute-start | bytes 196616 | tf_op jit(solution)/shard_map/ppermute | solution.py:190
  43.1 6.1 %collective-permute-start.22 = (bf16[128,384]{1,0:T(8,128)(2,1)S(1)}, bf16[128,384]{1,0:T(8,128)(2,1)S(1)}, u32[]{:S(2)}, u32[]{:S(2)}) collective-permute-start(bf16[128,384]{1,0:T(8,128)(2,1)S(1)} %add_convert_fusion.1), channel_id=1, source_target_pairs={{0,8},{4,12},{8,0},{12,4},{16,24},{20,28},{24,16},{28,20},{1,9},{5... | collective-permute-start | bytes 294920 | tf_op jit(solution)/shard_map/ppermute | solution.py:190
  44.7 5.7 %collective-permute-start.23 = (bf16[128,384]{1,0:T(8,128)(2,1)S(1)}, bf16[128,384]{1,0:T(8,128)(2,1)S(1)}, u32[]{:S(2)}, u32[]{:S(2)}) collective-permute-start(bf16[128,384]{1,0:T(8,128)(2,1)S(1)} %add_convert_fusion.1), channel_id=1, source_target_pairs={{0,16},{4,20},{8,24},{12,28},{16,0},{20,4},{24,8},{28,12},{1,17},{... | collective-permute-start | bytes 294920 | tf_op jit(solution)/shard_map/ppermute | solution.py:190
  46.2 5.5 %collective-permute-start.24 = (bf16[128,384]{1,0:T(8,128)(2,1)S(1)}, bf16[128,384]{1,0:T(8,128)(2,1)S(1)}, u32[]{:S(2)}, u32[]{:S(2)}) collective-permute-start(bf16[128,384]{1,0:T(8,128)(2,1)S(1)} %add_convert_fusion.1), channel_id=1, source_target_pairs={{0,24},{4,28},{8,16},{12,20},{16,8},{20,12},{24,0},{28,4},{1,25},{... | collective-permute-start | bytes 294920 | tf_op jit(solution)/shard_map/ppermute | solution.py:190
  49.1 7.1 %collective-permute-start.14 = (bf16[1024,128]{1,0:T(8,128)(2,1)S(1)}, bf16[1024,128]{1,0:T(8,128)(2,1)S(1)}, u32[]{:S(2)}, u32[]{:S(2)}) collective-permute-start(bf16[1024,128]{1,0:T(8,128)(2,1)S(1)} %fusion.9), channel_id=1, source_target_pairs={{0,4},{4,0},{8,12},{12,8},{16,20},{20,16},{24,28},{28,24},{1,5},{5... | collective-permute-start | bytes 786440 | tf_op jit(solution)/shard_map/ppermute | solution.py:190
  51.8 6.8 %collective-permute-start.25 = (bf16[128,384]{1,0:T(8,128)(2,1)S(1)}, bf16[128,384]{1,0:T(8,128)(2,1)S(1)}, u32[]{:S(2)}, u32[]{:S(2)}) collective-permute-start(bf16[128,384]{1,0:T(8,128)(2,1)S(1)} %add_convert_fusion), channel_id=1, source_target_pairs={{0,1},{1,0},{2,3},{3,2},{4,5},{5,4},{6,7},{7,6},{8,9},{9,8},{10,11... | collective-permute-start | bytes 294920 | tf_op jit(solution)/shard_map/ppermute | solution.py:190
  52.2 9.7 %collective-permute-start.26 = (bf16[128,384]{1,0:T(8,128)(2,1)S(1)}, bf16[128,384]{1,0:T(8,128)(2,1)S(1)}, u32[]{:S(2)}, u32[]{:S(2)}) collective-permute-start(bf16[128,384]{1,0:T(8,128)(2,1)S(1)} %add_convert_fusion), channel_id=1, source_target_pairs={{0,2},{1,3},{2,0},{3,1},{4,6},{5,7},{6,4},{7,5},{8,10},{9,11},{10,... | collective-permute-start | bytes 294920 | tf_op jit(solution)/shard_map/ppermute | solution.py:190
  54.6 7.2 %collective-permute-start.27 = (bf16[128,384]{1,0:T(8,128)(2,1)S(1)}, bf16[128,384]{1,0:T(8,128)(2,1)S(1)}, u32[]{:S(2)}, u32[]{:S(2)}) collective-permute-start(bf16[128,384]{1,0:T(8,128)(2,1)S(1)} %add_convert_fusion), channel_id=1, source_target_pairs={{0,3},{1,2},{2,1},{3,0},{4,7},{5,6},{6,5},{7,4},{8,11},{9,10},{10,... | collective-permute-start | bytes 294920 | tf_op jit(solution)/shard_map/ppermute | solution.py:190
  57.0 5.0 %collective-permute-start.15 = (bf16[256,128]{1,0:T(8,128)(2,1)S(1)}, bf16[256,128]{1,0:T(8,128)(2,1)S(1)}, u32[]{:S(2)}, u32[]{:S(2)}) collective-permute-start(bf16[256,128]{1,0:T(8,128)(2,1)S(1)} %get-tuple-element.27), channel_id=1, source_target_pairs={{0,8},{4,12},{8,0},{12,4},{16,24},{20,28},{24,16},{28,20},{1,9},{5... | collective-permute-start | bytes 196616 | tf_op jit(solution)/shard_map/ppermute | solution.py:190
  58.5 5.2 %collective-permute-start.17 = (bf16[256,128]{1,0:T(8,128)(2,1)S(1)}, bf16[256,128]{1,0:T(8,128)(2,1)S(1)}, u32[]{:S(2)}, u32[]{:S(2)}) collective-permute-start(bf16[256,128]{1,0:T(8,128)(2,1)S(1)} %get-tuple-element.28), channel_id=1, source_target_pairs={{0,24},{4,28},{8,16},{12,20},{16,8},{20,12},{24,0},{28,4},{1,25},{... | collective-permute-start | bytes 196616 | tf_op jit(solution)/shard_map/ppermute | solution.py:190
  (11 other events, 65.7 us)

commit v3 on v2

--- a/solution.py
+++ b/solution.py
@@ -44,6 +44,7 @@
     live = count_ref[0]
     strip = math.gcd(rows, 256)
     shift = per_node.bit_length() - 1
+    far_bit = lax.axis_size("col") // 2
 
     @pl.when(live * edge * edge < halves * rows * cols)
     def _():
@@ -59,7 +60,7 @@
         row, col = coords_ref[0, slot], coords_ref[1, slot]
         offset = (row >> shift) ^ me_row
         row_place = ((offset >> 1) << shift) + (row & (per_node - 1))
-        col_place = (((col >> shift) ^ me_col) << shift) + (col & (per_node - 1))
+        col_place = (((col >> shift) ^ me_col ^ far_bit) << shift) + (col & (per_node - 1))
         pltpu.make_async_copy(
             tiles_ref.at[slot],
             dense_ref.at[
@@ -119,7 +120,8 @@
     mean_ref, pre_ref, back_ref = refs[:3]
     arrived_refs = refs[3 : 2 + grid_cols]
     weight_ref, mine_ref, theirs_ref = refs[2 + grid_cols :]
-    back_sum = tree_sum([back_ref[: mean_ref.shape[0], :]] + [ref[...] for ref in arrived_refs])
+    own = pl.ds(grid_cols // 2 * mean_ref.shape[0], mean_ref.shape[0])
+    back_sum = tree_sum([back_ref[own, :]] + [ref[...] for ref in arrived_refs])
     hidden_grad = dot_parts(back_sum, weight_ref[...], 1, 1)
     first_pre = pre_ref[...]
     sigma = jax.nn.sigmoid(first_pre)
@@ -190,6 +192,15 @@
     return lax.ppermute(value, axis, [(i, i ^ offset) for i in range(size)])
 
 
+def exchange(values, axis, stride, near=False):
+    half = 0 if near else len(values) // 2
+    arrived = [
+        values[0] if k == 0 else swap(values[k], axis, k * stride)
+        for k in (i ^ half for i in range(len(values)))
+    ]
+    return arrived
+
+
 def on_device(
     node_features, tile_values, tile_coords, tile_counts, first_weight, second_weight, out_grad
 ):
@@ -202,11 +213,10 @@
     per_node = node_rows // edge
 
     def gather_col(value):
-        return jnp.concatenate(
-            [value] + [swap(value, "col", k) for k in range(1, grid_cols)], axis=0
-        )
-
-    gathered_x = gather_col(node_features)
+        return exchange([value] * grid_cols, "col", 1)
+
+    parts_x = gather_col(node_features)
+    gathered_x = jnp.concatenate(parts_x, axis=0)
     dense = assemble(
         tile_values.reshape(slots, edge, edge),
         tile_coords.reshape(slots, 2).T,
@@ -216,21 +226,20 @@
         per_node,
     )
     dense_own, dense_other = dense[0], dense[1]
-    grad_own = jnp.concatenate(
-        [out_grad] + [swap(out_grad, "row", 2 * i) for i in range(1, chips)], axis=0
-    )
+    grad_own, offset = out_grad, 2
+    while offset < grid_rows:
+        grad_own = jnp.concatenate([grad_own, swap(grad_own, "row", offset)], axis=0)
+        offset *= 2
 
     def chip_blocks(source):
         other = dot_parts(dense_other, source).astype(BF16)
         arrived = swap(other, "row", 1)
-        chip_sum = dot_parts(dense_own, source) + arrived.astype(F32)
-        return chip_sum.reshape(chips, node_rows, -1)
-
-    def plane_sum(blocks):
-        return tree_sum(
-            [blocks[0]]
-            + [swap(blocks[i].astype(BF16), "row", 2 * i) for i in range(1, chips)]
-        )
+        own, arrived = lax.optimization_barrier((dot_parts(dense_own, source), arrived))
+        return (own + arrived.astype(F32)).reshape(chips, node_rows, -1)
+
+    def plane_sum(blocks, near):
+        sent = [blocks[0]] + [blocks[i].astype(BF16) for i in range(1, chips)]
+        return tree_sum(exchange(sent, "row", 2, near))
 
     gathered_x, grad_own = lax.optimization_barrier((gathered_x, grad_own))
     grad_other = swap(grad_own, "row", 1)
@@ -239,22 +248,30 @@
     first_blocks, grad_own, grad_other = lax.optimization_barrier(
         (first_blocks, grad_own, grad_other)
     )
-    first_mean = plane_sum(first_blocks)
+    first_mean = plane_sum(first_blocks, False)
     back_part = dot_parts(dense_own, grad_own, 0) + dot_parts(dense_other, grad_other, 0)
     back_blocks = back_part.reshape(grid_cols, node_rows, -1)
-    back_arrived = [swap(back_blocks[k].astype(BF16), "col", k) for k in range(1, grid_cols)]
+    back_sent = [back_blocks[i ^ (grid_cols // 2)] for i in range(grid_cols)]
+    back_sent = [back_sent[0]] + [block.astype(BF16) for block in back_sent[1:]]
+    back_arrived = exchange(back_sent, "col", 1, False)
+    back_arrived.pop(grid_cols // 2)
 
     first_pre = dot_parts(first_mean, first_weight)
     projected = dot_parts(first_pre * jax.nn.sigmoid(first_pre), second_weight).astype(BF16)
-    output = plane_sum(chip_blocks(gather_col(projected))).astype(BF16)
+    projected, first_pre = lax.optimization_barrier((projected, first_pre))
+    parts_h = exchange([projected] * grid_cols, "col", 1, True)
 
     scale = 1.0 / math.sqrt(node_rows * grid_rows * grid_cols)
     mine, theirs = local_grads(
         first_mean, first_pre, back_part, back_arrived, second_weight, scale
     )
     mine = (mine + swap(theirs, "row", 1).astype(F32)).astype(BF16)
-    mine = tree_sum([mine] + [swap(mine, "row", 2 * i) for i in range(1, chips)]).astype(BF16)
-    mine = tree_sum([mine] + [swap(mine, "col", k) for k in range(1, grid_cols)])
+    _, *parts_h = lax.optimization_barrier((mine, *parts_h))
+    parts_h = lax.optimization_barrier(parts_h)
+    parts_h = [parts_h[i ^ (grid_cols // 2)] for i in range(grid_cols)]
+    output = plane_sum(chip_blocks(jnp.concatenate(parts_h, axis=0)), False).astype(BF16)
+    mine = tree_sum(exchange([mine] * chips, "row", 2, False)).astype(BF16)
+    mine = tree_sum(exchange([mine] * grid_cols, "col", 1, True))
     first_grad, second_grad = join(mine, swap(mine, "row", 1), first_weight.shape[1])
     return (output, first_grad, second_grad)
 

time: 65.3 us -> 61.6 us (0.943)
  waiting for transfers between devices: 17.1 us -> 12.4 us
  other arithmetic: 0.95 us -> 1.98 us
    ppermute x29 -> x28, waiting for transfers between devices: 17.1 us -> 12.4 us  [swap(): return lax.ppermute(value, axis, [(i, i ^ offset) for i in range(size)])]
    concatenate x2 -> x3, other arithmetic: 0.05 us -> 0.9 us  [the longest x2 0.87 us: on_device(): jnp.concatenate([grad_own, swap(grad_own, 'row', offset)], axis=0)]
    ppermute x29 -> x28, starting transfers between devices: 34.6 us -> 34.2 us  [swap(): return lax.ppermute(value, axis, [(i, i ^ offset) for i in range(size)])]
    unnamed x12 -> x15, local copies, waits for them, and re-layouts: 2.88 us -> 2.91 us
  transfers between devices with their start and end apart: 29 -> 28, of which waited for: 8 -> 11; matrix products, arithmetic and copies ran while one was open for 8% -> 10% of each run, Pallas kernels for 2% -> 3%
where the time goes in v3:
time: 61.6 us; the launch traced here: 61.3 us
  starting transfers between devices  34.2 us (56%)
  waiting for transfers between devices  12.4 us (20%)
  matrix products  5.1 us (8%)
  Pallas kernels  3.16 us (5%)
  local copies, waits for them, and re-layouts  2.99 us (5%)
  other arithmetic  1.98 us (3%)
  between operations  1.56 us (3%)
    ppermute x28, starting transfers between devices, swap(): return lax.ppermute(value, axis, [(i, i ^ offset) for i in range(size)])  34.2 us
    ppermute x28, waiting for transfers between devices, swap(): return lax.ppermute(value, axis, [(i, i ^ offset) for i in range(size)])  12.4 us
    dot_general x10, matrix products, dot_parts(): lax.dot_general(one, other, (((left_dim,), (right_dim,)), ((), ())), pref...  5.1 us
    unnamed x15, local copies, waits for them, and re-layouts  2.91 us
    pallas_call x1, Pallas kernels, assemble(): pl.pallas_call(kernel, out_shape=jax.ShapeDtypeStruct((2, rows // 2, cols...  1.71 us
  transfers between devices with their start and end apart: 28, of which 11 were waited for; matrix products, arithmetic and copies ran while one was open for 10% of the time, Pallas kernels for 3%

profile of v3, /device:TPU:0, one launch (start us, length us, event | category | flops | bytes accessed | tf_op | source)
XLA Modules:
  0.0 61.3 jit_solution(13962229357708999036)
XLA Ops:
  0.6 3.0 %collective-permute-start.3 = (bf16[256,128]{1,0:T(8,128)(2,1)}, bf16[256,128]{1,0:T(8,128)(2,1)S(1)}, u32[]{:S(2)}, u32[]{:S(2)}) collective-permute-start(bf16[256,128]{1,0:T(8,128)(2,1)} %param.13), channel_id=1, source_target_pairs={{0,8},{4,12},{8,0},{12,4},{16,24},{20,28},{24,16},{28,20},{1,9},{5... | collective-permute-start | bytes 196616 | tf_op jit(solution)/shard_map/ppermute | solution.py:192
  3.6 2.6 %collective-permute-start = (bf16[256,256]{1,0:T(8,128)(2,1)}, bf16[256,256]{1,0:T(8,128)(2,1)S(1)}, u32[]{:S(2)}, u32[]{:S(2)}) collective-permute-start(bf16[256,256]{1,0:T(8,128)(2,1)} %param.7), channel_id=1, source_target_pairs={{0,2},{1,3},{2,0},{3,1},{4,6},{5,7},{6,4},{7,5},{8,10},{9,11},{10,... | collective-permute-start | bytes 393224 | tf_op jit(solution)/shard_map/ppermute | solution.py:192
  6.2 1.3 %collective-permute-start.1 = (bf16[256,256]{1,0:T(8,128)(2,1)}, bf16[256,256]{1,0:T(8,128)(2,1)S(1)}, u32[]{:S(2)}, u32[]{:S(2)}) collective-permute-start(bf16[256,256]{1,0:T(8,128)(2,1)} %param.7), channel_id=1, source_target_pairs={{0,3},{1,2},{2,1},{3,0},{4,7},{5,6},{6,5},{7,4},{8,11},{9,10},{10,... | collective-permute-start | bytes 393224 | tf_op jit(solution)/shard_map/ppermute | solution.py:192
  7.8 0.8 %pad_maximum_fusion.2 = bf16[512,128]{1,0:T(8,128)(2,1)S(1)} fusion(bf16[256,128]{1,0:T(8,128)(2,1)S(1)} %collective-permute-done.3, bf16[256,128]{1,0:T(8,128)(2,1)} %param.13), kind=kLoop, calls=%fused_computation.38 | loop fusion | flops 262144 | bytes 262144 | tf_op jit(solution)/shard_map/concatenate | solution.py:231
  8.7 1.6 %collective-permute-start.4 = (bf16[512,128]{1,0:T(8,128)(2,1)S(1)}, bf16[512,128]{1,0:T(8,128)(2,1)S(1)}, u32[]{:S(2)}, u32[]{:S(2)}) collective-permute-start(bf16[512,128]{1,0:T(8,128)(2,1)S(1)} %pad_maximum_fusion.2), channel_id=1, source_target_pairs={{0,16},{4,20},{8,24},{12,28},{16,0},{20,4},{24,8},{28,12},{1,17},{... | collective-permute-start | bytes 393224 | tf_op jit(solution)/shard_map/ppermute | solution.py:192
  10.9 2.2 %copy-done.1 = bf16[1,1,128,128,128]{4,3,2,1,0:T(8,128)(2,1)S(1)} copy-done((bf16[1,1,128,128,128]{4,3,2,1,0:T(8,128)(2,1)S(1)}, bf16[1,1,128,128,128]{4,3,2,1,0:T(8,128)(2,1)}, u32[]{:S(2)}) %copy-start.1) | copy-done | bytes 4194328
  13.8 1.7 %assemble.1 = bf16[2,1024,1024]{2,1,0:T(8,128)(2,1)S(1)} custom-call(s32[2,128]{1,0:T(2,128)S(1)} %bitcast.46, s32[1]{0:T(128)} %bitcast.44.refs_1_, bf16[128,128,128]{2,1,0:T(8,128)(2,1)S(1)} %bitcast.45), custom_call_target="tpu_custom_call" | custom-call | bytes 8388608 | tf_op jit(solution)/shard_map/assemble/pallas_call | solution.py:101
  15.5 1.0 %collective-permute-done = bf16[256,256]{1,0:T(8,128)(2,1)S(1)} collective-permute-done((bf16[256,256]{1,0:T(8,128)(2,1)}, bf16[256,256]{1,0:T(8,128)(2,1)S(1)}, u32[]{:S(2)}, u32[]{:S(2)}) %collective-permute-start) | collective-permute-done | bytes 131104 | tf_op jit(solution)/shard_map/ppermute | solution.py:192
  19.9 1.6 %collective-permute-start.7 = (bf16[256,256]{1,0:T(8,128)(2,1)S(1)}, bf16[256,256]{1,0:T(8,128)(2,1)S(1)}, u32[]{:S(2)}, u32[]{:S(2)}) collective-permute-start(bf16[256,256]{1,0:T(8,128)(2,1)S(1)} %get-tuple-element.51), channel_id=1, source_target_pairs={{0,16},{4,20},{8,24},{12,28},{16,0},{20,4},{24,8},{28,12},{1,17},{... | collective-permute-start | bytes 393224 | tf_op jit(solution)/shard_map/ppermute | solution.py:192
  22.0 1.5 %collective-permute-start.9 = (bf16[256,256]{1,0:T(8,128)(2,1)S(1)}, bf16[256,256]{1,0:T(8,128)(2,1)S(1)}, u32[]{:S(2)}, u32[]{:S(2)}) collective-permute-start(bf16[256,256]{1,0:T(8,128)(2,1)S(1)} %get-tuple-element.52), channel_id=1, source_target_pairs={{0,8},{4,12},{8,0},{12,4},{16,24},{20,28},{24,16},{28,20},{1,9},{5... | collective-permute-start | bytes 393224 | tf_op jit(solution)/shard_map/ppermute | solution.py:192
  25.0 4.1 %collective-permute-start.10 = (bf16[256,128]{1,0:T(8,128)(2,1)S(1)}, bf16[256,128]{1,0:T(8,128)(2,1)S(1)}, u32[]{:S(2)}, u32[]{:S(2)}) collective-permute-start(bf16[256,128]{1,0:T(8,128)(2,1)S(1)} %get-tuple-element.59), channel_id=1, source_target_pairs={{0,2},{1,3},{2,0},{3,1},{4,6},{5,7},{6,4},{7,5},{8,10},{9,11},{10,... | collective-permute-start | bytes 196616 | tf_op jit(solution)/shard_map/ppermute | solution.py:192
  31.0 2.5 %collective-permute-done.10.refs_3_ = bf16[256,128]{1,0:T(8,128)(2,1)S(1)} collective-permute-done((bf16[256,128]{1,0:T(8,128)(2,1)S(1)}, bf16[256,128]{1,0:T(8,128)(2,1)S(1)}, u32[]{:S(2)}, u32[]{:S(2)}) %collective-permute-start.10) | collective-permute-done | bytes 65568 | tf_op jit(solution)/shard_map/ppermute | solution.py:192
  33.5 1.7 %collective-permute-done.11.refs_4_ = bf16[256,128]{1,0:T(8,128)(2,1)S(1)} collective-permute-done((bf16[256,128]{1,0:T(8,128)(2,1)S(1)}, bf16[256,128]{1,0:T(8,128)(2,1)S(1)}, u32[]{:S(2)}, u32[]{:S(2)}) %collective-permute-start.11) | collective-permute-done | bytes 65568 | tf_op jit(solution)/shard_map/ppermute | solution.py:192
  36.1 2.5 %collective-permute-start.15 = (bf16[256,128]{1,0:T(8,128)(2,1)S(1)}, bf16[256,128]{1,0:T(8,128)(2,1)S(1)}, u32[]{:S(2)}, u32[]{:S(2)}) collective-permute-start(bf16[256,128]{1,0:T(8,128)(2,1)S(1)} %fusion.9), channel_id=1, source_target_pairs={{0,2},{1,3},{2,0},{3,1},{4,6},{5,7},{6,4},{7,5},{8,10},{9,11},{10,... | collective-permute-start | bytes 196616 | tf_op jit(solution)/shard_map/ppermute | solution.py:192
  38.6 1.8 %collective-permute-start.16 = (bf16[256,128]{1,0:T(8,128)(2,1)S(1)}, bf16[256,128]{1,0:T(8,128)(2,1)S(1)}, u32[]{:S(2)}, u32[]{:S(2)}) collective-permute-start(bf16[256,128]{1,0:T(8,128)(2,1)S(1)} %fusion.9), channel_id=1, source_target_pairs={{0,3},{1,2},{2,1},{3,0},{4,7},{5,6},{6,5},{7,4},{8,11},{9,10},{10,... | collective-permute-start | bytes 196616 | tf_op jit(solution)/shard_map/ppermute | solution.py:192
  40.4 1.6 %collective-permute-start.21 = (bf16[128,384]{1,0:T(8,128)(2,1)S(1)}, bf16[128,384]{1,0:T(8,128)(2,1)S(1)}, u32[]{:S(2)}, u32[]{:S(2)}) collective-permute-start(bf16[128,384]{1,0:T(8,128)(2,1)S(1)} %add_convert_fusion.1), channel_id=1, source_target_pairs={{0,16},{4,20},{8,24},{12,28},{16,0},{20,4},{24,8},{28,12},{1,17},{... | collective-permute-start | bytes 294920 | tf_op jit(solution)/shard_map/ppermute | solution.py:192
  42.5 1.5 %collective-permute-start.23 = (bf16[128,384]{1,0:T(8,128)(2,1)S(1)}, bf16[128,384]{1,0:T(8,128)(2,1)S(1)}, u32[]{:S(2)}, u32[]{:S(2)}) collective-permute-start(bf16[128,384]{1,0:T(8,128)(2,1)S(1)} %add_convert_fusion.1), channel_id=1, source_target_pairs={{0,8},{4,12},{8,0},{12,4},{16,24},{20,28},{24,16},{28,20},{1,9},{5... | collective-permute-start | bytes 294920 | tf_op jit(solution)/shard_map/ppermute | solution.py:192
  46.3 1.8 %collective-permute-done.22 = bf16[128,384]{1,0:T(8,128)(2,1)S(1)} collective-permute-done((bf16[128,384]{1,0:T(8,128)(2,1)S(1)}, bf16[128,384]{1,0:T(8,128)(2,1)S(1)}, u32[]{:S(2)}, u32[]{:S(2)}) %collective-permute-start.22) | collective-permute-done | bytes 98336 | tf_op jit(solution)/shard_map/ppermute | solution.py:192
  48.2 2.6 %collective-permute-start.25 = (bf16[128,384]{1,0:T(8,128)(2,1)S(1)}, bf16[128,384]{1,0:T(8,128)(2,1)S(1)}, u32[]{:S(2)}, u32[]{:S(2)}) collective-permute-start(bf16[128,384]{1,0:T(8,128)(2,1)S(1)} %add_convert_fusion), channel_id=1, source_target_pairs={{0,2},{1,3},{2,0},{3,1},{4,6},{5,7},{6,4},{7,5},{8,10},{9,11},{10,... | collective-permute-start | bytes 294920 | tf_op jit(solution)/shard_map/ppermute | solution.py:192
  50.8 1.8 %collective-permute-start.26 = (bf16[128,384]{1,0:T(8,128)(2,1)S(1)}, bf16[128,384]{1,0:T(8,128)(2,1)S(1)}, u32[]{:S(2)}, u32[]{:S(2)}) collective-permute-start(bf16[128,384]{1,0:T(8,128)(2,1)S(1)} %add_convert_fusion), channel_id=1, source_target_pairs={{0,3},{1,2},{2,1},{3,0},{4,7},{5,6},{6,5},{7,4},{8,11},{9,10},{10,... | collective-permute-start | bytes 294920 | tf_op jit(solution)/shard_map/ppermute | solution.py:192
  52.7 1.6 %collective-permute-start.18 = (bf16[256,128]{1,0:T(8,128)(2,1)S(1)}, bf16[256,128]{1,0:T(8,128)(2,1)S(1)}, u32[]{:S(2)}, u32[]{:S(2)}) collective-permute-start(bf16[256,128]{1,0:T(8,128)(2,1)S(1)} %get-tuple-element.54), channel_id=1, source_target_pairs={{0,16},{4,20},{8,24},{12,28},{16,0},{20,4},{24,8},{28,12},{1,17},{... | collective-permute-start | bytes 196616 | tf_op jit(solution)/shard_map/ppermute | solution.py:192
  54.9 1.3 %collective-permute-start.20 = (bf16[256,128]{1,0:T(8,128)(2,1)S(1)}, bf16[256,128]{1,0:T(8,128)(2,1)S(1)}, u32[]{:S(2)}, u32[]{:S(2)}) collective-permute-start(bf16[256,128]{1,0:T(8,128)(2,1)S(1)} %get-tuple-element.55), channel_id=1, source_target_pairs={{0,8},{4,12},{8,0},{12,4},{16,24},{20,28},{24,16},{28,20},{1,9},{5... | collective-permute-start | bytes 196616 | tf_op jit(solution)/shard_map/ppermute | solution.py:192
  56.3 2.7 %collective-permute-done.25 = bf16[128,384]{1,0:T(8,128)(2,1)S(1)} collective-permute-done((bf16[128,384]{1,0:T(8,128)(2,1)S(1)}, bf16[128,384]{1,0:T(8,128)(2,1)S(1)}, u32[]{:S(2)}, u32[]{:S(2)}) %collective-permute-start.25) | collective-permute-done | bytes 98336 | tf_op jit(solution)/shard_map/ppermute | solution.py:192
  60.6 0.8 %join_grads.1 = (f32[256,256]{1,0:T(8,128)}, f32[256,128]{1,0:T(8,128)}) custom-call(f32[128,384]{1,0:T(8,128)S(1)} %add_add_fusion.mine_ref, f32[128,384]{1,0:T(8,128)S(1)} %collective-permute-done.27.theirs_ref), custom_call_target="tpu_custom_call" | custom-call | tf_op jit(solution)/shard_map/join_grads/pallas_call | solution.py:177
  (75 shorter events, 14.1 us)
Async XLA Ops:
  0.6 7.2 %collective-permute-start.3 = (bf16[256,128]{1,0:T(8,128)(2,1)}, bf16[256,128]{1,0:T(8,128)(2,1)S(1)}, u32[]{:S(2)}, u32[]{:S(2)}) collective-permute-start(bf16[256,128]{1,0:T(8,128)(2,1)} %param.13), channel_id=1, source_target_pairs={{0,8},{4,12},{8,0},{12,4},{16,24},{20,28},{24,16},{28,20},{1,9},{5... | collective-permute-start | bytes 196616 | tf_op jit(solution)/shard_map/ppermute | solution.py:192
  3.6 12.9 %collective-permute-start = (bf16[256,256]{1,0:T(8,128)(2,1)}, bf16[256,256]{1,0:T(8,128)(2,1)S(1)}, u32[]{:S(2)}, u32[]{:S(2)}) collective-permute-start(bf16[256,256]{1,0:T(8,128)(2,1)} %param.7), channel_id=1, source_target_pairs={{0,2},{1,3},{2,0},{3,1},{4,6},{5,7},{6,4},{7,5},{8,10},{9,11},{10,... | collective-permute-start | bytes 393224 | tf_op jit(solution)/shard_map/ppermute | solution.py:192
  6.2 10.3 %collective-permute-start.1 = (bf16[256,256]{1,0:T(8,128)(2,1)}, bf16[256,256]{1,0:T(8,128)(2,1)S(1)}, u32[]{:S(2)}, u32[]{:S(2)}) collective-permute-start(bf16[256,256]{1,0:T(8,128)(2,1)} %param.7), channel_id=1, source_target_pairs={{0,3},{1,2},{2,1},{3,0},{4,7},{5,6},{6,5},{7,4},{8,11},{9,10},{10,... | collective-permute-start | bytes 393224 | tf_op jit(solution)/shard_map/ppermute | solution.py:192
  7.6 9.1 %collective-permute-start.2 = (bf16[256,256]{1,0:T(8,128)(2,1)}, bf16[256,256]{1,0:T(8,128)(2,1)S(1)}, u32[]{:S(2)}, u32[]{:S(2)}) collective-permute-start(bf16[256,256]{1,0:T(8,128)(2,1)} %param.7), channel_id=1, source_target_pairs={{0,1},{1,0},{2,3},{3,2},{4,5},{5,4},{6,7},{7,6},{8,9},{9,8},{10,11... | collective-permute-start | bytes 393224 | tf_op jit(solution)/shard_map/ppermute | solution.py:192
  8.7 8.1 %collective-permute-start.4 = (bf16[512,128]{1,0:T(8,128)(2,1)S(1)}, bf16[512,128]{1,0:T(8,128)(2,1)S(1)}, u32[]{:S(2)}, u32[]{:S(2)}) collective-permute-start(bf16[512,128]{1,0:T(8,128)(2,1)S(1)} %pad_maximum_fusion.2), channel_id=1, source_target_pairs={{0,16},{4,20},{8,24},{12,28},{16,0},{20,4},{24,8},{28,12},{1,17},{... | collective-permute-start | bytes 393224 | tf_op jit(solution)/shard_map/ppermute | solution.py:192
  19.9 9.7 %collective-permute-start.7 = (bf16[256,256]{1,0:T(8,128)(2,1)S(1)}, bf16[256,256]{1,0:T(8,128)(2,1)S(1)}, u32[]{:S(2)}, u32[]{:S(2)}) collective-permute-start(bf16[256,256]{1,0:T(8,128)(2,1)S(1)} %get-tuple-element.51), channel_id=1, source_target_pairs={{0,16},{4,20},{8,24},{12,28},{16,0},{20,4},{24,8},{28,12},{1,17},{... | collective-permute-start | bytes 393224 | tf_op jit(solution)/shard_map/ppermute | solution.py:192
  21.5 8.6 %collective-permute-start.8 = (bf16[256,256]{1,0:T(8,128)(2,1)S(1)}, bf16[256,256]{1,0:T(8,128)(2,1)S(1)}, u32[]{:S(2)}, u32[]{:S(2)}) collective-permute-start(bf16[256,256]{1,0:T(8,128)(2,1)S(1)} %get-tuple-element.53), channel_id=1, source_target_pairs={{0,24},{4,28},{8,16},{12,20},{16,8},{20,12},{24,0},{28,4},{1,25},{... | collective-permute-start | bytes 393224 | tf_op jit(solution)/shard_map/ppermute | solution.py:192
  22.0 8.2 %collective-permute-start.9 = (bf16[256,256]{1,0:T(8,128)(2,1)S(1)}, bf16[256,256]{1,0:T(8,128)(2,1)S(1)}, u32[]{:S(2)}, u32[]{:S(2)}) collective-permute-start(bf16[256,256]{1,0:T(8,128)(2,1)S(1)} %get-tuple-element.52), channel_id=1, source_target_pairs={{0,8},{4,12},{8,0},{12,4},{16,24},{20,28},{24,16},{28,20},{1,9},{5... | collective-permute-start | bytes 393224 | tf_op jit(solution)/shard_map/ppermute | solution.py:192
  25.0 8.5 %collective-permute-start.10 = (bf16[256,128]{1,0:T(8,128)(2,1)S(1)}, bf16[256,128]{1,0:T(8,128)(2,1)S(1)}, u32[]{:S(2)}, u32[]{:S(2)}) collective-permute-start(bf16[256,128]{1,0:T(8,128)(2,1)S(1)} %get-tuple-element.59), channel_id=1, source_target_pairs={{0,2},{1,3},{2,0},{3,1},{4,6},{5,7},{6,4},{7,5},{8,10},{9,11},{10,... | collective-permute-start | bytes 196616 | tf_op jit(solution)/shard_map/ppermute | solution.py:192
  29.1 6.1 %collective-permute-start.11 = (bf16[256,128]{1,0:T(8,128)(2,1)S(1)}, bf16[256,128]{1,0:T(8,128)(2,1)S(1)}, u32[]{:S(2)}, u32[]{:S(2)}) collective-permute-start(bf16[256,128]{1,0:T(8,128)(2,1)S(1)} %get-tuple-element.58), channel_id=1, source_target_pairs={{0,3},{1,2},{2,1},{3,0},{4,7},{5,6},{6,5},{7,4},{8,11},{9,10},{10,... | collective-permute-start | bytes 196616 | tf_op jit(solution)/shard_map/ppermute | solution.py:192
  29.7 5.5 %collective-permute-start.12 = (bf16[256,128]{1,0:T(8,128)(2,1)S(1)}, bf16[256,128]{1,0:T(8,128)(2,1)S(1)}, u32[]{:S(2)}, u32[]{:S(2)}) collective-permute-start(bf16[256,128]{1,0:T(8,128)(2,1)S(1)} %get-tuple-element.57), channel_id=1, source_target_pairs={{0,1},{1,0},{2,3},{3,2},{4,5},{5,4},{6,7},{7,6},{8,9},{9,8},{10,11... | collective-permute-start | bytes 196616 | tf_op jit(solution)/shard_map/ppermute | solution.py:192
  36.0 6.5 %collective-permute-start.14 = (bf16[256,128]{1,0:T(8,128)(2,1)S(1)}, bf16[256,128]{1,0:T(8,128)(2,1)S(1)}, u32[]{:S(2)}, u32[]{:S(2)}) collective-permute-start(bf16[256,128]{1,0:T(8,128)(2,1)S(1)} %fusion.9), channel_id=1, source_target_pairs={{0,1},{1,0},{2,3},{3,2},{4,5},{5,4},{6,7},{7,6},{8,9},{9,8},{10,11... | collective-permute-start | bytes 196616 | tf_op jit(solution)/shard_map/ppermute | solution.py:192
  36.1 7.9 %collective-permute-start.15 = (bf16[256,128]{1,0:T(8,128)(2,1)S(1)}, bf16[256,128]{1,0:T(8,128)(2,1)S(1)}, u32[]{:S(2)}, u32[]{:S(2)}) collective-permute-start(bf16[256,128]{1,0:T(8,128)(2,1)S(1)} %fusion.9), channel_id=1, source_target_pairs={{0,2},{1,3},{2,0},{3,1},{4,6},{5,7},{6,4},{7,5},{8,10},{9,11},{10,... | collective-permute-start | bytes 196616 | tf_op jit(solution)/shard_map/ppermute | solution.py:192
  38.6 6.1 %collective-permute-start.16 = (bf16[256,128]{1,0:T(8,128)(2,1)S(1)}, bf16[256,128]{1,0:T(8,128)(2,1)S(1)}, u32[]{:S(2)}, u32[]{:S(2)}) collective-permute-start(bf16[256,128]{1,0:T(8,128)(2,1)S(1)} %fusion.9), channel_id=1, source_target_pairs={{0,3},{1,2},{2,1},{3,0},{4,7},{5,6},{6,5},{7,4},{8,11},{9,10},{10,... | collective-permute-start | bytes 196616 | tf_op jit(solution)/shard_map/ppermute | solution.py:192
  40.4 5.9 %collective-permute-start.21 = (bf16[128,384]{1,0:T(8,128)(2,1)S(1)}, bf16[128,384]{1,0:T(8,128)(2,1)S(1)}, u32[]{:S(2)}, u32[]{:S(2)}) collective-permute-start(bf16[128,384]{1,0:T(8,128)(2,1)S(1)} %add_convert_fusion.1), channel_id=1, source_target_pairs={{0,16},{4,20},{8,24},{12,28},{16,0},{20,4},{24,8},{28,12},{1,17},{... | collective-permute-start | bytes 294920 | tf_op jit(solution)/shard_map/ppermute | solution.py:192
  42.0 6.0 %collective-permute-start.22 = (bf16[128,384]{1,0:T(8,128)(2,1)S(1)}, bf16[128,384]{1,0:T(8,128)(2,1)S(1)}, u32[]{:S(2)}, u32[]{:S(2)}) collective-permute-start(bf16[128,384]{1,0:T(8,128)(2,1)S(1)} %add_convert_fusion.1), channel_id=1, source_target_pairs={{0,24},{4,28},{8,16},{12,20},{16,8},{20,12},{24,0},{28,4},{1,25},{... | collective-permute-start | bytes 294920 | tf_op jit(solution)/shard_map/ppermute | solution.py:192
  42.5 5.6 %collective-permute-start.23 = (bf16[128,384]{1,0:T(8,128)(2,1)S(1)}, bf16[128,384]{1,0:T(8,128)(2,1)S(1)}, u32[]{:S(2)}, u32[]{:S(2)}) collective-permute-start(bf16[128,384]{1,0:T(8,128)(2,1)S(1)} %add_convert_fusion.1), channel_id=1, source_target_pairs={{0,8},{4,12},{8,0},{12,4},{16,24},{20,28},{24,16},{28,20},{1,9},{5... | collective-permute-start | bytes 294920 | tf_op jit(solution)/shard_map/ppermute | solution.py:192
  45.5 7.1 %collective-permute-start.17 = (bf16[1024,128]{1,0:T(8,128)(2,1)S(1)}, bf16[1024,128]{1,0:T(8,128)(2,1)S(1)}, u32[]{:S(2)}, u32[]{:S(2)}) collective-permute-start(bf16[1024,128]{1,0:T(8,128)(2,1)S(1)} %fusion.8), channel_id=1, source_target_pairs={{0,4},{4,0},{8,12},{12,8},{16,20},{20,16},{24,28},{28,24},{1,5},{5... | collective-permute-start | bytes 786440 | tf_op jit(solution)/shard_map/ppermute | solution.py:192
  48.2 6.8 %collective-permute-start.24 = (bf16[128,384]{1,0:T(8,128)(2,1)S(1)}, bf16[128,384]{1,0:T(8,128)(2,1)S(1)}, u32[]{:S(2)}, u32[]{:S(2)}) collective-permute-start(bf16[128,384]{1,0:T(8,128)(2,1)S(1)} %add_convert_fusion), channel_id=1, source_target_pairs={{0,1},{1,0},{2,3},{3,2},{4,5},{5,4},{6,7},{7,6},{8,9},{9,8},{10,11... | collective-permute-start | bytes 294920 | tf_op jit(solution)/shard_map/ppermute | solution.py:192
  48.2 10.8 %collective-permute-start.25 = (bf16[128,384]{1,0:T(8,128)(2,1)S(1)}, bf16[128,384]{1,0:T(8,128)(2,1)S(1)}, u32[]{:S(2)}, u32[]{:S(2)}) collective-permute-start(bf16[128,384]{1,0:T(8,128)(2,1)S(1)} %add_convert_fusion), channel_id=1, source_target_pairs={{0,2},{1,3},{2,0},{3,1},{4,6},{5,7},{6,4},{7,5},{8,10},{9,11},{10,... | collective-permute-start | bytes 294920 | tf_op jit(solution)/shard_map/ppermute | solution.py:192
  50.8 8.2 %collective-permute-start.26 = (bf16[128,384]{1,0:T(8,128)(2,1)S(1)}, bf16[128,384]{1,0:T(8,128)(2,1)S(1)}, u32[]{:S(2)}, u32[]{:S(2)}) collective-permute-start(bf16[128,384]{1,0:T(8,128)(2,1)S(1)} %add_convert_fusion), channel_id=1, source_target_pairs={{0,3},{1,2},{2,1},{3,0},{4,7},{5,6},{6,5},{7,4},{8,11},{9,10},{10,... | collective-permute-start | bytes 294920 | tf_op jit(solution)/shard_map/ppermute | solution.py:192
  52.7 6.4 %collective-permute-start.18 = (bf16[256,128]{1,0:T(8,128)(2,1)S(1)}, bf16[256,128]{1,0:T(8,128)(2,1)S(1)}, u32[]{:S(2)}, u32[]{:S(2)}) collective-permute-start(bf16[256,128]{1,0:T(8,128)(2,1)S(1)} %get-tuple-element.54), channel_id=1, source_target_pairs={{0,16},{4,20},{8,24},{12,28},{16,0},{20,4},{24,8},{28,12},{1,17},{... | collective-permute-start | bytes 196616 | tf_op jit(solution)/shard_map/ppermute | solution.py:192
  54.3 5.2 %collective-permute-start.19 = (bf16[256,128]{1,0:T(8,128)(2,1)S(1)}, bf16[256,128]{1,0:T(8,128)(2,1)S(1)}, u32[]{:S(2)}, u32[]{:S(2)}) collective-permute-start(bf16[256,128]{1,0:T(8,128)(2,1)S(1)} %get-tuple-element.56), channel_id=1, source_target_pairs={{0,24},{4,28},{8,16},{12,20},{16,8},{20,12},{24,0},{28,4},{1,25},{... | collective-permute-start | bytes 196616 | tf_op jit(solution)/shard_map/ppermute | solution.py:192
  54.9 4.6 %collective-permute-start.20 = (bf16[256,128]{1,0:T(8,128)(2,1)S(1)}, bf16[256,128]{1,0:T(8,128)(2,1)S(1)}, u32[]{:S(2)}, u32[]{:S(2)}) collective-permute-start(bf16[256,128]{1,0:T(8,128)(2,1)S(1)} %get-tuple-element.55), channel_id=1, source_target_pairs={{0,8},{4,12},{8,0},{12,4},{16,24},{20,28},{24,16},{28,20},{1,9},{5... | collective-permute-start | bytes 196616 | tf_op jit(solution)/shard_map/ppermute | solution.py:192
  (10 other events, 57.3 us)

commit v4 on v3

--- a/solution.py
+++ b/solution.py
@@ -44,7 +44,7 @@
     live = count_ref[0]
     strip = math.gcd(rows, 256)
     shift = per_node.bit_length() - 1
-    far_bit = lax.axis_size("col") // 2
+    far_bit = lax.axis_size("col") - 1
 
     @pl.when(live * edge * edge < halves * rows * cols)
     def _():
@@ -108,7 +108,7 @@
         ],
         out_specs=pl.BlockSpec(memory_space=pltpu.VMEM),
         scratch_shapes=[pltpu.SemaphoreType.DMA],
-        compiler_params=pltpu.CompilerParams(vmem_limit_bytes=rows * cols * 2 + (2 << 20)),
+        compiler_params=pltpu.CompilerParams(vmem_limit_bytes=max(47 << 20, rows * cols * 2 + (2 << 20))),
         cost_estimate=pl.CostEstimate(
             flops=0, bytes_accessed=2 * rows * cols * 2, transcendentals=0
         ),
@@ -120,7 +120,7 @@
     mean_ref, pre_ref, back_ref = refs[:3]
     arrived_refs = refs[3 : 2 + grid_cols]
     weight_ref, mine_ref, theirs_ref = refs[2 + grid_cols :]
-    own = pl.ds(grid_cols // 2 * mean_ref.shape[0], mean_ref.shape[0])
+    own = pl.ds((grid_cols - 1) * mean_ref.shape[0], mean_ref.shape[0])
     back_sum = tree_sum([back_ref[own, :]] + [ref[...] for ref in arrived_refs])
     hidden_grad = dot_parts(back_sum, weight_ref[...], 1, 1)
     first_pre = pre_ref[...]
@@ -187,18 +187,59 @@
     )(mine, theirs)
 
 
+def activate_kernel(chips, flip, *refs):
+    blocks_ref, arrived_refs = refs[0], refs[1:chips]
+    first_ref, second_ref, mean_ref, pre_ref, projected_ref = refs[chips:]
+    parts = [ref[...] for ref in arrived_refs]
+    parts.insert(flip, blocks_ref[0])
+    mean = tree_sum(parts)
+    pre = dot_parts(mean, first_ref[...])
+    mean_ref[...] = mean
+    pre_ref[...] = pre
+    projected_ref[...] = dot_parts(pre * jax.nn.sigmoid(pre), second_ref[...]).astype(BF16)
+
+
+def activate(blocks, parts, flip, first_weight, second_weight):
+    chips, rows, _ = blocks.shape
+    arrived = parts[:flip] + parts[flip + 1 :]
+
+    def kernel(*refs):
+        activate_kernel(chips, flip, *refs)
+
+    vmem = pl.BlockSpec(memory_space=pltpu.VMEM)
+    return pl.pallas_call(
+        kernel,
+        out_shape=(
+            jax.ShapeDtypeStruct((rows, first_weight.shape[0]), F32),
+            jax.ShapeDtypeStruct((rows, first_weight.shape[1]), F32),
+            jax.ShapeDtypeStruct((rows, second_weight.shape[1]), BF16),
+        ),
+        in_specs=[vmem] * (chips + 2),
+        out_specs=(vmem, vmem, vmem),
+        compiler_params=pltpu.CompilerParams(vmem_limit_bytes=6 << 20),
+        name="activate",
+    )(blocks, *arrived, first_weight, second_weight)
+
+
 def swap(value, axis, offset):
     size = lax.axis_size(axis)
     return lax.ppermute(value, axis, [(i, i ^ offset) for i in range(size)])
 
 
-def exchange(values, axis, stride, near=False):
-    half = 0 if near else len(values) // 2
-    arrived = [
-        values[0] if k == 0 else swap(values[k], axis, k * stride)
-        for k in (i ^ half for i in range(len(values)))
-    ]
-    return arrived
+def exchange(values, axis, stride, flip):
+    arrived = {}
+    for i in range(len(values)):
+        k = i ^ flip
+        arrived[k] = swap(values[k], axis, k * stride) if k else values[0]
+    return [arrived[k] for k in range(len(values))]
+
+
+def in_order(values, flip):
+    return [values[i ^ flip] for i in range(len(values))]
+
+
+def tree_in_order(values, flip):
+    return tree_sum(in_order(values, flip))
 
 
 def on_device(
@@ -211,12 +252,10 @@
     grid_cols = lax.axis_size("col")
     chips = grid_rows // 2
     per_node = node_rows // edge
-
-    def gather_col(value):
-        return exchange([value] * grid_cols, "col", 1)
-
-    parts_x = gather_col(node_features)
-    gathered_x = jnp.concatenate(parts_x, axis=0)
+    far = grid_cols - 1
+
+    features = exchange([node_features] * grid_cols, "col", 1, far)
+    gathered_x = jnp.concatenate(in_order(features, far), axis=0)
     dense = assemble(
         tile_values.reshape(slots, edge, edge),
         tile_coords.reshape(slots, 2).T,
@@ -230,36 +269,26 @@
     while offset < grid_rows:
         grad_own = jnp.concatenate([grad_own, swap(grad_own, "row", offset)], axis=0)
         offset *= 2
-
-    def chip_blocks(source):
-        other = dot_parts(dense_other, source).astype(BF16)
-        arrived = swap(other, "row", 1)
-        own, arrived = lax.optimization_barrier((dot_parts(dense_own, source), arrived))
-        return (own + arrived.astype(F32)).reshape(chips, node_rows, -1)
-
-    def plane_sum(blocks, near):
-        sent = [blocks[0]] + [blocks[i].astype(BF16) for i in range(1, chips)]
-        return tree_sum(exchange(sent, "row", 2, near))
-
-    gathered_x, grad_own = lax.optimization_barrier((gathered_x, grad_own))
+    partner = dot_parts(dense_other, gathered_x).astype(BF16)
+    back_own = dot_parts(dense_own, grad_own, 0)
+    arrived = swap(partner, "row", 1)
+    own, arrived = lax.optimization_barrier((dot_parts(dense_own, gathered_x), arrived))
+    first_blocks = (own + arrived.astype(F32)).reshape(chips, node_rows, -1)
     grad_other = swap(grad_own, "row", 1)
-    first_blocks = chip_blocks(gathered_x)
-
-    first_blocks, grad_own, grad_other = lax.optimization_barrier(
-        (first_blocks, grad_own, grad_other)
+    back_part = back_own + dot_parts(dense_other, grad_other, 0)
+    first_blocks, back_part = lax.optimization_barrier((first_blocks, back_part))
+    first_sent = [first_blocks[0]] + [block.astype(BF16) for block in first_blocks[1:]]
+    back_blocks = back_part.reshape(grid_cols, node_rows, -1)
+    back_sent = [back_blocks[k ^ far] for k in range(grid_cols)]
+    back_sent = [back_sent[0]] + [block.astype(BF16) for block in back_sent[1:]]
+    first_parts = exchange(first_sent, "row", 2, chips - 1)
+    back_arrived = in_order(exchange(back_sent, "col", 1, grid_cols // 2), grid_cols // 2)
+    back_arrived.pop(grid_cols // 2)
+    first_mean, first_pre, projected = activate(
+        first_blocks, in_order(first_parts, chips - 1), chips - 1, first_weight, second_weight
     )
-    first_mean = plane_sum(first_blocks, False)
-    back_part = dot_parts(dense_own, grad_own, 0) + dot_parts(dense_other, grad_other, 0)
-    back_blocks = back_part.reshape(grid_cols, node_rows, -1)
-    back_sent = [back_blocks[i ^ (grid_cols // 2)] for i in range(grid_cols)]
-    back_sent = [back_sent[0]] + [block.astype(BF16) for block in back_sent[1:]]
-    back_arrived = exchange(back_sent, "col", 1, False)
-    back_arrived.pop(grid_cols // 2)
-
-    first_pre = dot_parts(first_mean, first_weight)
-    projected = dot_parts(first_pre * jax.nn.sigmoid(first_pre), second_weight).astype(BF16)
     projected, first_pre = lax.optimization_barrier((projected, first_pre))
-    parts_h = exchange([projected] * grid_cols, "col", 1, True)
+    parts_h = exchange([projected] * grid_cols, "col", 1, grid_cols - 1)
 
     scale = 1.0 / math.sqrt(node_rows * grid_rows * grid_cols)
     mine, theirs = local_grads(
@@ -267,11 +296,16 @@
     )
     mine = (mine + swap(theirs, "row", 1).astype(F32)).astype(BF16)
     _, *parts_h = lax.optimization_barrier((mine, *parts_h))
-    parts_h = lax.optimization_barrier(parts_h)
-    parts_h = [parts_h[i ^ (grid_cols // 2)] for i in range(grid_cols)]
-    output = plane_sum(chip_blocks(jnp.concatenate(parts_h, axis=0)), False).astype(BF16)
-    mine = tree_sum(exchange([mine] * chips, "row", 2, False)).astype(BF16)
-    mine = tree_sum(exchange([mine] * grid_cols, "col", 1, True))
+    parts_h = in_order(lax.optimization_barrier(in_order(parts_h, grid_cols - 1)), grid_cols - 1)
+    gathered_h = jnp.concatenate(in_order(parts_h, far), axis=0)
+    partner = dot_parts(dense_other, gathered_h).astype(BF16)
+    arrived = swap(partner, "row", 1)
+    own, arrived = lax.optimization_barrier((dot_parts(dense_own, gathered_h), arrived))
+    blocks = (own + arrived.astype(F32)).reshape(chips, node_rows, -1)
+    mine = tree_in_order(exchange([mine] * chips, "row", 2, 0), 0).astype(BF16)
+    sent = [blocks[0]] + [block.astype(BF16) for block in blocks[1:]]
+    output = tree_in_order(exchange(sent, "row", 2, chips // 2), chips // 2).astype(BF16)
+    mine = tree_in_order(exchange([mine] * grid_cols, "col", 1, 0), 0)
     first_grad, second_grad = join(mine, swap(mine, "row", 1), first_weight.shape[1])
     return (output, first_grad, second_grad)
 

time: 61.6 us -> 60.2 us (0.977)
  waiting for transfers between devices: 12.4 us -> 15.3 us
  local copies, waits for them, and re-layouts: 2.99 us -> 0.88 us
  starting transfers between devices: 34.2 us -> 32.7 us
  Pallas kernels: 3.16 us -> 4.12 us
  other arithmetic: 1.98 us -> 1.05 us
  matrix products: 5.1 us -> 4.33 us
    ppermute x28, waiting for transfers between devices: 12.4 us -> 15.3 us  [swap(): return lax.ppermute(value, axis, [(i, i ^ offset) for i in range(size)])]
    unnamed x15 -> x18, local copies, waits for them, and re-layouts: 2.91 us -> 0.78 us
    ppermute x28, starting transfers between devices: 34.2 us -> 32.7 us  [swap(): return lax.ppermute(value, axis, [(i, i ^ offset) for i in range(size)])]
    concatenate x2 -> x1, other arithmetic: 0.87 us -> 0.01 us  [on_device(): jnp.concatenate([grad_own, swap(grad_own, 'row', offset)], axis=0)]
    dot_general x10 -> x6, matrix products: 5.1 us -> 4.33 us  [dot_parts(): lax.dot_general(one, other, (((left_dim,), (right_dim,)), ((), ())), pref...]
  transfers between devices with their start and end apart: 28 -> 28, of which waited for: 11 -> 13; matrix products, arithmetic and copies ran while one was open for 10% -> 9% of each run, Pallas kernels for 3% -> 4%
where the time goes in v4:
time: 60.2 us; the launch traced here: 60 us
  starting transfers between devices  32.7 us (54%)
  waiting for transfers between devices  15.3 us (25%)
  matrix products  4.33 us (7%)
  Pallas kernels  4.12 us (7%)
  between operations  1.62 us (3%)
  other arithmetic  1.05 us (2%)
  local copies, waits for them, and re-layouts  0.88 us (1%)
    ppermute x28, starting transfers between devices, swap(): return lax.ppermute(value, axis, [(i, i ^ offset) for i in range(size)])  32.7 us
    ppermute x28, waiting for transfers between devices, swap(): return lax.ppermute(value, axis, [(i, i ^ offset) for i in range(size)])  15.3 us
    dot_general x6, matrix products, dot_parts(): lax.dot_general(one, other, (((left_dim,), (right_dim,)), ((), ())), pref...  4.33 us
    pallas_call x1, Pallas kernels, assemble(): pl.pallas_call(kernel, out_shape=jax.ShapeDtypeStruct((2, rows // 2, cols...  2.11 us
  transfers between devices with their start and end apart: 28, of which 13 were waited for; matrix products, arithmetic and copies ran while one was open for 9% of the time, Pallas kernels for 4%

profile of v4, /device:TPU:0, one launch (start us, length us, event | category | flops | bytes accessed | tf_op | source)
XLA Modules:
  0.0 60.0 jit_solution(1515955673530053260)
XLA Ops:
  0.6 5.1 %collective-permute-start = (bf16[256,256]{1,0:T(8,128)(2,1)}, bf16[256,256]{1,0:T(8,128)(2,1)S(1)}, u32[]{:S(2)}, u32[]{:S(2)}) collective-permute-start(bf16[256,256]{1,0:T(8,128)(2,1)} %param.7), channel_id=1, source_target_pairs={{0,3},{1,2},{2,1},{3,0},{4,7},{5,6},{6,5},{7,4},{8,11},{9,10},{10,... | collective-permute-start | bytes 393224 | tf_op jit(solution)/shard_map/ppermute | solution.py:226
  6.4 1.6 %collective-permute-start.4 = (bf16[256,128]{1,0:T(8,128)(2,1)}, bf16[256,128]{1,0:T(8,128)(2,1)S(1)}, u32[]{:S(2)}, u32[]{:S(2)}) collective-permute-start(bf16[256,128]{1,0:T(8,128)(2,1)} %param.13), channel_id=1, source_target_pairs={{0,8},{4,12},{8,0},{12,4},{16,24},{20,28},{24,16},{28,20},{1,9},{5... | collective-permute-start | bytes 196616 | tf_op jit(solution)/shard_map/ppermute | solution.py:226
  9.4 2.1 %assemble.1 = bf16[2,1024,1024]{2,1,0:T(8,128)(2,1)S(1)} custom-call(s32[2,128]{1,0:T(2,128)S(1)} %bitcast.37, s32[1]{0:T(128)} %bitcast.34.refs_1_, bf16[128,128,128]{2,1,0:T(8,128)(2,1)} %bitcast.38), custom_call_target="tpu_custom_call" | custom-call | bytes 8388608 | tf_op jit(solution)/shard_map/assemble/pallas_call | solution.py:101
  11.5 1.9 %collective-permute-start.5 = (bf16[512,128]{1,0:T(8,128)(2,1)S(1)}, bf16[512,128]{1,0:T(8,128)(2,1)S(1)}, u32[]{:S(2)}, u32[]{:S(2)}) collective-permute-start(bf16[512,128]{1,0:T(8,128)(2,1)S(1)} %pad_maximum_fusion), channel_id=1, source_target_pairs={{0,16},{4,20},{8,24},{12,28},{16,0},{20,4},{24,8},{28,12},{1,17},{... | collective-permute-start | bytes 393224 | tf_op jit(solution)/shard_map/ppermute | solution.py:226
  13.5 3.5 %collective-permute-done.1 = bf16[256,256]{1,0:T(8,128)(2,1)S(1)} collective-permute-done((bf16[256,256]{1,0:T(8,128)(2,1)}, bf16[256,256]{1,0:T(8,128)(2,1)S(1)}, u32[]{:S(2)}, u32[]{:S(2)}) %collective-permute-start.1) | collective-permute-done | bytes 131104 | tf_op jit(solution)/shard_map/ppermute | solution.py:226
  19.2 1.0 %collective-permute-done.6 = bf16[1024,128]{1,0:T(8,128)(2,1)S(1)} collective-permute-done((bf16[1024,128]{1,0:T(8,128)(2,1)S(1)}, bf16[1024,128]{1,0:T(8,128)(2,1)S(1)}, u32[]{:S(2)}, u32[]{:S(2)}) %collective-permute-start.6) | collective-permute-done | bytes 262176 | tf_op jit(solution)/shard_map/ppermute | solution.py:226
  20.9 0.8 %fusion.7.refs_2_ = f32[1024,128]{1,0:T(8,128)S(1)} fusion(f32[1024,128]{1,0:T(8,128)S(1)} %fusion.4, bf16[1024,128]{1,0:T(8,128)(2,1)S(1)} %constant_dynamic-update-slice_fusion.4, bf16[2,1024,1024]{2,1,0:T(8,128)(2,1)S(1)} %assemble.1), kind=kOutput, calls=%fused_computation.9 | convolution fusion | flops 268566528 | bytes 3407872 | tf_op jit(solution)/shard_map/dot_general | solution.py:26
  21.9 2.5 %collective-permute-start.7 = (bf16[256,256]{1,0:T(8,128)(2,1)S(1)}, bf16[256,256]{1,0:T(8,128)(2,1)S(1)}, u32[]{:S(2)}, u32[]{:S(2)}) collective-permute-start(bf16[256,256]{1,0:T(8,128)(2,1)S(1)} %get-tuple-element.53), channel_id=1, source_target_pairs={{0,24},{4,28},{8,16},{12,20},{16,8},{20,12},{24,0},{28,4},{1,25},{... | collective-permute-start | bytes 393224 | tf_op jit(solution)/shard_map/ppermute | solution.py:226
  25.9 2.2 %collective-permute-start.11 = (bf16[256,128]{1,0:T(8,128)(2,1)S(1)}, bf16[256,128]{1,0:T(8,128)(2,1)S(1)}, u32[]{:S(2)}, u32[]{:S(2)}) collective-permute-start(bf16[256,128]{1,0:T(8,128)(2,1)S(1)} %get-tuple-element.58), channel_id=1, source_target_pairs={{0,3},{1,2},{2,1},{3,0},{4,7},{5,6},{6,5},{7,4},{8,11},{9,10},{10,... | collective-permute-start | bytes 196616 | tf_op jit(solution)/shard_map/ppermute | solution.py:226
  29.1 2.1 %collective-permute-done.8.refs_2_ = bf16[256,256]{1,0:T(8,128)(2,1)S(1)} collective-permute-done((bf16[256,256]{1,0:T(8,128)(2,1)S(1)}, bf16[256,256]{1,0:T(8,128)(2,1)S(1)}, u32[]{:S(2)}, u32[]{:S(2)}) %collective-permute-start.8) | collective-permute-done | bytes 131104 | tf_op jit(solution)/shard_map/ppermute | solution.py:226
  31.9 1.0 %collective-permute-done.10.refs_3_ = bf16[256,128]{1,0:T(8,128)(2,1)S(1)} collective-permute-done((bf16[256,128]{1,0:T(8,128)(2,1)S(1)}, bf16[256,128]{1,0:T(8,128)(2,1)S(1)}, u32[]{:S(2)}, u32[]{:S(2)}) %collective-permute-start.10) | collective-permute-done | bytes 65568 | tf_op jit(solution)/shard_map/ppermute | solution.py:226
  34.2 1.0 %collective-permute-start.14 = (bf16[256,128]{1,0:T(8,128)(2,1)S(1)}, bf16[256,128]{1,0:T(8,128)(2,1)S(1)}, u32[]{:S(2)}, u32[]{:S(2)}) collective-permute-start(bf16[256,128]{1,0:T(8,128)(2,1)S(1)} %get-tuple-element.44), channel_id=1, source_target_pairs={{0,1},{1,0},{2,3},{3,2},{4,5},{5,4},{6,7},{7,6},{8,9},{9,8},{10,11... | collective-permute-start | bytes 196616 | tf_op jit(solution)/shard_map/ppermute | solution.py:226
  35.2 1.9 %collective-permute-start.15 = (bf16[256,128]{1,0:T(8,128)(2,1)S(1)}, bf16[256,128]{1,0:T(8,128)(2,1)S(1)}, u32[]{:S(2)}, u32[]{:S(2)}) collective-permute-start(bf16[256,128]{1,0:T(8,128)(2,1)S(1)} %get-tuple-element.44), channel_id=1, source_target_pairs={{0,2},{1,3},{2,0},{3,1},{4,6},{5,7},{6,4},{7,5},{8,10},{9,11},{10,... | collective-permute-start | bytes 196616 | tf_op jit(solution)/shard_map/ppermute | solution.py:226
  37.2 1.5 %collective-permute-start.16 = (bf16[256,128]{1,0:T(8,128)(2,1)S(1)}, bf16[256,128]{1,0:T(8,128)(2,1)S(1)}, u32[]{:S(2)}, u32[]{:S(2)}) collective-permute-start(bf16[256,128]{1,0:T(8,128)(2,1)S(1)} %get-tuple-element.44), channel_id=1, source_target_pairs={{0,3},{1,2},{2,1},{3,0},{4,7},{5,6},{6,5},{7,4},{8,11},{9,10},{10,... | collective-permute-start | bytes 196616 | tf_op jit(solution)/shard_map/ppermute | solution.py:226
  38.7 1.6 %collective-permute-start.21 = (bf16[128,384]{1,0:T(8,128)(2,1)S(1)}, bf16[128,384]{1,0:T(8,128)(2,1)S(1)}, u32[]{:S(2)}, u32[]{:S(2)}) collective-permute-start(bf16[128,384]{1,0:T(8,128)(2,1)S(1)} %add_convert_fusion.1), channel_id=1, source_target_pairs={{0,8},{4,12},{8,0},{12,4},{16,24},{20,28},{24,16},{28,20},{1,9},{5... | collective-permute-start | bytes 294920 | tf_op jit(solution)/shard_map/ppermute | solution.py:226
  40.4 1.5 %collective-permute-start.22 = (bf16[128,384]{1,0:T(8,128)(2,1)S(1)}, bf16[128,384]{1,0:T(8,128)(2,1)S(1)}, u32[]{:S(2)}, u32[]{:S(2)}) collective-permute-start(bf16[128,384]{1,0:T(8,128)(2,1)S(1)} %add_convert_fusion.1), channel_id=1, source_target_pairs={{0,16},{4,20},{8,24},{12,28},{16,0},{20,4},{24,8},{28,12},{1,17},{... | collective-permute-start | bytes 294920 | tf_op jit(solution)/shard_map/ppermute | solution.py:226
  42.3 1.4 %collective-permute-done.15 = bf16[256,128]{1,0:T(8,128)(2,1)S(1)} collective-permute-done((bf16[256,128]{1,0:T(8,128)(2,1)S(1)}, bf16[256,128]{1,0:T(8,128)(2,1)S(1)}, u32[]{:S(2)}, u32[]{:S(2)}) %collective-permute-start.15) | collective-permute-done | bytes 65568 | tf_op jit(solution)/shard_map/ppermute | solution.py:226
  46.0 1.4 %collective-permute-done.23 = bf16[128,384]{1,0:T(8,128)(2,1)S(1)} collective-permute-done((bf16[128,384]{1,0:T(8,128)(2,1)S(1)}, bf16[128,384]{1,0:T(8,128)(2,1)S(1)}, u32[]{:S(2)}, u32[]{:S(2)}) %collective-permute-start.23) | collective-permute-done | bytes 98336 | tf_op jit(solution)/shard_map/ppermute | solution.py:226
  47.6 3.0 %collective-permute-start.25 = (bf16[128,384]{1,0:T(8,128)(2,1)S(1)}, bf16[128,384]{1,0:T(8,128)(2,1)S(1)}, u32[]{:S(2)}, u32[]{:S(2)}) collective-permute-start(bf16[128,384]{1,0:T(8,128)(2,1)S(1)} %add_convert_fusion), channel_id=1, source_target_pairs={{0,2},{1,3},{2,0},{3,1},{4,6},{5,7},{6,4},{7,5},{8,10},{9,11},{10,... | collective-permute-start | bytes 294920 | tf_op jit(solution)/shard_map/ppermute | solution.py:226
  50.5 1.4 %collective-permute-start.26 = (bf16[128,384]{1,0:T(8,128)(2,1)S(1)}, bf16[128,384]{1,0:T(8,128)(2,1)S(1)}, u32[]{:S(2)}, u32[]{:S(2)}) collective-permute-start(bf16[128,384]{1,0:T(8,128)(2,1)S(1)} %add_convert_fusion), channel_id=1, source_target_pairs={{0,3},{1,2},{2,1},{3,0},{4,7},{5,6},{6,5},{7,4},{8,11},{9,10},{10,... | collective-permute-start | bytes 294920 | tf_op jit(solution)/shard_map/ppermute | solution.py:226
  52.8 1.4 %collective-permute-start.19 = (bf16[256,128]{1,0:T(8,128)(2,1)S(1)}, bf16[256,128]{1,0:T(8,128)(2,1)S(1)}, u32[]{:S(2)}, u32[]{:S(2)}) collective-permute-start(bf16[256,128]{1,0:T(8,128)(2,1)S(1)} %get-tuple-element.56), channel_id=1, source_target_pairs={{0,24},{4,28},{8,16},{12,20},{16,8},{20,12},{24,0},{28,4},{1,25},{... | collective-permute-start | bytes 196616 | tf_op jit(solution)/shard_map/ppermute | solution.py:226
  54.2 1.4 %collective-permute-start.20 = (bf16[256,128]{1,0:T(8,128)(2,1)S(1)}, bf16[256,128]{1,0:T(8,128)(2,1)S(1)}, u32[]{:S(2)}, u32[]{:S(2)}) collective-permute-start(bf16[256,128]{1,0:T(8,128)(2,1)S(1)} %get-tuple-element.55), channel_id=1, source_target_pairs={{0,8},{4,12},{8,0},{12,4},{16,24},{20,28},{24,16},{28,20},{1,9},{5... | collective-permute-start | bytes 196616 | tf_op jit(solution)/shard_map/ppermute | solution.py:226
  55.6 1.9 %collective-permute-done.25 = bf16[128,384]{1,0:T(8,128)(2,1)S(1)} collective-permute-done((bf16[128,384]{1,0:T(8,128)(2,1)S(1)}, bf16[128,384]{1,0:T(8,128)(2,1)S(1)}, u32[]{:S(2)}, u32[]{:S(2)}) %collective-permute-start.25) | collective-permute-done | bytes 98336 | tf_op jit(solution)/shard_map/ppermute | solution.py:226
  59.2 0.8 %join_grads.1 = (f32[256,256]{1,0:T(8,128)}, f32[256,128]{1,0:T(8,128)}) custom-call(f32[128,384]{1,0:T(8,128)S(1)} %add_add_fusion.mine_ref, f32[128,384]{1,0:T(8,128)S(1)} %collective-permute-done.27.theirs_ref), custom_call_target="tpu_custom_call" | custom-call | tf_op jit(solution)/shard_map/join_grads/pallas_call | solution.py:177
  (75 shorter events, 14.0 us)
Async XLA Ops:
  0.6 12.8 %collective-permute-start = (bf16[256,256]{1,0:T(8,128)(2,1)}, bf16[256,256]{1,0:T(8,128)(2,1)S(1)}, u32[]{:S(2)}, u32[]{:S(2)}) collective-permute-start(bf16[256,256]{1,0:T(8,128)(2,1)} %param.7), channel_id=1, source_target_pairs={{0,3},{1,2},{2,1},{3,0},{4,7},{5,6},{6,5},{7,4},{8,11},{9,10},{10,... | collective-permute-start | bytes 393224 | tf_op jit(solution)/shard_map/ppermute | solution.py:226
  5.7 11.3 %collective-permute-start.1 = (bf16[256,256]{1,0:T(8,128)(2,1)}, bf16[256,256]{1,0:T(8,128)(2,1)S(1)}, u32[]{:S(2)}, u32[]{:S(2)}) collective-permute-start(bf16[256,256]{1,0:T(8,128)(2,1)} %param.7), channel_id=1, source_target_pairs={{0,2},{1,3},{2,0},{3,1},{4,6},{5,7},{6,4},{7,5},{8,10},{9,11},{10,... | collective-permute-start | bytes 393224 | tf_op jit(solution)/shard_map/ppermute | solution.py:226
  5.7 11.3 %collective-permute-start.2 = (bf16[256,256]{1,0:T(8,128)(2,1)}, bf16[256,256]{1,0:T(8,128)(2,1)S(1)}, u32[]{:S(2)}, u32[]{:S(2)}) collective-permute-start(bf16[256,256]{1,0:T(8,128)(2,1)} %param.7), channel_id=1, source_target_pairs={{0,1},{1,0},{2,3},{3,2},{4,5},{5,4},{6,7},{7,6},{8,9},{9,8},{10,11... | collective-permute-start | bytes 393224 | tf_op jit(solution)/shard_map/ppermute | solution.py:226
  6.4 5.1 %collective-permute-start.4 = (bf16[256,128]{1,0:T(8,128)(2,1)}, bf16[256,128]{1,0:T(8,128)(2,1)S(1)}, u32[]{:S(2)}, u32[]{:S(2)}) collective-permute-start(bf16[256,128]{1,0:T(8,128)(2,1)} %param.13), channel_id=1, source_target_pairs={{0,8},{4,12},{8,0},{12,4},{16,24},{20,28},{24,16},{28,20},{1,9},{5... | collective-permute-start | bytes 196616 | tf_op jit(solution)/shard_map/ppermute | solution.py:226
  11.5 6.4 %collective-permute-start.5 = (bf16[512,128]{1,0:T(8,128)(2,1)S(1)}, bf16[512,128]{1,0:T(8,128)(2,1)S(1)}, u32[]{:S(2)}, u32[]{:S(2)}) collective-permute-start(bf16[512,128]{1,0:T(8,128)(2,1)S(1)} %pad_maximum_fusion), channel_id=1, source_target_pairs={{0,16},{4,20},{8,24},{12,28},{16,0},{20,4},{24,8},{28,12},{1,17},{... | collective-permute-start | bytes 393224 | tf_op jit(solution)/shard_map/ppermute | solution.py:226
  21.9 6.8 %collective-permute-start.7 = (bf16[256,256]{1,0:T(8,128)(2,1)S(1)}, bf16[256,256]{1,0:T(8,128)(2,1)S(1)}, u32[]{:S(2)}, u32[]{:S(2)}) collective-permute-start(bf16[256,256]{1,0:T(8,128)(2,1)S(1)} %get-tuple-element.53), channel_id=1, source_target_pairs={{0,24},{4,28},{8,16},{12,20},{16,8},{20,12},{24,0},{28,4},{1,25},{... | collective-permute-start | bytes 393224 | tf_op jit(solution)/shard_map/ppermute | solution.py:226
  24.4 6.8 %collective-permute-start.8 = (bf16[256,256]{1,0:T(8,128)(2,1)S(1)}, bf16[256,256]{1,0:T(8,128)(2,1)S(1)}, u32[]{:S(2)}, u32[]{:S(2)}) collective-permute-start(bf16[256,256]{1,0:T(8,128)(2,1)S(1)} %get-tuple-element.52), channel_id=1, source_target_pairs={{0,16},{4,20},{8,24},{12,28},{16,0},{20,4},{24,8},{28,12},{1,17},{... | collective-permute-start | bytes 393224 | tf_op jit(solution)/shard_map/ppermute | solution.py:226
  24.9 6.4 %collective-permute-start.9 = (bf16[256,256]{1,0:T(8,128)(2,1)S(1)}, bf16[256,256]{1,0:T(8,128)(2,1)S(1)}, u32[]{:S(2)}, u32[]{:S(2)}) collective-permute-start(bf16[256,256]{1,0:T(8,128)(2,1)S(1)} %get-tuple-element.51), channel_id=1, source_target_pairs={{0,8},{4,12},{8,0},{12,4},{16,24},{20,28},{24,16},{28,20},{1,9},{5... | collective-permute-start | bytes 393224 | tf_op jit(solution)/shard_map/ppermute | solution.py:226
  25.5 7.4 %collective-permute-start.10 = (bf16[256,128]{1,0:T(8,128)(2,1)S(1)}, bf16[256,128]{1,0:T(8,128)(2,1)S(1)}, u32[]{:S(2)}, u32[]{:S(2)}) collective-permute-start(bf16[256,128]{1,0:T(8,128)(2,1)S(1)} %get-tuple-element.59), channel_id=1, source_target_pairs={{0,2},{1,3},{2,0},{3,1},{4,6},{5,7},{6,4},{7,5},{8,10},{9,11},{10,... | collective-permute-start | bytes 196616 | tf_op jit(solution)/shard_map/ppermute | solution.py:226
  25.9 7.0 %collective-permute-start.11 = (bf16[256,128]{1,0:T(8,128)(2,1)S(1)}, bf16[256,128]{1,0:T(8,128)(2,1)S(1)}, u32[]{:S(2)}, u32[]{:S(2)}) collective-permute-start(bf16[256,128]{1,0:T(8,128)(2,1)S(1)} %get-tuple-element.58), channel_id=1, source_target_pairs={{0,3},{1,2},{2,1},{3,0},{4,7},{5,6},{6,5},{7,4},{8,11},{9,10},{10,... | collective-permute-start | bytes 196616 | tf_op jit(solution)/shard_map/ppermute | solution.py:226
  28.7 4.8 %collective-permute-start.12 = (bf16[256,128]{1,0:T(8,128)(2,1)S(1)}, bf16[256,128]{1,0:T(8,128)(2,1)S(1)}, u32[]{:S(2)}, u32[]{:S(2)}) collective-permute-start(bf16[256,128]{1,0:T(8,128)(2,1)S(1)} %get-tuple-element.57), channel_id=1, source_target_pairs={{0,1},{1,0},{2,3},{3,2},{4,5},{5,4},{6,7},{7,6},{8,9},{9,8},{10,11... | collective-permute-start | bytes 196616 | tf_op jit(solution)/shard_map/ppermute | solution.py:226
  34.2 4.5 %collective-permute-start.13 = (bf16[128,384]{1,0:T(8,128)(2,1)S(1)}, bf16[128,384]{1,0:T(8,128)(2,1)S(1)}, u32[]{:S(2)}, u32[]{:S(2)}) collective-permute-start(bf16[128,384]{1,0:T(8,128)(2,1)S(1)} %get-tuple-element.35), channel_id=1, source_target_pairs={{0,4},{4,0},{8,12},{12,8},{16,20},{20,16},{24,28},{28,24},{1,5},{5... | collective-permute-start | bytes 294920 | tf_op jit(solution)/shard_map/ppermute | solution.py:226
  34.2 7.7 %collective-permute-start.14 = (bf16[256,128]{1,0:T(8,128)(2,1)S(1)}, bf16[256,128]{1,0:T(8,128)(2,1)S(1)}, u32[]{:S(2)}, u32[]{:S(2)}) collective-permute-start(bf16[256,128]{1,0:T(8,128)(2,1)S(1)} %get-tuple-element.44), channel_id=1, source_target_pairs={{0,1},{1,0},{2,3},{3,2},{4,5},{5,4},{6,7},{7,6},{8,9},{9,8},{10,11... | collective-permute-start | bytes 196616 | tf_op jit(solution)/shard_map/ppermute | solution.py:226
  35.2 8.5 %collective-permute-start.15 = (bf16[256,128]{1,0:T(8,128)(2,1)S(1)}, bf16[256,128]{1,0:T(8,128)(2,1)S(1)}, u32[]{:S(2)}, u32[]{:S(2)}) collective-permute-start(bf16[256,128]{1,0:T(8,128)(2,1)S(1)} %get-tuple-element.44), channel_id=1, source_target_pairs={{0,2},{1,3},{2,0},{3,1},{4,6},{5,7},{6,4},{7,5},{8,10},{9,11},{10,... | collective-permute-start | bytes 196616 | tf_op jit(solution)/shard_map/ppermute | solution.py:226
  37.2 6.6 %collective-permute-start.16 = (bf16[256,128]{1,0:T(8,128)(2,1)S(1)}, bf16[256,128]{1,0:T(8,128)(2,1)S(1)}, u32[]{:S(2)}, u32[]{:S(2)}) collective-permute-start(bf16[256,128]{1,0:T(8,128)(2,1)S(1)} %get-tuple-element.44), channel_id=1, source_target_pairs={{0,3},{1,2},{2,1},{3,0},{4,7},{5,6},{6,5},{7,4},{8,11},{9,10},{10,... | collective-permute-start | bytes 196616 | tf_op jit(solution)/shard_map/ppermute | solution.py:226
  38.7 6.6 %collective-permute-start.21 = (bf16[128,384]{1,0:T(8,128)(2,1)S(1)}, bf16[128,384]{1,0:T(8,128)(2,1)S(1)}, u32[]{:S(2)}, u32[]{:S(2)}) collective-permute-start(bf16[128,384]{1,0:T(8,128)(2,1)S(1)} %add_convert_fusion.1), channel_id=1, source_target_pairs={{0,8},{4,12},{8,0},{12,4},{16,24},{20,28},{24,16},{28,20},{1,9},{5... | collective-permute-start | bytes 294920 | tf_op jit(solution)/shard_map/ppermute | solution.py:226
  40.4 5.7 %collective-permute-start.22 = (bf16[128,384]{1,0:T(8,128)(2,1)S(1)}, bf16[128,384]{1,0:T(8,128)(2,1)S(1)}, u32[]{:S(2)}, u32[]{:S(2)}) collective-permute-start(bf16[128,384]{1,0:T(8,128)(2,1)S(1)} %add_convert_fusion.1), channel_id=1, source_target_pairs={{0,16},{4,20},{8,24},{12,28},{16,0},{20,4},{24,8},{28,12},{1,17},{... | collective-permute-start | bytes 294920 | tf_op jit(solution)/shard_map/ppermute | solution.py:226
  41.9 5.5 %collective-permute-start.23 = (bf16[128,384]{1,0:T(8,128)(2,1)S(1)}, bf16[128,384]{1,0:T(8,128)(2,1)S(1)}, u32[]{:S(2)}, u32[]{:S(2)}) collective-permute-start(bf16[128,384]{1,0:T(8,128)(2,1)S(1)} %add_convert_fusion.1), channel_id=1, source_target_pairs={{0,24},{4,28},{8,16},{12,20},{16,8},{20,12},{24,0},{28,4},{1,25},{... | collective-permute-start | bytes 294920 | tf_op jit(solution)/shard_map/ppermute | solution.py:226
  44.5 7.4 %collective-permute-start.17 = (bf16[1024,128]{1,0:T(8,128)(2,1)S(1)}, bf16[1024,128]{1,0:T(8,128)(2,1)S(1)}, u32[]{:S(2)}, u32[]{:S(2)}) collective-permute-start(bf16[1024,128]{1,0:T(8,128)(2,1)S(1)} %fusion.8), channel_id=1, source_target_pairs={{0,4},{4,0},{8,12},{12,8},{16,20},{20,16},{24,28},{28,24},{1,5},{5... | collective-permute-start | bytes 786440 | tf_op jit(solution)/shard_map/ppermute | solution.py:226
  47.5 6.7 %collective-permute-start.24 = (bf16[128,384]{1,0:T(8,128)(2,1)S(1)}, bf16[128,384]{1,0:T(8,128)(2,1)S(1)}, u32[]{:S(2)}, u32[]{:S(2)}) collective-permute-start(bf16[128,384]{1,0:T(8,128)(2,1)S(1)} %add_convert_fusion), channel_id=1, source_target_pairs={{0,1},{1,0},{2,3},{3,2},{4,5},{5,4},{6,7},{7,6},{8,9},{9,8},{10,11... | collective-permute-start | bytes 294920 | tf_op jit(solution)/shard_map/ppermute | solution.py:226
  47.6 10.0 %collective-permute-start.25 = (bf16[128,384]{1,0:T(8,128)(2,1)S(1)}, bf16[128,384]{1,0:T(8,128)(2,1)S(1)}, u32[]{:S(2)}, u32[]{:S(2)}) collective-permute-start(bf16[128,384]{1,0:T(8,128)(2,1)S(1)} %add_convert_fusion), channel_id=1, source_target_pairs={{0,2},{1,3},{2,0},{3,1},{4,6},{5,7},{6,4},{7,5},{8,10},{9,11},{10,... | collective-permute-start | bytes 294920 | tf_op jit(solution)/shard_map/ppermute | solution.py:226
  50.5 7.0 %collective-permute-start.26 = (bf16[128,384]{1,0:T(8,128)(2,1)S(1)}, bf16[128,384]{1,0:T(8,128)(2,1)S(1)}, u32[]{:S(2)}, u32[]{:S(2)}) collective-permute-start(bf16[128,384]{1,0:T(8,128)(2,1)S(1)} %add_convert_fusion), channel_id=1, source_target_pairs={{0,3},{1,2},{2,1},{3,0},{4,7},{5,6},{6,5},{7,4},{8,11},{9,10},{10,... | collective-permute-start | bytes 294920 | tf_op jit(solution)/shard_map/ppermute | solution.py:226
  52.0 5.6 %collective-permute-start.18 = (bf16[256,128]{1,0:T(8,128)(2,1)S(1)}, bf16[256,128]{1,0:T(8,128)(2,1)S(1)}, u32[]{:S(2)}, u32[]{:S(2)}) collective-permute-start(bf16[256,128]{1,0:T(8,128)(2,1)S(1)} %get-tuple-element.54), channel_id=1, source_target_pairs={{0,16},{4,20},{8,24},{12,28},{16,0},{20,4},{24,8},{28,12},{1,17},{... | collective-permute-start | bytes 196616 | tf_op jit(solution)/shard_map/ppermute | solution.py:226
  52.8 5.2 %collective-permute-start.19 = (bf16[256,128]{1,0:T(8,128)(2,1)S(1)}, bf16[256,128]{1,0:T(8,128)(2,1)S(1)}, u32[]{:S(2)}, u32[]{:S(2)}) collective-permute-start(bf16[256,128]{1,0:T(8,128)(2,1)S(1)} %get-tuple-element.56), channel_id=1, source_target_pairs={{0,24},{4,28},{8,16},{12,20},{16,8},{20,12},{24,0},{28,4},{1,25},{... | collective-permute-start | bytes 196616 | tf_op jit(solution)/shard_map/ppermute | solution.py:226
  (9 other events, 43.4 us)

commit v5 on v4

--- a/solution.py
+++ b/solution.py
@@ -288,7 +288,7 @@
         first_blocks, in_order(first_parts, chips - 1), chips - 1, first_weight, second_weight
     )
     projected, first_pre = lax.optimization_barrier((projected, first_pre))
-    parts_h = exchange([projected] * grid_cols, "col", 1, grid_cols - 1)
+    parts_h = exchange([projected] * grid_cols, "col", 1, grid_cols // 2)
 
     scale = 1.0 / math.sqrt(node_rows * grid_rows * grid_cols)
     mine, theirs = local_grads(
@@ -296,13 +296,13 @@
     )
     mine = (mine + swap(theirs, "row", 1).astype(F32)).astype(BF16)
     _, *parts_h = lax.optimization_barrier((mine, *parts_h))
-    parts_h = in_order(lax.optimization_barrier(in_order(parts_h, grid_cols - 1)), grid_cols - 1)
+    parts_h = in_order(lax.optimization_barrier(in_order(parts_h, grid_cols // 2)), grid_cols // 2)
     gathered_h = jnp.concatenate(in_order(parts_h, far), axis=0)
     partner = dot_parts(dense_other, gathered_h).astype(BF16)
     arrived = swap(partner, "row", 1)
     own, arrived = lax.optimization_barrier((dot_parts(dense_own, gathered_h), arrived))
     blocks = (own + arrived.astype(F32)).reshape(chips, node_rows, -1)
-    mine = tree_in_order(exchange([mine] * chips, "row", 2, 0), 0).astype(BF16)
+    mine = tree_in_order(exchange([mine] * chips, "row", 2, chips - 1), chips - 1).astype(BF16)
     sent = [blocks[0]] + [block.astype(BF16) for block in blocks[1:]]
     output = tree_in_order(exchange(sent, "row", 2, chips // 2), chips // 2).astype(BF16)
     mine = tree_in_order(exchange([mine] * grid_cols, "col", 1, 0), 0)

time: 60.2 us -> 60.1 us (level)
  transfers between devices with their start and end apart: 28 -> 28, of which waited for: 13 -> 14; matrix products, arithmetic and copies ran while one was open for 9% -> 9% of each run, Pallas kernels for 4% -> 5%
where the time goes in v5:
time: 60.1 us; the launch traced here: 59.8 us
  starting transfers between devices  32.5 us (54%)
  waiting for transfers between devices  15 us (25%)
  Pallas kernels  4.44 us (7%)
  matrix products  4.33 us (7%)
  between operations  1.62 us (3%)
  other arithmetic  1.05 us (2%)
  local copies, waits for them, and re-layouts  0.88 us (1%)
    ppermute x28, starting transfers between devices, swap(): return lax.ppermute(value, axis, [(i, i ^ offset) for i in range(size)])  32.5 us
    ppermute x28, waiting for transfers between devices, swap(): return lax.ppermute(value, axis, [(i, i ^ offset) for i in range(size)])  15 us
    dot_general x6, matrix products, dot_parts(): lax.dot_general(one, other, (((left_dim,), (right_dim,)), ((), ())), pref...  4.33 us
    pallas_call x1, Pallas kernels, assemble(): pl.pallas_call(kernel, out_shape=jax.ShapeDtypeStruct((2, rows // 2, cols...  2.43 us
  transfers between devices with their start and end apart: 28, of which 14 were waited for; matrix products, arithmetic and copies ran while one was open for 9% of the time, Pallas kernels for 5%

profile of v5, /device:TPU:0, one launch (start us, length us, event | category | flops | bytes accessed | tf_op | source)
XLA Modules:
  0.0 59.8 jit_solution(13895114415378150828)
XLA Ops:
  0.6 5.1 %collective-permute-start = (bf16[256,256]{1,0:T(8,128)(2,1)}, bf16[256,256]{1,0:T(8,128)(2,1)S(1)}, u32[]{:S(2)}, u32[]{:S(2)}) collective-permute-start(bf16[256,256]{1,0:T(8,128)(2,1)} %param.7), channel_id=1, source_target_pairs={{0,3},{1,2},{2,1},{3,0},{4,7},{5,6},{6,5},{7,4},{8,11},{9,10},{10,... | collective-permute-start | bytes 393224 | tf_op jit(solution)/shard_map/ppermute | solution.py:226
  6.4 1.6 %collective-permute-start.4 = (bf16[256,128]{1,0:T(8,128)(2,1)}, bf16[256,128]{1,0:T(8,128)(2,1)S(1)}, u32[]{:S(2)}, u32[]{:S(2)}) collective-permute-start(bf16[256,128]{1,0:T(8,128)(2,1)} %param.13), channel_id=1, source_target_pairs={{0,8},{4,12},{8,0},{12,4},{16,24},{20,28},{24,16},{28,20},{1,9},{5... | collective-permute-start | bytes 196616 | tf_op jit(solution)/shard_map/ppermute | solution.py:226
  9.4 2.4 %assemble.1 = bf16[2,1024,1024]{2,1,0:T(8,128)(2,1)S(1)} custom-call(s32[2,128]{1,0:T(2,128)S(1)} %bitcast.37, s32[1]{0:T(128)} %bitcast.34.refs_1_, bf16[128,128,128]{2,1,0:T(8,128)(2,1)} %bitcast.38), custom_call_target="tpu_custom_call" | custom-call | bytes 8388608 | tf_op jit(solution)/shard_map/assemble/pallas_call | solution.py:101
  11.8 1.7 %collective-permute-start.5 = (bf16[512,128]{1,0:T(8,128)(2,1)S(1)}, bf16[512,128]{1,0:T(8,128)(2,1)S(1)}, u32[]{:S(2)}, u32[]{:S(2)}) collective-permute-start(bf16[512,128]{1,0:T(8,128)(2,1)S(1)} %pad_maximum_fusion), channel_id=1, source_target_pairs={{0,16},{4,20},{8,24},{12,28},{16,0},{20,4},{24,8},{28,12},{1,17},{... | collective-permute-start | bytes 393224 | tf_op jit(solution)/shard_map/ppermute | solution.py:226
  13.6 3.4 %collective-permute-done.1 = bf16[256,256]{1,0:T(8,128)(2,1)S(1)} collective-permute-done((bf16[256,256]{1,0:T(8,128)(2,1)}, bf16[256,256]{1,0:T(8,128)(2,1)S(1)}, u32[]{:S(2)}, u32[]{:S(2)}) %collective-permute-start.1) | collective-permute-done | bytes 131104 | tf_op jit(solution)/shard_map/ppermute | solution.py:226
  19.2 1.0 %collective-permute-done.6 = bf16[1024,128]{1,0:T(8,128)(2,1)S(1)} collective-permute-done((bf16[1024,128]{1,0:T(8,128)(2,1)S(1)}, bf16[1024,128]{1,0:T(8,128)(2,1)S(1)}, u32[]{:S(2)}, u32[]{:S(2)}) %collective-permute-start.6) | collective-permute-done | bytes 262176 | tf_op jit(solution)/shard_map/ppermute | solution.py:226
  20.9 0.8 %fusion.7.refs_2_ = f32[1024,128]{1,0:T(8,128)S(1)} fusion(f32[1024,128]{1,0:T(8,128)S(1)} %fusion.4, bf16[1024,128]{1,0:T(8,128)(2,1)S(1)} %constant_dynamic-update-slice_fusion.4, bf16[2,1024,1024]{2,1,0:T(8,128)(2,1)S(1)} %assemble.1), kind=kOutput, calls=%fused_computation.9 | convolution fusion | flops 268566528 | bytes 3407872 | tf_op jit(solution)/shard_map/dot_general | solution.py:26
  21.9 2.5 %collective-permute-start.7 = (bf16[256,256]{1,0:T(8,128)(2,1)S(1)}, bf16[256,256]{1,0:T(8,128)(2,1)S(1)}, u32[]{:S(2)}, u32[]{:S(2)}) collective-permute-start(bf16[256,256]{1,0:T(8,128)(2,1)S(1)} %get-tuple-element.53), channel_id=1, source_target_pairs={{0,24},{4,28},{8,16},{12,20},{16,8},{20,12},{24,0},{28,4},{1,25},{... | collective-permute-start | bytes 393224 | tf_op jit(solution)/shard_map/ppermute | solution.py:226
  25.8 2.4 %collective-permute-start.11 = (bf16[256,128]{1,0:T(8,128)(2,1)S(1)}, bf16[256,128]{1,0:T(8,128)(2,1)S(1)}, u32[]{:S(2)}, u32[]{:S(2)}) collective-permute-start(bf16[256,128]{1,0:T(8,128)(2,1)S(1)} %get-tuple-element.58), channel_id=1, source_target_pairs={{0,3},{1,2},{2,1},{3,0},{4,7},{5,6},{6,5},{7,4},{8,11},{9,10},{10,... | collective-permute-start | bytes 196616 | tf_op jit(solution)/shard_map/ppermute | solution.py:226
  29.1 2.1 %collective-permute-done.8.refs_2_ = bf16[256,256]{1,0:T(8,128)(2,1)S(1)} collective-permute-done((bf16[256,256]{1,0:T(8,128)(2,1)S(1)}, bf16[256,256]{1,0:T(8,128)(2,1)S(1)}, u32[]{:S(2)}, u32[]{:S(2)}) %collective-permute-start.8) | collective-permute-done | bytes 131104 | tf_op jit(solution)/shard_map/ppermute | solution.py:226
  31.9 1.0 %collective-permute-done.10.refs_3_ = bf16[256,128]{1,0:T(8,128)(2,1)S(1)} collective-permute-done((bf16[256,128]{1,0:T(8,128)(2,1)S(1)}, bf16[256,128]{1,0:T(8,128)(2,1)S(1)}, u32[]{:S(2)}, u32[]{:S(2)}) %collective-permute-start.10) | collective-permute-done | bytes 65568 | tf_op jit(solution)/shard_map/ppermute | solution.py:226
  34.2 1.0 %collective-permute-start.14 = (bf16[256,128]{1,0:T(8,128)(2,1)S(1)}, bf16[256,128]{1,0:T(8,128)(2,1)S(1)}, u32[]{:S(2)}, u32[]{:S(2)}) collective-permute-start(bf16[256,128]{1,0:T(8,128)(2,1)S(1)} %get-tuple-element.44), channel_id=1, source_target_pairs={{0,1},{1,0},{2,3},{3,2},{4,5},{5,4},{6,7},{7,6},{8,9},{9,8},{10,11... | collective-permute-start | bytes 196616 | tf_op jit(solution)/shard_map/ppermute | solution.py:226
  35.2 1.9 %collective-permute-start.15 = (bf16[256,128]{1,0:T(8,128)(2,1)S(1)}, bf16[256,128]{1,0:T(8,128)(2,1)S(1)}, u32[]{:S(2)}, u32[]{:S(2)}) collective-permute-start(bf16[256,128]{1,0:T(8,128)(2,1)S(1)} %get-tuple-element.44), channel_id=1, source_target_pairs={{0,2},{1,3},{2,0},{3,1},{4,6},{5,7},{6,4},{7,5},{8,10},{9,11},{10,... | collective-permute-start | bytes 196616 | tf_op jit(solution)/shard_map/ppermute | solution.py:226
  37.2 1.5 %collective-permute-start.16 = (bf16[256,128]{1,0:T(8,128)(2,1)S(1)}, bf16[256,128]{1,0:T(8,128)(2,1)S(1)}, u32[]{:S(2)}, u32[]{:S(2)}) collective-permute-start(bf16[256,128]{1,0:T(8,128)(2,1)S(1)} %get-tuple-element.44), channel_id=1, source_target_pairs={{0,3},{1,2},{2,1},{3,0},{4,7},{5,6},{6,5},{7,4},{8,11},{9,10},{10,... | collective-permute-start | bytes 196616 | tf_op jit(solution)/shard_map/ppermute | solution.py:226
  38.7 2.6 %collective-permute-start.21 = (bf16[128,384]{1,0:T(8,128)(2,1)S(1)}, bf16[128,384]{1,0:T(8,128)(2,1)S(1)}, u32[]{:S(2)}, u32[]{:S(2)}) collective-permute-start(bf16[128,384]{1,0:T(8,128)(2,1)S(1)} %add_convert_fusion.1), channel_id=1, source_target_pairs={{0,24},{4,28},{8,16},{12,20},{16,8},{20,12},{24,0},{28,4},{1,25},{... | collective-permute-start | bytes 294920 | tf_op jit(solution)/shard_map/ppermute | solution.py:226
  42.3 1.4 %collective-permute-done.15 = bf16[256,128]{1,0:T(8,128)(2,1)S(1)} collective-permute-done((bf16[256,128]{1,0:T(8,128)(2,1)S(1)}, bf16[256,128]{1,0:T(8,128)(2,1)S(1)}, u32[]{:S(2)}, u32[]{:S(2)}) %collective-permute-start.15) | collective-permute-done | bytes 65568 | tf_op jit(solution)/shard_map/ppermute | solution.py:226
  45.3 1.1 %collective-permute-done.22 = bf16[128,384]{1,0:T(8,128)(2,1)S(1)} collective-permute-done((bf16[128,384]{1,0:T(8,128)(2,1)S(1)}, bf16[128,384]{1,0:T(8,128)(2,1)S(1)}, u32[]{:S(2)}, u32[]{:S(2)}) %collective-permute-start.22) | collective-permute-done | bytes 98336 | tf_op jit(solution)/shard_map/ppermute | solution.py:226
  46.8 2.9 %collective-permute-start.25 = (bf16[128,384]{1,0:T(8,128)(2,1)S(1)}, bf16[128,384]{1,0:T(8,128)(2,1)S(1)}, u32[]{:S(2)}, u32[]{:S(2)}) collective-permute-start(bf16[128,384]{1,0:T(8,128)(2,1)S(1)} %add_convert_fusion), channel_id=1, source_target_pairs={{0,2},{1,3},{2,0},{3,1},{4,6},{5,7},{6,4},{7,5},{8,10},{9,11},{10,... | collective-permute-start | bytes 294920 | tf_op jit(solution)/shard_map/ppermute | solution.py:226
  49.7 1.4 %collective-permute-start.26 = (bf16[128,384]{1,0:T(8,128)(2,1)S(1)}, bf16[128,384]{1,0:T(8,128)(2,1)S(1)}, u32[]{:S(2)}, u32[]{:S(2)}) collective-permute-start(bf16[128,384]{1,0:T(8,128)(2,1)S(1)} %add_convert_fusion), channel_id=1, source_target_pairs={{0,3},{1,2},{2,1},{3,0},{4,7},{5,6},{6,5},{7,4},{8,11},{9,10},{10,... | collective-permute-start | bytes 294920 | tf_op jit(solution)/shard_map/ppermute | solution.py:226
  51.2 1.5 %collective-permute-start.18 = (bf16[256,128]{1,0:T(8,128)(2,1)S(1)}, bf16[256,128]{1,0:T(8,128)(2,1)S(1)}, u32[]{:S(2)}, u32[]{:S(2)}) collective-permute-start(bf16[256,128]{1,0:T(8,128)(2,1)S(1)} %get-tuple-element.54), channel_id=1, source_target_pairs={{0,16},{4,20},{8,24},{12,28},{16,0},{20,4},{24,8},{28,12},{1,17},{... | collective-permute-start | bytes 196616 | tf_op jit(solution)/shard_map/ppermute | solution.py:226
  52.7 1.3 %collective-permute-start.19 = (bf16[256,128]{1,0:T(8,128)(2,1)S(1)}, bf16[256,128]{1,0:T(8,128)(2,1)S(1)}, u32[]{:S(2)}, u32[]{:S(2)}) collective-permute-start(bf16[256,128]{1,0:T(8,128)(2,1)S(1)} %get-tuple-element.56), channel_id=1, source_target_pairs={{0,24},{4,28},{8,16},{12,20},{16,8},{20,12},{24,0},{28,4},{1,25},{... | collective-permute-start | bytes 196616 | tf_op jit(solution)/shard_map/ppermute | solution.py:226
  53.9 0.8 %collective-permute-start.20 = (bf16[256,128]{1,0:T(8,128)(2,1)S(1)}, bf16[256,128]{1,0:T(8,128)(2,1)S(1)}, u32[]{:S(2)}, u32[]{:S(2)}) collective-permute-start(bf16[256,128]{1,0:T(8,128)(2,1)S(1)} %get-tuple-element.55), channel_id=1, source_target_pairs={{0,8},{4,12},{8,0},{12,4},{16,24},{20,28},{24,16},{28,20},{1,9},{5... | collective-permute-start | bytes 196616 | tf_op jit(solution)/shard_map/ppermute | solution.py:226
  54.7 2.7 %collective-permute-done.25 = bf16[128,384]{1,0:T(8,128)(2,1)S(1)} collective-permute-done((bf16[128,384]{1,0:T(8,128)(2,1)S(1)}, bf16[128,384]{1,0:T(8,128)(2,1)S(1)}, u32[]{:S(2)}, u32[]{:S(2)}) %collective-permute-start.25) | collective-permute-done | bytes 98336 | tf_op jit(solution)/shard_map/ppermute | solution.py:226
  59.0 0.8 %join_grads.1 = (f32[256,256]{1,0:T(8,128)}, f32[256,128]{1,0:T(8,128)}) custom-call(f32[128,384]{1,0:T(8,128)S(1)} %add_add_fusion.mine_ref, f32[128,384]{1,0:T(8,128)S(1)} %collective-permute-done.27.theirs_ref), custom_call_target="tpu_custom_call" | custom-call | tf_op jit(solution)/shard_map/join_grads/pallas_call | solution.py:177
  (75 shorter events, 13.1 us)
Async XLA Ops:
  0.6 12.9 %collective-permute-start = (bf16[256,256]{1,0:T(8,128)(2,1)}, bf16[256,256]{1,0:T(8,128)(2,1)S(1)}, u32[]{:S(2)}, u32[]{:S(2)}) collective-permute-start(bf16[256,256]{1,0:T(8,128)(2,1)} %param.7), channel_id=1, source_target_pairs={{0,3},{1,2},{2,1},{3,0},{4,7},{5,6},{6,5},{7,4},{8,11},{9,10},{10,... | collective-permute-start | bytes 393224 | tf_op jit(solution)/shard_map/ppermute | solution.py:226
  5.7 11.3 %collective-permute-start.1 = (bf16[256,256]{1,0:T(8,128)(2,1)}, bf16[256,256]{1,0:T(8,128)(2,1)S(1)}, u32[]{:S(2)}, u32[]{:S(2)}) collective-permute-start(bf16[256,256]{1,0:T(8,128)(2,1)} %param.7), channel_id=1, source_target_pairs={{0,2},{1,3},{2,0},{3,1},{4,6},{5,7},{6,4},{7,5},{8,10},{9,11},{10,... | collective-permute-start | bytes 393224 | tf_op jit(solution)/shard_map/ppermute | solution.py:226
  5.7 11.3 %collective-permute-start.2 = (bf16[256,256]{1,0:T(8,128)(2,1)}, bf16[256,256]{1,0:T(8,128)(2,1)S(1)}, u32[]{:S(2)}, u32[]{:S(2)}) collective-permute-start(bf16[256,256]{1,0:T(8,128)(2,1)} %param.7), channel_id=1, source_target_pairs={{0,1},{1,0},{2,3},{3,2},{4,5},{5,4},{6,7},{7,6},{8,9},{9,8},{10,11... | collective-permute-start | bytes 393224 | tf_op jit(solution)/shard_map/ppermute | solution.py:226
  6.4 5.4 %collective-permute-start.4 = (bf16[256,128]{1,0:T(8,128)(2,1)}, bf16[256,128]{1,0:T(8,128)(2,1)S(1)}, u32[]{:S(2)}, u32[]{:S(2)}) collective-permute-start(bf16[256,128]{1,0:T(8,128)(2,1)} %param.13), channel_id=1, source_target_pairs={{0,8},{4,12},{8,0},{12,4},{16,24},{20,28},{24,16},{28,20},{1,9},{5... | collective-permute-start | bytes 196616 | tf_op jit(solution)/shard_map/ppermute | solution.py:226
  11.8 6.0 %collective-permute-start.5 = (bf16[512,128]{1,0:T(8,128)(2,1)S(1)}, bf16[512,128]{1,0:T(8,128)(2,1)S(1)}, u32[]{:S(2)}, u32[]{:S(2)}) collective-permute-start(bf16[512,128]{1,0:T(8,128)(2,1)S(1)} %pad_maximum_fusion), channel_id=1, source_target_pairs={{0,16},{4,20},{8,24},{12,28},{16,0},{20,4},{24,8},{28,12},{1,17},{... | collective-permute-start | bytes 393224 | tf_op jit(solution)/shard_map/ppermute | solution.py:226
  21.9 6.8 %collective-permute-start.7 = (bf16[256,256]{1,0:T(8,128)(2,1)S(1)}, bf16[256,256]{1,0:T(8,128)(2,1)S(1)}, u32[]{:S(2)}, u32[]{:S(2)}) collective-permute-start(bf16[256,256]{1,0:T(8,128)(2,1)S(1)} %get-tuple-element.53), channel_id=1, source_target_pairs={{0,24},{4,28},{8,16},{12,20},{16,8},{20,12},{24,0},{28,4},{1,25},{... | collective-permute-start | bytes 393224 | tf_op jit(solution)/shard_map/ppermute | solution.py:226
  24.4 6.8 %collective-permute-start.8 = (bf16[256,256]{1,0:T(8,128)(2,1)S(1)}, bf16[256,256]{1,0:T(8,128)(2,1)S(1)}, u32[]{:S(2)}, u32[]{:S(2)}) collective-permute-start(bf16[256,256]{1,0:T(8,128)(2,1)S(1)} %get-tuple-element.52), channel_id=1, source_target_pairs={{0,16},{4,20},{8,24},{12,28},{16,0},{20,4},{24,8},{28,12},{1,17},{... | collective-permute-start | bytes 393224 | tf_op jit(solution)/shard_map/ppermute | solution.py:226
  24.9 6.4 %collective-permute-start.9 = (bf16[256,256]{1,0:T(8,128)(2,1)S(1)}, bf16[256,256]{1,0:T(8,128)(2,1)S(1)}, u32[]{:S(2)}, u32[]{:S(2)}) collective-permute-start(bf16[256,256]{1,0:T(8,128)(2,1)S(1)} %get-tuple-element.51), channel_id=1, source_target_pairs={{0,8},{4,12},{8,0},{12,4},{16,24},{20,28},{24,16},{28,20},{1,9},{5... | collective-permute-start | bytes 393224 | tf_op jit(solution)/shard_map/ppermute | solution.py:226
  25.5 7.4 %collective-permute-start.10 = (bf16[256,128]{1,0:T(8,128)(2,1)S(1)}, bf16[256,128]{1,0:T(8,128)(2,1)S(1)}, u32[]{:S(2)}, u32[]{:S(2)}) collective-permute-start(bf16[256,128]{1,0:T(8,128)(2,1)S(1)} %get-tuple-element.59), channel_id=1, source_target_pairs={{0,2},{1,3},{2,0},{3,1},{4,6},{5,7},{6,4},{7,5},{8,10},{9,11},{10,... | collective-permute-start | bytes 196616 | tf_op jit(solution)/shard_map/ppermute | solution.py:226
  25.8 7.1 %collective-permute-start.11 = (bf16[256,128]{1,0:T(8,128)(2,1)S(1)}, bf16[256,128]{1,0:T(8,128)(2,1)S(1)}, u32[]{:S(2)}, u32[]{:S(2)}) collective-permute-start(bf16[256,128]{1,0:T(8,128)(2,1)S(1)} %get-tuple-element.58), channel_id=1, source_target_pairs={{0,3},{1,2},{2,1},{3,0},{4,7},{5,6},{6,5},{7,4},{8,11},{9,10},{10,... | collective-permute-start | bytes 196616 | tf_op jit(solution)/shard_map/ppermute | solution.py:226
  28.7 4.8 %collective-permute-start.12 = (bf16[256,128]{1,0:T(8,128)(2,1)S(1)}, bf16[256,128]{1,0:T(8,128)(2,1)S(1)}, u32[]{:S(2)}, u32[]{:S(2)}) collective-permute-start(bf16[256,128]{1,0:T(8,128)(2,1)S(1)} %get-tuple-element.57), channel_id=1, source_target_pairs={{0,1},{1,0},{2,3},{3,2},{4,5},{5,4},{6,7},{7,6},{8,9},{9,8},{10,11... | collective-permute-start | bytes 196616 | tf_op jit(solution)/shard_map/ppermute | solution.py:226
  34.2 4.5 %collective-permute-start.13 = (bf16[128,384]{1,0:T(8,128)(2,1)S(1)}, bf16[128,384]{1,0:T(8,128)(2,1)S(1)}, u32[]{:S(2)}, u32[]{:S(2)}) collective-permute-start(bf16[128,384]{1,0:T(8,128)(2,1)S(1)} %get-tuple-element.35), channel_id=1, source_target_pairs={{0,4},{4,0},{8,12},{12,8},{16,20},{20,16},{24,28},{28,24},{1,5},{5... | collective-permute-start | bytes 294920 | tf_op jit(solution)/shard_map/ppermute | solution.py:226
  34.2 7.6 %collective-permute-start.14 = (bf16[256,128]{1,0:T(8,128)(2,1)S(1)}, bf16[256,128]{1,0:T(8,128)(2,1)S(1)}, u32[]{:S(2)}, u32[]{:S(2)}) collective-permute-start(bf16[256,128]{1,0:T(8,128)(2,1)S(1)} %get-tuple-element.44), channel_id=1, source_target_pairs={{0,1},{1,0},{2,3},{3,2},{4,5},{5,4},{6,7},{7,6},{8,9},{9,8},{10,11... | collective-permute-start | bytes 196616 | tf_op jit(solution)/shard_map/ppermute | solution.py:226
  35.2 8.5 %collective-permute-start.15 = (bf16[256,128]{1,0:T(8,128)(2,1)S(1)}, bf16[256,128]{1,0:T(8,128)(2,1)S(1)}, u32[]{:S(2)}, u32[]{:S(2)}) collective-permute-start(bf16[256,128]{1,0:T(8,128)(2,1)S(1)} %get-tuple-element.44), channel_id=1, source_target_pairs={{0,2},{1,3},{2,0},{3,1},{4,6},{5,7},{6,4},{7,5},{8,10},{9,11},{10,... | collective-permute-start | bytes 196616 | tf_op jit(solution)/shard_map/ppermute | solution.py:226
  37.2 6.6 %collective-permute-start.16 = (bf16[256,128]{1,0:T(8,128)(2,1)S(1)}, bf16[256,128]{1,0:T(8,128)(2,1)S(1)}, u32[]{:S(2)}, u32[]{:S(2)}) collective-permute-start(bf16[256,128]{1,0:T(8,128)(2,1)S(1)} %get-tuple-element.44), channel_id=1, source_target_pairs={{0,3},{1,2},{2,1},{3,0},{4,7},{5,6},{6,5},{7,4},{8,11},{9,10},{10,... | collective-permute-start | bytes 196616 | tf_op jit(solution)/shard_map/ppermute | solution.py:226
  38.7 6.6 %collective-permute-start.21 = (bf16[128,384]{1,0:T(8,128)(2,1)S(1)}, bf16[128,384]{1,0:T(8,128)(2,1)S(1)}, u32[]{:S(2)}, u32[]{:S(2)}) collective-permute-start(bf16[128,384]{1,0:T(8,128)(2,1)S(1)} %add_convert_fusion.1), channel_id=1, source_target_pairs={{0,24},{4,28},{8,16},{12,20},{16,8},{20,12},{24,0},{28,4},{1,25},{... | collective-permute-start | bytes 294920 | tf_op jit(solution)/shard_map/ppermute | solution.py:226
  41.3 5.1 %collective-permute-start.22 = (bf16[128,384]{1,0:T(8,128)(2,1)S(1)}, bf16[128,384]{1,0:T(8,128)(2,1)S(1)}, u32[]{:S(2)}, u32[]{:S(2)}) collective-permute-start(bf16[128,384]{1,0:T(8,128)(2,1)S(1)} %add_convert_fusion.1), channel_id=1, source_target_pairs={{0,16},{4,20},{8,24},{12,28},{16,0},{20,4},{24,8},{28,12},{1,17},{... | collective-permute-start | bytes 294920 | tf_op jit(solution)/shard_map/ppermute | solution.py:226
  41.8 4.7 %collective-permute-start.23 = (bf16[128,384]{1,0:T(8,128)(2,1)S(1)}, bf16[128,384]{1,0:T(8,128)(2,1)S(1)}, u32[]{:S(2)}, u32[]{:S(2)}) collective-permute-start(bf16[128,384]{1,0:T(8,128)(2,1)S(1)} %add_convert_fusion.1), channel_id=1, source_target_pairs={{0,8},{4,12},{8,0},{12,4},{16,24},{20,28},{24,16},{28,20},{1,9},{5... | collective-permute-start | bytes 294920 | tf_op jit(solution)/shard_map/ppermute | solution.py:226
  44.5 6.6 %collective-permute-start.17 = (bf16[1024,128]{1,0:T(8,128)(2,1)S(1)}, bf16[1024,128]{1,0:T(8,128)(2,1)S(1)}, u32[]{:S(2)}, u32[]{:S(2)}) collective-permute-start(bf16[1024,128]{1,0:T(8,128)(2,1)S(1)} %fusion.8), channel_id=1, source_target_pairs={{0,4},{4,0},{8,12},{12,8},{16,20},{20,16},{24,28},{28,24},{1,5},{5... | collective-permute-start | bytes 786440 | tf_op jit(solution)/shard_map/ppermute | solution.py:226
  46.6 7.3 %collective-permute-start.24 = (bf16[128,384]{1,0:T(8,128)(2,1)S(1)}, bf16[128,384]{1,0:T(8,128)(2,1)S(1)}, u32[]{:S(2)}, u32[]{:S(2)}) collective-permute-start(bf16[128,384]{1,0:T(8,128)(2,1)S(1)} %add_convert_fusion), channel_id=1, source_target_pairs={{0,1},{1,0},{2,3},{3,2},{4,5},{5,4},{6,7},{7,6},{8,9},{9,8},{10,11... | collective-permute-start | bytes 294920 | tf_op jit(solution)/shard_map/ppermute | solution.py:226
  46.8 10.6 %collective-permute-start.25 = (bf16[128,384]{1,0:T(8,128)(2,1)S(1)}, bf16[128,384]{1,0:T(8,128)(2,1)S(1)}, u32[]{:S(2)}, u32[]{:S(2)}) collective-permute-start(bf16[128,384]{1,0:T(8,128)(2,1)S(1)} %add_convert_fusion), channel_id=1, source_target_pairs={{0,2},{1,3},{2,0},{3,1},{4,6},{5,7},{6,4},{7,5},{8,10},{9,11},{10,... | collective-permute-start | bytes 294920 | tf_op jit(solution)/shard_map/ppermute | solution.py:226
  49.7 7.8 %collective-permute-start.26 = (bf16[128,384]{1,0:T(8,128)(2,1)S(1)}, bf16[128,384]{1,0:T(8,128)(2,1)S(1)}, u32[]{:S(2)}, u32[]{:S(2)}) collective-permute-start(bf16[128,384]{1,0:T(8,128)(2,1)S(1)} %add_convert_fusion), channel_id=1, source_target_pairs={{0,3},{1,2},{2,1},{3,0},{4,7},{5,6},{6,5},{7,4},{8,11},{9,10},{10,... | collective-permute-start | bytes 294920 | tf_op jit(solution)/shard_map/ppermute | solution.py:226
  51.2 6.4 %collective-permute-start.18 = (bf16[256,128]{1,0:T(8,128)(2,1)S(1)}, bf16[256,128]{1,0:T(8,128)(2,1)S(1)}, u32[]{:S(2)}, u32[]{:S(2)}) collective-permute-start(bf16[256,128]{1,0:T(8,128)(2,1)S(1)} %get-tuple-element.54), channel_id=1, source_target_pairs={{0,16},{4,20},{8,24},{12,28},{16,0},{20,4},{24,8},{28,12},{1,17},{... | collective-permute-start | bytes 196616 | tf_op jit(solution)/shard_map/ppermute | solution.py:226
  52.7 5.2 %collective-permute-start.19 = (bf16[256,128]{1,0:T(8,128)(2,1)S(1)}, bf16[256,128]{1,0:T(8,128)(2,1)S(1)}, u32[]{:S(2)}, u32[]{:S(2)}) collective-permute-start(bf16[256,128]{1,0:T(8,128)(2,1)S(1)} %get-tuple-element.56), channel_id=1, source_target_pairs={{0,24},{4,28},{8,16},{12,20},{16,8},{20,12},{24,0},{28,4},{1,25},{... | collective-permute-start | bytes 196616 | tf_op jit(solution)/shard_map/ppermute | solution.py:226
  (9 other events, 43.5 us)

commit v6 on v5

--- a/solution.py
+++ b/solution.py
@@ -117,18 +117,14 @@
 
 
 def local_grads_kernel(scale, grid_cols, *refs):
-    mean_ref, pre_ref, back_ref = refs[:3]
-    arrived_refs = refs[3 : 2 + grid_cols]
-    weight_ref, mine_ref, theirs_ref = refs[2 + grid_cols :]
-    own = pl.ds((grid_cols - 1) * mean_ref.shape[0], mean_ref.shape[0])
+    mean_ref, act_ref, slope_ref, back_ref = refs[:4]
+    arrived_refs = refs[4 : 3 + grid_cols]
+    weight_ref, mine_ref, theirs_ref = refs[3 + grid_cols :]
+    own = pl.ds((grid_cols - 1) * slope_ref.shape[0], slope_ref.shape[0])
     back_sum = tree_sum([back_ref[own, :]] + [ref[...] for ref in arrived_refs])
     hidden_grad = dot_parts(back_sum, weight_ref[...], 1, 1)
-    first_pre = pre_ref[...]
-    sigma = jax.nn.sigmoid(first_pre)
-    hidden_act = (first_pre * sigma).astype(BF16)
-    pre_grad = hidden_grad * (sigma * (1.0 + first_pre * (1.0 - sigma)))
-    first = dot_parts(mean_ref[...], pre_grad, 0, 0) * scale
-    second = dot_parts(hidden_act, back_sum, 0, 0) * scale
+    first = dot_parts(mean_ref[...], hidden_grad * slope_ref[...]) * scale
+    second = dot_parts(act_ref[...], back_sum) * scale
     half, width = mine_ref.shape[0], first.shape[1]
     low_core = lax.axis_index("row") % 2 == 0
     for value, place in ((first, slice(0, width)), (second, slice(width, None))):
@@ -137,10 +133,10 @@
         theirs_ref[:, place] = jnp.where(low_core, high, low).astype(BF16)
 
 
-def local_grads(mean, pre, back, arrived, weight, scale):
+def local_grads(mean, act, slope, back, arrived, weight, scale):
     grid_cols = len(arrived) + 1
-    half = mean.shape[1] // 2
-    width = pre.shape[1] + weight.shape[1]
+    half = mean.shape[0] // 2
+    width = slope.shape[1] + weight.shape[1]
 
     def kernel(*refs):
         local_grads_kernel(scale, grid_cols, *refs)
@@ -152,14 +148,14 @@
             jax.ShapeDtypeStruct((half, width), F32),
             jax.ShapeDtypeStruct((half, width), BF16),
         ),
-        in_specs=[vmem] * (4 + len(arrived)),
+        in_specs=[vmem] * (5 + len(arrived)),
         out_specs=(vmem, vmem),
         compiler_params=pltpu.CompilerParams(vmem_limit_bytes=6 << 20),
         cost_estimate=pl.CostEstimate(
             flops=2 * 256 * 256 * 384 * 3, bytes_accessed=1 << 20, transcendentals=1 << 16
         ),
         name="local_grads",
-    )(mean, pre, back, *arrived, weight)
+    )(mean, act, slope, back, *arrived, weight)
 
 
 def join_kernel(mine_ref, theirs_ref, first_ref, second_ref):
@@ -189,14 +185,17 @@
 
 def activate_kernel(chips, flip, *refs):
     blocks_ref, arrived_refs = refs[0], refs[1:chips]
-    first_ref, second_ref, mean_ref, pre_ref, projected_ref = refs[chips:]
+    first_ref, second_ref, mean_ref, act_ref, slope_ref, projected_ref = refs[chips:]
     parts = [ref[...] for ref in arrived_refs]
     parts.insert(flip, blocks_ref[0])
     mean = tree_sum(parts)
     pre = dot_parts(mean, first_ref[...])
-    mean_ref[...] = mean
-    pre_ref[...] = pre
-    projected_ref[...] = dot_parts(pre * jax.nn.sigmoid(pre), second_ref[...]).astype(BF16)
+    sigma = jax.nn.sigmoid(pre)
+    act = pre * sigma
+    projected_ref[...] = dot_parts(act, second_ref[...]).astype(BF16)
+    mean_ref[...] = mean.T
+    act_ref[...] = act.T.astype(BF16)
+    slope_ref[...] = sigma * (1.0 + pre * (1.0 - sigma))
 
 
 def activate(blocks, parts, flip, first_weight, second_weight):
@@ -210,12 +209,13 @@
     return pl.pallas_call(
         kernel,
         out_shape=(
-            jax.ShapeDtypeStruct((rows, first_weight.shape[0]), F32),
+            jax.ShapeDtypeStruct((first_weight.shape[0], rows), F32),
+            jax.ShapeDtypeStruct((first_weight.shape[1], rows), BF16),
             jax.ShapeDtypeStruct((rows, first_weight.shape[1]), F32),
             jax.ShapeDtypeStruct((rows, second_weight.shape[1]), BF16),
         ),
         in_specs=[vmem] * (chips + 2),
-        out_specs=(vmem, vmem, vmem),
+        out_specs=(vmem, vmem, vmem, vmem),
         compiler_params=pltpu.CompilerParams(vmem_limit_bytes=6 << 20),
         name="activate",
     )(blocks, *arrived, first_weight, second_weight)
@@ -284,15 +284,14 @@
     first_parts = exchange(first_sent, "row", 2, chips - 1)
     back_arrived = in_order(exchange(back_sent, "col", 1, grid_cols // 2), grid_cols // 2)
     back_arrived.pop(grid_cols // 2)
-    first_mean, first_pre, projected = activate(
+    mean, act, slope, projected = activate(
         first_blocks, in_order(first_parts, chips - 1), chips - 1, first_weight, second_weight
     )
-    projected, first_pre = lax.optimization_barrier((projected, first_pre))
     parts_h = exchange([projected] * grid_cols, "col", 1, grid_cols // 2)
 
     scale = 1.0 / math.sqrt(node_rows * grid_rows * grid_cols)
     mine, theirs = local_grads(
-        first_mean, first_pre, back_part, back_arrived, second_weight, scale
+        mean, act, slope, back_part, back_arrived, second_weight, scale
     )
     mine = (mine + swap(theirs, "row", 1).astype(F32)).astype(BF16)
     _, *parts_h = lax.optimization_barrier((mine, *parts_h))
@@ -304,7 +303,7 @@
     blocks = (own + arrived.astype(F32)).reshape(chips, node_rows, -1)
     mine = tree_in_order(exchange([mine] * chips, "row", 2, chips - 1), chips - 1).astype(BF16)
     sent = [blocks[0]] + [block.astype(BF16) for block in blocks[1:]]
-    output = tree_in_order(exchange(sent, "row", 2, chips // 2), chips // 2).astype(BF16)
+    output = tree_in_order(exchange(sent, "row", 2, chips - 1), chips - 1).astype(BF16)
     mine = tree_in_order(exchange([mine] * grid_cols, "col", 1, 0), 0)
     first_grad, second_grad = join(mine, swap(mine, "row", 1), first_weight.shape[1])
     return (output, first_grad, second_grad)

time: 60.1 us -> 60.1 us (level)
  transfers between devices with their start and end apart: 28 -> 28, of which waited for: 14 -> 13; matrix products, arithmetic and copies ran while one was open for 9% -> 9% of each run, Pallas kernels for 5% -> 5%
where the time goes in v6:
time: 60.1 us; the launch traced here: 59.8 us
  starting transfers between devices  32.5 us (54%)
  waiting for transfers between devices  15.1 us (25%)
  matrix products  4.33 us (7%)
  Pallas kernels  4.21 us (7%)
  between operations  1.62 us (3%)
  other arithmetic  1.05 us (2%)
  local copies, waits for them, and re-layouts  0.88 us (1%)
    ppermute x28, starting transfers between devices, swap(): return lax.ppermute(value, axis, [(i, i ^ offset) for i in range(size)])  32.5 us
    ppermute x28, waiting for transfers between devices, swap(): return lax.ppermute(value, axis, [(i, i ^ offset) for i in range(size)])  15.1 us
    dot_general x6, matrix products, dot_parts(): lax.dot_general(one, other, (((left_dim,), (right_dim,)), ((), ())), pref...  4.33 us
    pallas_call x1, Pallas kernels, assemble(): pl.pallas_call(kernel, out_shape=jax.ShapeDtypeStruct((2, rows // 2, cols...  2.22 us
  transfers between devices with their start and end apart: 28, of which 13 were waited for; matrix products, arithmetic and copies ran while one was open for 9% of the time, Pallas kernels for 5%

profile of v6, /device:TPU:0, one launch (start us, length us, event | category | flops | bytes accessed | tf_op | source)
XLA Modules:
  0.0 59.8 jit_solution(17688898659276818845)
XLA Ops:
  0.6 5.1 %collective-permute-start = (bf16[256,256]{1,0:T(8,128)(2,1)}, bf16[256,256]{1,0:T(8,128)(2,1)S(1)}, u32[]{:S(2)}, u32[]{:S(2)}) collective-permute-start(bf16[256,256]{1,0:T(8,128)(2,1)} %param.7), channel_id=1, source_target_pairs={{0,3},{1,2},{2,1},{3,0},{4,7},{5,6},{6,5},{7,4},{8,11},{9,10},{10,... | collective-permute-start | bytes 393224 | tf_op jit(solution)/shard_map/ppermute | solution.py:226
  6.4 1.6 %collective-permute-start.4 = (bf16[256,128]{1,0:T(8,128)(2,1)}, bf16[256,128]{1,0:T(8,128)(2,1)S(1)}, u32[]{:S(2)}, u32[]{:S(2)}) collective-permute-start(bf16[256,128]{1,0:T(8,128)(2,1)} %param.13), channel_id=1, source_target_pairs={{0,8},{4,12},{8,0},{12,4},{16,24},{20,28},{24,16},{28,20},{1,9},{5... | collective-permute-start | bytes 196616 | tf_op jit(solution)/shard_map/ppermute | solution.py:226
  9.4 2.2 %assemble.1 = bf16[2,1024,1024]{2,1,0:T(8,128)(2,1)S(1)} custom-call(s32[2,128]{1,0:T(2,128)S(1)} %bitcast.37, s32[1]{0:T(128)} %bitcast.34.refs_1_, bf16[128,128,128]{2,1,0:T(8,128)(2,1)} %bitcast.38), custom_call_target="tpu_custom_call" | custom-call | bytes 8388608 | tf_op jit(solution)/shard_map/assemble/pallas_call | solution.py:101
  11.6 1.5 %collective-permute-start.5 = (bf16[512,128]{1,0:T(8,128)(2,1)S(1)}, bf16[512,128]{1,0:T(8,128)(2,1)S(1)}, u32[]{:S(2)}, u32[]{:S(2)}) collective-permute-start(bf16[512,128]{1,0:T(8,128)(2,1)S(1)} %pad_maximum_fusion), channel_id=1, source_target_pairs={{0,16},{4,20},{8,24},{12,28},{16,0},{20,4},{24,8},{28,12},{1,17},{... | collective-permute-start | bytes 393224 | tf_op jit(solution)/shard_map/ppermute | solution.py:226
  13.2 3.8 %collective-permute-done.1 = bf16[256,256]{1,0:T(8,128)(2,1)S(1)} collective-permute-done((bf16[256,256]{1,0:T(8,128)(2,1)}, bf16[256,256]{1,0:T(8,128)(2,1)S(1)}, u32[]{:S(2)}, u32[]{:S(2)}) %collective-permute-start.1) | collective-permute-done | bytes 131104 | tf_op jit(solution)/shard_map/ppermute | solution.py:226
  19.2 1.0 %collective-permute-done.6 = bf16[1024,128]{1,0:T(8,128)(2,1)S(1)} collective-permute-done((bf16[1024,128]{1,0:T(8,128)(2,1)S(1)}, bf16[1024,128]{1,0:T(8,128)(2,1)S(1)}, u32[]{:S(2)}, u32[]{:S(2)}) %collective-permute-start.6) | collective-permute-done | bytes 262176 | tf_op jit(solution)/shard_map/ppermute | solution.py:226
  20.9 0.8 %fusion.7.refs_3_ = f32[1024,128]{1,0:T(8,128)S(1)} fusion(f32[1024,128]{1,0:T(8,128)S(1)} %fusion.4, bf16[1024,128]{1,0:T(8,128)(2,1)S(1)} %constant_dynamic-update-slice_fusion.4, bf16[2,1024,1024]{2,1,0:T(8,128)(2,1)S(1)} %assemble.1), kind=kOutput, calls=%fused_computation.9 | convolution fusion | flops 268566528 | bytes 3407872 | tf_op jit(solution)/shard_map/dot_general | solution.py:26
  21.9 2.5 %collective-permute-start.7 = (bf16[256,256]{1,0:T(8,128)(2,1)S(1)}, bf16[256,256]{1,0:T(8,128)(2,1)S(1)}, u32[]{:S(2)}, u32[]{:S(2)}) collective-permute-start(bf16[256,256]{1,0:T(8,128)(2,1)S(1)} %get-tuple-element.51), channel_id=1, source_target_pairs={{0,24},{4,28},{8,16},{12,20},{16,8},{20,12},{24,0},{28,4},{1,25},{... | collective-permute-start | bytes 393224 | tf_op jit(solution)/shard_map/ppermute | solution.py:226
  26.2 2.0 %collective-permute-start.11 = (bf16[256,128]{1,0:T(8,128)(2,1)S(1)}, bf16[256,128]{1,0:T(8,128)(2,1)S(1)}, u32[]{:S(2)}, u32[]{:S(2)}) collective-permute-start(bf16[256,128]{1,0:T(8,128)(2,1)S(1)} %get-tuple-element.56), channel_id=1, source_target_pairs={{0,3},{1,2},{2,1},{3,0},{4,7},{5,6},{6,5},{7,4},{8,11},{9,10},{10,... | collective-permute-start | bytes 196616 | tf_op jit(solution)/shard_map/ppermute | solution.py:226
  29.3 1.9 %collective-permute-done.8.refs_2_ = bf16[256,256]{1,0:T(8,128)(2,1)S(1)} collective-permute-done((bf16[256,256]{1,0:T(8,128)(2,1)S(1)}, bf16[256,256]{1,0:T(8,128)(2,1)S(1)}, u32[]{:S(2)}, u32[]{:S(2)}) %collective-permute-start.8) | collective-permute-done | bytes 131104 | tf_op jit(solution)/shard_map/ppermute | solution.py:226
  31.9 1.2 %collective-permute-done.10.refs_4_ = bf16[256,128]{1,0:T(8,128)(2,1)S(1)} collective-permute-done((bf16[256,128]{1,0:T(8,128)(2,1)S(1)}, bf16[256,128]{1,0:T(8,128)(2,1)S(1)}, u32[]{:S(2)}, u32[]{:S(2)}) %collective-permute-start.10) | collective-permute-done | bytes 65568 | tf_op jit(solution)/shard_map/ppermute | solution.py:226
  34.3 0.9 %collective-permute-start.14 = (bf16[256,128]{1,0:T(8,128)(2,1)S(1)}, bf16[256,128]{1,0:T(8,128)(2,1)S(1)}, u32[]{:S(2)}, u32[]{:S(2)}) collective-permute-start(bf16[256,128]{1,0:T(8,128)(2,1)S(1)} %get-tuple-element.42), channel_id=1, source_target_pairs={{0,1},{1,0},{2,3},{3,2},{4,5},{5,4},{6,7},{7,6},{8,9},{9,8},{10,11... | collective-permute-start | bytes 196616 | tf_op jit(solution)/shard_map/ppermute | solution.py:226
  35.2 2.0 %collective-permute-start.15 = (bf16[256,128]{1,0:T(8,128)(2,1)S(1)}, bf16[256,128]{1,0:T(8,128)(2,1)S(1)}, u32[]{:S(2)}, u32[]{:S(2)}) collective-permute-start(bf16[256,128]{1,0:T(8,128)(2,1)S(1)} %get-tuple-element.42), channel_id=1, source_target_pairs={{0,2},{1,3},{2,0},{3,1},{4,6},{5,7},{6,4},{7,5},{8,10},{9,11},{10,... | collective-permute-start | bytes 196616 | tf_op jit(solution)/shard_map/ppermute | solution.py:226
  37.2 1.6 %collective-permute-start.16 = (bf16[256,128]{1,0:T(8,128)(2,1)S(1)}, bf16[256,128]{1,0:T(8,128)(2,1)S(1)}, u32[]{:S(2)}, u32[]{:S(2)}) collective-permute-start(bf16[256,128]{1,0:T(8,128)(2,1)S(1)} %get-tuple-element.42), channel_id=1, source_target_pairs={{0,3},{1,2},{2,1},{3,0},{4,7},{5,6},{6,5},{7,4},{8,11},{9,10},{10,... | collective-permute-start | bytes 196616 | tf_op jit(solution)/shard_map/ppermute | solution.py:226
  38.8 2.5 %collective-permute-start.21 = (bf16[128,384]{1,0:T(8,128)(2,1)S(1)}, bf16[128,384]{1,0:T(8,128)(2,1)S(1)}, u32[]{:S(2)}, u32[]{:S(2)}) collective-permute-start(bf16[128,384]{1,0:T(8,128)(2,1)S(1)} %add_convert_fusion.1), channel_id=1, source_target_pairs={{0,24},{4,28},{8,16},{12,20},{16,8},{20,12},{24,0},{28,4},{1,25},{... | collective-permute-start | bytes 294920 | tf_op jit(solution)/shard_map/ppermute | solution.py:226
  42.4 1.4 %collective-permute-done.15 = bf16[256,128]{1,0:T(8,128)(2,1)S(1)} collective-permute-done((bf16[256,128]{1,0:T(8,128)(2,1)S(1)}, bf16[256,128]{1,0:T(8,128)(2,1)S(1)}, u32[]{:S(2)}, u32[]{:S(2)}) %collective-permute-start.15) | collective-permute-done | bytes 65568 | tf_op jit(solution)/shard_map/ppermute | solution.py:226
  45.4 1.0 %collective-permute-done.22 = bf16[128,384]{1,0:T(8,128)(2,1)S(1)} collective-permute-done((bf16[128,384]{1,0:T(8,128)(2,1)S(1)}, bf16[128,384]{1,0:T(8,128)(2,1)S(1)}, u32[]{:S(2)}, u32[]{:S(2)}) %collective-permute-start.22) | collective-permute-done | bytes 98336 | tf_op jit(solution)/shard_map/ppermute | solution.py:226
  46.8 2.8 %collective-permute-start.25 = (bf16[128,384]{1,0:T(8,128)(2,1)S(1)}, bf16[128,384]{1,0:T(8,128)(2,1)S(1)}, u32[]{:S(2)}, u32[]{:S(2)}) collective-permute-start(bf16[128,384]{1,0:T(8,128)(2,1)S(1)} %add_convert_fusion), channel_id=1, source_target_pairs={{0,2},{1,3},{2,0},{3,1},{4,6},{5,7},{6,4},{7,5},{8,10},{9,11},{10,... | collective-permute-start | bytes 294920 | tf_op jit(solution)/shard_map/ppermute | solution.py:226
  49.6 1.5 %collective-permute-start.26 = (bf16[128,384]{1,0:T(8,128)(2,1)S(1)}, bf16[128,384]{1,0:T(8,128)(2,1)S(1)}, u32[]{:S(2)}, u32[]{:S(2)}) collective-permute-start(bf16[128,384]{1,0:T(8,128)(2,1)S(1)} %add_convert_fusion), channel_id=1, source_target_pairs={{0,3},{1,2},{2,1},{3,0},{4,7},{5,6},{6,5},{7,4},{8,11},{9,10},{10,... | collective-permute-start | bytes 294920 | tf_op jit(solution)/shard_map/ppermute | solution.py:226
  51.2 1.5 %collective-permute-start.18 = (bf16[256,128]{1,0:T(8,128)(2,1)S(1)}, bf16[256,128]{1,0:T(8,128)(2,1)S(1)}, u32[]{:S(2)}, u32[]{:S(2)}) collective-permute-start(bf16[256,128]{1,0:T(8,128)(2,1)S(1)} %get-tuple-element.52), channel_id=1, source_target_pairs={{0,24},{4,28},{8,16},{12,20},{16,8},{20,12},{24,0},{28,4},{1,25},{... | collective-permute-start | bytes 196616 | tf_op jit(solution)/shard_map/ppermute | solution.py:226
  52.7 1.2 %collective-permute-start.19 = (bf16[256,128]{1,0:T(8,128)(2,1)S(1)}, bf16[256,128]{1,0:T(8,128)(2,1)S(1)}, u32[]{:S(2)}, u32[]{:S(2)}) collective-permute-start(bf16[256,128]{1,0:T(8,128)(2,1)S(1)} %get-tuple-element.54), channel_id=1, source_target_pairs={{0,16},{4,20},{8,24},{12,28},{16,0},{20,4},{24,8},{28,12},{1,17},{... | collective-permute-start | bytes 196616 | tf_op jit(solution)/shard_map/ppermute | solution.py:226
  53.9 0.9 %collective-permute-start.20 = (bf16[256,128]{1,0:T(8,128)(2,1)S(1)}, bf16[256,128]{1,0:T(8,128)(2,1)S(1)}, u32[]{:S(2)}, u32[]{:S(2)}) collective-permute-start(bf16[256,128]{1,0:T(8,128)(2,1)S(1)} %get-tuple-element.53), channel_id=1, source_target_pairs={{0,8},{4,12},{8,0},{12,4},{16,24},{20,28},{24,16},{28,20},{1,9},{5... | collective-permute-start | bytes 196616 | tf_op jit(solution)/shard_map/ppermute | solution.py:226
  54.8 2.7 %collective-permute-done.25 = bf16[128,384]{1,0:T(8,128)(2,1)S(1)} collective-permute-done((bf16[128,384]{1,0:T(8,128)(2,1)S(1)}, bf16[128,384]{1,0:T(8,128)(2,1)S(1)}, u32[]{:S(2)}, u32[]{:S(2)}) %collective-permute-start.25) | collective-permute-done | bytes 98336 | tf_op jit(solution)/shard_map/ppermute | solution.py:226
  59.0 0.8 %join_grads.1 = (f32[256,256]{1,0:T(8,128)}, f32[256,128]{1,0:T(8,128)}) custom-call(f32[128,384]{1,0:T(8,128)S(1)} %add_add_fusion.mine_ref, f32[128,384]{1,0:T(8,128)S(1)} %collective-permute-done.27.theirs_ref), custom_call_target="tpu_custom_call" | custom-call | tf_op jit(solution)/shard_map/join_grads/pallas_call | solution.py:173
  (75 shorter events, 13.8 us)
Async XLA Ops:
  0.6 12.6 %collective-permute-start = (bf16[256,256]{1,0:T(8,128)(2,1)}, bf16[256,256]{1,0:T(8,128)(2,1)S(1)}, u32[]{:S(2)}, u32[]{:S(2)}) collective-permute-start(bf16[256,256]{1,0:T(8,128)(2,1)} %param.7), channel_id=1, source_target_pairs={{0,3},{1,2},{2,1},{3,0},{4,7},{5,6},{6,5},{7,4},{8,11},{9,10},{10,... | collective-permute-start | bytes 393224 | tf_op jit(solution)/shard_map/ppermute | solution.py:226
  5.7 11.3 %collective-permute-start.1 = (bf16[256,256]{1,0:T(8,128)(2,1)}, bf16[256,256]{1,0:T(8,128)(2,1)S(1)}, u32[]{:S(2)}, u32[]{:S(2)}) collective-permute-start(bf16[256,256]{1,0:T(8,128)(2,1)} %param.7), channel_id=1, source_target_pairs={{0,2},{1,3},{2,0},{3,1},{4,6},{5,7},{6,4},{7,5},{8,10},{9,11},{10,... | collective-permute-start | bytes 393224 | tf_op jit(solution)/shard_map/ppermute | solution.py:226
  5.7 11.3 %collective-permute-start.2 = (bf16[256,256]{1,0:T(8,128)(2,1)}, bf16[256,256]{1,0:T(8,128)(2,1)S(1)}, u32[]{:S(2)}, u32[]{:S(2)}) collective-permute-start(bf16[256,256]{1,0:T(8,128)(2,1)} %param.7), channel_id=1, source_target_pairs={{0,1},{1,0},{2,3},{3,2},{4,5},{5,4},{6,7},{7,6},{8,9},{9,8},{10,11... | collective-permute-start | bytes 393224 | tf_op jit(solution)/shard_map/ppermute | solution.py:226
  6.4 5.2 %collective-permute-start.4 = (bf16[256,128]{1,0:T(8,128)(2,1)}, bf16[256,128]{1,0:T(8,128)(2,1)S(1)}, u32[]{:S(2)}, u32[]{:S(2)}) collective-permute-start(bf16[256,128]{1,0:T(8,128)(2,1)} %param.13), channel_id=1, source_target_pairs={{0,8},{4,12},{8,0},{12,4},{16,24},{20,28},{24,16},{28,20},{1,9},{5... | collective-permute-start | bytes 196616 | tf_op jit(solution)/shard_map/ppermute | solution.py:226
  11.6 6.3 %collective-permute-start.5 = (bf16[512,128]{1,0:T(8,128)(2,1)S(1)}, bf16[512,128]{1,0:T(8,128)(2,1)S(1)}, u32[]{:S(2)}, u32[]{:S(2)}) collective-permute-start(bf16[512,128]{1,0:T(8,128)(2,1)S(1)} %pad_maximum_fusion), channel_id=1, source_target_pairs={{0,16},{4,20},{8,24},{12,28},{16,0},{20,4},{24,8},{28,12},{1,17},{... | collective-permute-start | bytes 393224 | tf_op jit(solution)/shard_map/ppermute | solution.py:226
  21.9 6.8 %collective-permute-start.7 = (bf16[256,256]{1,0:T(8,128)(2,1)S(1)}, bf16[256,256]{1,0:T(8,128)(2,1)S(1)}, u32[]{:S(2)}, u32[]{:S(2)}) collective-permute-start(bf16[256,256]{1,0:T(8,128)(2,1)S(1)} %get-tuple-element.51), channel_id=1, source_target_pairs={{0,24},{4,28},{8,16},{12,20},{16,8},{20,12},{24,0},{28,4},{1,25},{... | collective-permute-start | bytes 393224 | tf_op jit(solution)/shard_map/ppermute | solution.py:226
  24.4 6.8 %collective-permute-start.8 = (bf16[256,256]{1,0:T(8,128)(2,1)S(1)}, bf16[256,256]{1,0:T(8,128)(2,1)S(1)}, u32[]{:S(2)}, u32[]{:S(2)}) collective-permute-start(bf16[256,256]{1,0:T(8,128)(2,1)S(1)} %get-tuple-element.50), channel_id=1, source_target_pairs={{0,16},{4,20},{8,24},{12,28},{16,0},{20,4},{24,8},{28,12},{1,17},{... | collective-permute-start | bytes 393224 | tf_op jit(solution)/shard_map/ppermute | solution.py:226
  24.9 6.4 %collective-permute-start.9 = (bf16[256,256]{1,0:T(8,128)(2,1)S(1)}, bf16[256,256]{1,0:T(8,128)(2,1)S(1)}, u32[]{:S(2)}, u32[]{:S(2)}) collective-permute-start(bf16[256,256]{1,0:T(8,128)(2,1)S(1)} %get-tuple-element.49), channel_id=1, source_target_pairs={{0,8},{4,12},{8,0},{12,4},{16,24},{20,28},{24,16},{28,20},{1,9},{5... | collective-permute-start | bytes 393224 | tf_op jit(solution)/shard_map/ppermute | solution.py:226
  25.5 7.6 %collective-permute-start.10 = (bf16[256,128]{1,0:T(8,128)(2,1)S(1)}, bf16[256,128]{1,0:T(8,128)(2,1)S(1)}, u32[]{:S(2)}, u32[]{:S(2)}) collective-permute-start(bf16[256,128]{1,0:T(8,128)(2,1)S(1)} %get-tuple-element.57), channel_id=1, source_target_pairs={{0,2},{1,3},{2,0},{3,1},{4,6},{5,7},{6,4},{7,5},{8,10},{9,11},{10,... | collective-permute-start | bytes 196616 | tf_op jit(solution)/shard_map/ppermute | solution.py:226
  26.2 7.0 %collective-permute-start.11 = (bf16[256,128]{1,0:T(8,128)(2,1)S(1)}, bf16[256,128]{1,0:T(8,128)(2,1)S(1)}, u32[]{:S(2)}, u32[]{:S(2)}) collective-permute-start(bf16[256,128]{1,0:T(8,128)(2,1)S(1)} %get-tuple-element.56), channel_id=1, source_target_pairs={{0,3},{1,2},{2,1},{3,0},{4,7},{5,6},{6,5},{7,4},{8,11},{9,10},{10,... | collective-permute-start | bytes 196616 | tf_op jit(solution)/shard_map/ppermute | solution.py:226
  28.7 4.9 %collective-permute-start.12 = (bf16[256,128]{1,0:T(8,128)(2,1)S(1)}, bf16[256,128]{1,0:T(8,128)(2,1)S(1)}, u32[]{:S(2)}, u32[]{:S(2)}) collective-permute-start(bf16[256,128]{1,0:T(8,128)(2,1)S(1)} %get-tuple-element.55), channel_id=1, source_target_pairs={{0,1},{1,0},{2,3},{3,2},{4,5},{5,4},{6,7},{7,6},{8,9},{9,8},{10,11... | collective-permute-start | bytes 196616 | tf_op jit(solution)/shard_map/ppermute | solution.py:226
  34.3 4.5 %collective-permute-start.13 = (bf16[128,384]{1,0:T(8,128)(2,1)S(1)}, bf16[128,384]{1,0:T(8,128)(2,1)S(1)}, u32[]{:S(2)}, u32[]{:S(2)}) collective-permute-start(bf16[128,384]{1,0:T(8,128)(2,1)S(1)} %get-tuple-element.33), channel_id=1, source_target_pairs={{0,4},{4,0},{8,12},{12,8},{16,20},{20,16},{24,28},{28,24},{1,5},{5... | collective-permute-start | bytes 294920 | tf_op jit(solution)/shard_map/ppermute | solution.py:226
  34.3 7.5 %collective-permute-start.14 = (bf16[256,128]{1,0:T(8,128)(2,1)S(1)}, bf16[256,128]{1,0:T(8,128)(2,1)S(1)}, u32[]{:S(2)}, u32[]{:S(2)}) collective-permute-start(bf16[256,128]{1,0:T(8,128)(2,1)S(1)} %get-tuple-element.42), channel_id=1, source_target_pairs={{0,1},{1,0},{2,3},{3,2},{4,5},{5,4},{6,7},{7,6},{8,9},{9,8},{10,11... | collective-permute-start | bytes 196616 | tf_op jit(solution)/shard_map/ppermute | solution.py:226
  35.2 8.6 %collective-permute-start.15 = (bf16[256,128]{1,0:T(8,128)(2,1)S(1)}, bf16[256,128]{1,0:T(8,128)(2,1)S(1)}, u32[]{:S(2)}, u32[]{:S(2)}) collective-permute-start(bf16[256,128]{1,0:T(8,128)(2,1)S(1)} %get-tuple-element.42), channel_id=1, source_target_pairs={{0,2},{1,3},{2,0},{3,1},{4,6},{5,7},{6,4},{7,5},{8,10},{9,11},{10,... | collective-permute-start | bytes 196616 | tf_op jit(solution)/shard_map/ppermute | solution.py:226
  37.2 6.6 %collective-permute-start.16 = (bf16[256,128]{1,0:T(8,128)(2,1)S(1)}, bf16[256,128]{1,0:T(8,128)(2,1)S(1)}, u32[]{:S(2)}, u32[]{:S(2)}) collective-permute-start(bf16[256,128]{1,0:T(8,128)(2,1)S(1)} %get-tuple-element.42), channel_id=1, source_target_pairs={{0,3},{1,2},{2,1},{3,0},{4,7},{5,6},{6,5},{7,4},{8,11},{9,10},{10,... | collective-permute-start | bytes 196616 | tf_op jit(solution)/shard_map/ppermute | solution.py:226
  38.8 6.6 %collective-permute-start.21 = (bf16[128,384]{1,0:T(8,128)(2,1)S(1)}, bf16[128,384]{1,0:T(8,128)(2,1)S(1)}, u32[]{:S(2)}, u32[]{:S(2)}) collective-permute-start(bf16[128,384]{1,0:T(8,128)(2,1)S(1)} %add_convert_fusion.1), channel_id=1, source_target_pairs={{0,24},{4,28},{8,16},{12,20},{16,8},{20,12},{24,0},{28,4},{1,25},{... | collective-permute-start | bytes 294920 | tf_op jit(solution)/shard_map/ppermute | solution.py:226
  41.3 5.1 %collective-permute-start.22 = (bf16[128,384]{1,0:T(8,128)(2,1)S(1)}, bf16[128,384]{1,0:T(8,128)(2,1)S(1)}, u32[]{:S(2)}, u32[]{:S(2)}) collective-permute-start(bf16[128,384]{1,0:T(8,128)(2,1)S(1)} %add_convert_fusion.1), channel_id=1, source_target_pairs={{0,16},{4,20},{8,24},{12,28},{16,0},{20,4},{24,8},{28,12},{1,17},{... | collective-permute-start | bytes 294920 | tf_op jit(solution)/shard_map/ppermute | solution.py:226
  41.8 4.8 %collective-permute-start.23 = (bf16[128,384]{1,0:T(8,128)(2,1)S(1)}, bf16[128,384]{1,0:T(8,128)(2,1)S(1)}, u32[]{:S(2)}, u32[]{:S(2)}) collective-permute-start(bf16[128,384]{1,0:T(8,128)(2,1)S(1)} %add_convert_fusion.1), channel_id=1, source_target_pairs={{0,8},{4,12},{8,0},{12,4},{16,24},{20,28},{24,16},{28,20},{1,9},{5... | collective-permute-start | bytes 294920 | tf_op jit(solution)/shard_map/ppermute | solution.py:226
  44.6 6.5 %collective-permute-start.17 = (bf16[1024,128]{1,0:T(8,128)(2,1)S(1)}, bf16[1024,128]{1,0:T(8,128)(2,1)S(1)}, u32[]{:S(2)}, u32[]{:S(2)}) collective-permute-start(bf16[1024,128]{1,0:T(8,128)(2,1)S(1)} %fusion.8), channel_id=1, source_target_pairs={{0,4},{4,0},{8,12},{12,8},{16,20},{20,16},{24,28},{28,24},{1,5},{5... | collective-permute-start | bytes 786440 | tf_op jit(solution)/shard_map/ppermute | solution.py:226
  46.6 7.2 %collective-permute-start.24 = (bf16[128,384]{1,0:T(8,128)(2,1)S(1)}, bf16[128,384]{1,0:T(8,128)(2,1)S(1)}, u32[]{:S(2)}, u32[]{:S(2)}) collective-permute-start(bf16[128,384]{1,0:T(8,128)(2,1)S(1)} %add_convert_fusion), channel_id=1, source_target_pairs={{0,1},{1,0},{2,3},{3,2},{4,5},{5,4},{6,7},{7,6},{8,9},{9,8},{10,11... | collective-permute-start | bytes 294920 | tf_op jit(solution)/shard_map/ppermute | solution.py:226
  46.8 10.7 %collective-permute-start.25 = (bf16[128,384]{1,0:T(8,128)(2,1)S(1)}, bf16[128,384]{1,0:T(8,128)(2,1)S(1)}, u32[]{:S(2)}, u32[]{:S(2)}) collective-permute-start(bf16[128,384]{1,0:T(8,128)(2,1)S(1)} %add_convert_fusion), channel_id=1, source_target_pairs={{0,2},{1,3},{2,0},{3,1},{4,6},{5,7},{6,4},{7,5},{8,10},{9,11},{10,... | collective-permute-start | bytes 294920 | tf_op jit(solution)/shard_map/ppermute | solution.py:226
  49.6 7.8 %collective-permute-start.26 = (bf16[128,384]{1,0:T(8,128)(2,1)S(1)}, bf16[128,384]{1,0:T(8,128)(2,1)S(1)}, u32[]{:S(2)}, u32[]{:S(2)}) collective-permute-start(bf16[128,384]{1,0:T(8,128)(2,1)S(1)} %add_convert_fusion), channel_id=1, source_target_pairs={{0,3},{1,2},{2,1},{3,0},{4,7},{5,6},{6,5},{7,4},{8,11},{9,10},{10,... | collective-permute-start | bytes 294920 | tf_op jit(solution)/shard_map/ppermute | solution.py:226
  51.2 6.4 %collective-permute-start.18 = (bf16[256,128]{1,0:T(8,128)(2,1)S(1)}, bf16[256,128]{1,0:T(8,128)(2,1)S(1)}, u32[]{:S(2)}, u32[]{:S(2)}) collective-permute-start(bf16[256,128]{1,0:T(8,128)(2,1)S(1)} %get-tuple-element.52), channel_id=1, source_target_pairs={{0,24},{4,28},{8,16},{12,20},{16,8},{20,12},{24,0},{28,4},{1,25},{... | collective-permute-start | bytes 196616 | tf_op jit(solution)/shard_map/ppermute | solution.py:226
  52.7 4.9 %collective-permute-start.19 = (bf16[256,128]{1,0:T(8,128)(2,1)S(1)}, bf16[256,128]{1,0:T(8,128)(2,1)S(1)}, u32[]{:S(2)}, u32[]{:S(2)}) collective-permute-start(bf16[256,128]{1,0:T(8,128)(2,1)S(1)} %get-tuple-element.54), channel_id=1, source_target_pairs={{0,16},{4,20},{8,24},{12,28},{16,0},{20,4},{24,8},{28,12},{1,17},{... | collective-permute-start | bytes 196616 | tf_op jit(solution)/shard_map/ppermute | solution.py:226
  (9 other events, 43.3 us)
